TPU v7x, 32 devices: a whole 2x2x4 slice. The times are simulated.
32 devices in a mesh: row: 4 (over y, core), col: 8 (over z, x).
Axes of the slice: x: 2, y: 2, z: 4, core: 2. Of those that a mesh axis runs over, the one named last changes fastest.
Arguments:
- marginal: float32 [32768, 128], P(('row', 'col')), may hold values from -6 to 6
- penalty: float32 [128], replicated, may hold values from 0.5 to 8
- ld_diag: float32 [32, 1024, 1024], P(('row', 'col')), may hold values from -0.005 to 1, as said below
- ld_low: float32 [32, 2, 1024, 1024], P(('row', 'col')), may hold values from -0.006 to 0.36
- band: int32 [32], P(('row', 'col')), may hold values from 0 to 2
- genotypes: bfloat16 [1280, 32768], P(None, ('row', 'col')), may hold values from -5 to 5
Outputs:
- effects: float32 [32768, 128], P(('row', 'col'))
- scores: float32 [1280, 128], P(('row', 'col'))
Inputs may be any that keep to these rules, and one draw needn't show every extreme that they name: Each block of ld_diag is symmetric with ones on its diagonal.
All inputs are finite; a program needn't handle non-finite values.
Results may differ from a plain program's by a relative error of at most 0.0023.
The roundings to bfloat16 on the way count: a program that leaves them out, or rounds other values in their place, can miss the bound.
Values sent between devices are 32-bit elements; how exact they have to be, the bound alone decides.
No kernel may reach another device: no remote copies, remote signals or barrier semaphores. Data moves between devices by JAX's collectives and lax.ppermute only.
A program may use at most 128 MiB of HBM per device.

v0:
```python
import functools

import jax
import jax.numpy as jnp
from jax import lax
from jax.experimental import pallas as pl
from jax.experimental.pallas import tpu as pltpu
from jax.sharding import PartitionSpec as P

AXES = ("row", "col")
F32 = jnp.float32
BF16 = jnp.bfloat16
MIB = 1024 * 1024
VMEM = pl.BlockSpec(memory_space=pltpu.VMEM)
SMEM = pl.BlockSpec(memory_space=pltpu.SMEM)
ANY = pl.BlockSpec(memory_space=pl.ANY)


def params(mib=20):
    return pltpu.CompilerParams(vmem_limit_bytes=mib * MIB)


def cost(flops, num_bytes):
    return pl.CostEstimate(flops=int(flops), bytes_accessed=int(num_bytes), transcendentals=0)


def shifted(block, distance):
    n = lax.axis_size(AXES)
    route = [(i - distance, i) for i in range(n) if 0 <= i - distance < n]
    return lax.ppermute(block, AXES, route)


def active(d, band, position):
    return jnp.logical_and(band[0] >= d + 1, position[0] >= d + 1)


def split_store(value, first, second):
    half = first.shape[0]
    first[...] = value[:half]
    second[...] = value[half:]


GROUP = 4


def fetched(low, tiles, arrived, order):
    count, rows = tiles.shape[0] // len(order), tiles.shape[1]
    copies = []
    for place in range(tiles.shape[0]):
        source = low.at[order[place // count], pl.ds(place % count * rows, rows)]
        copies.append(pltpu.make_async_copy(source, tiles.at[place], arrived.at[place]))
        copies[-1].start()
    return copies


def rounded_rows(copies, tiles, place, alive):
    for copy in copies[place : place + GROUP]:
        copy.wait()
    tile = tiles[place : place + GROUP].reshape(GROUP * tiles.shape[1], tiles.shape[2])
    return jnp.where(alive, tile, 0.0).astype(BF16)


def first_kernel(band, position, vec, low, one_a, one_b, own, tiles, arrived):
    fetch = pltpu.make_async_copy(vec, own, arrived.at[tiles.shape[0]])
    fetch.start()
    copies = fetched(low, tiles, arrived, (0,))
    fetch.wait()
    across = own[...].T.astype(BF16)
    rows = GROUP * tiles.shape[1]
    acc = None
    for place in range(0, tiles.shape[0], GROUP):
        tile = rounded_rows(copies, tiles, place, active(0, band, position))
        start = place * tiles.shape[1]
        term = jnp.dot(across[:, start : start + rows], tile, preferred_element_type=F32)
        acc = term if acc is None else acc + term
    split_store(acc.T, one_a, one_b)


def second_kernel(band, position, vec, low, far_a, far_b, low_one, low_two, own, tiles, arrived):
    fetch = pltpu.make_async_copy(vec, own, arrived.at[tiles.shape[0]])
    fetch.start()
    copies = fetched(low, tiles, arrived, (1, 0))
    fetch.wait()
    across = own[...].T.astype(BF16)
    rows = GROUP * tiles.shape[1]
    count = tiles.shape[0] // 2
    acc = None
    for place in range(0, count, GROUP):
        tile = rounded_rows(copies, tiles, place, active(1, band, position))
        start = place * tiles.shape[1]
        low_two[start : start + rows] = tile
        term = jnp.dot(across[:, start : start + rows], tile, preferred_element_type=F32)
        acc = term if acc is None else acc + term
    split_store(acc.T, far_a, far_b)
    for place in range(0, count, GROUP):
        start = place * tiles.shape[1]
        low_one[start : start + rows] = rounded_rows(copies, tiles, count + place, active(0, band, position))


def from_tiles(kernel, tiles, narrow, mib, band, position, vec, low):
    size, k = vec.shape
    count = 16
    return pl.pallas_call(
        kernel,
        in_specs=[SMEM] * 2 + [pl.BlockSpec(memory_space=pltpu.HBM)] * 2,
        out_specs=[VMEM] * (2 + narrow),
        out_shape=[jax.ShapeDtypeStruct((size // 2, k), F32)] * 2 + [jax.ShapeDtypeStruct((size, size), BF16)] * narrow,
        scratch_shapes=[
            pltpu.VMEM((size, k), F32),
            pltpu.VMEM((tiles * count, size // count, size), F32),
            pltpu.SemaphoreType.DMA((tiles * count + 1,)),
        ],
        compiler_params=params(mib),
        cost_estimate=cost(2 * size * size * k, 4 * tiles * size * size),
    )(band, position, vec, low)


def coupling_kernel(vec, low_one, low_two, one_a, one_b, far_a, far_b):
    across = vec[...].T.astype(BF16)
    split_store(jnp.dot(across, low_one[...], preferred_element_type=F32).T, one_a, one_b)
    split_store(jnp.dot(across, low_two[...], preferred_element_type=F32).T, far_a, far_b)


def coupling(vec, low_one, low_two):
    size, k = vec.shape
    return pl.pallas_call(
        coupling_kernel,
        in_specs=[VMEM] * 3,
        out_specs=[VMEM] * 4,
        out_shape=[jax.ShapeDtypeStruct((size // 2, k), F32)] * 4,
        compiler_params=params(),
        cost_estimate=cost(4 * size * size * k, 4 * size * size),
    )(vec, low_one, low_two)


def relay_kernel(odd, far, pair, after, out):
    out[...] = far[...] + jnp.where(odd[0] > 0, pair[...], 0.0)


def choose_kernel(odd, vec, two, after, *parts):
    rows = parts[0].shape[0]
    for place, part in enumerate(parts):
        here = slice(place * rows, (place + 1) * rows)
        part[...] = jnp.where(odd[0] > 0, two[here], vec[here])


def choose(odd, vec, two, after, parts):
    rows, k = vec.shape
    return pl.pallas_call(
        choose_kernel,
        in_specs=[SMEM, VMEM, VMEM, ANY],
        out_specs=[VMEM] * parts,
        out_shape=[jax.ShapeDtypeStruct((rows // parts, k), F32)] * parts,
        compiler_params=params(),
        cost_estimate=cost(vec.size, 12 * vec.size),
    )(odd, vec, two, after)


def relay(odd, far, pair, after):
    return pl.pallas_call(
        relay_kernel,
        in_specs=[SMEM, VMEM, VMEM, ANY],
        out_specs=VMEM,
        out_shape=jax.ShapeDtypeStruct(far.shape, F32),
        compiler_params=params(),
        cost_estimate=cost(far.size, 12 * far.size),
    )(odd, far, pair, after)


def first_diag_kernel(vec, diag, after, narrow, product):
    tile = diag[...].astype(BF16)
    narrow[...] = tile
    product[...] = jnp.dot(tile, vec[...].astype(BF16), preferred_element_type=F32)


def first_diag(vec, diag, after):
    size, k = vec.shape
    rows = size // 4
    return pl.pallas_call(
        first_diag_kernel,
        grid=(4,),
        in_specs=[pl.BlockSpec((size, k), lambda r: (0, 0)), pl.BlockSpec((rows, size), lambda r: (r, 0)), ANY],
        out_specs=[pl.BlockSpec((rows, size), lambda r: (r, 0)), pl.BlockSpec((rows, k), lambda r: (r, 0))],
        out_shape=[jax.ShapeDtypeStruct(diag.shape, BF16), jax.ShapeDtypeStruct(vec.shape, F32)],
        compiler_params=params(),
        cost_estimate=cost(2 * size * size * k, 6 * size * size),
    )(vec, diag, after)


def diag_kernel(vec, diag, after, product):
    product[...] = jnp.dot(diag[...], vec[...].astype(BF16), preferred_element_type=F32)


def diag_times(vec, diag, after):
    size, k = vec.shape
    return pl.pallas_call(
        diag_kernel,
        in_specs=[VMEM, VMEM, ANY],
        out_specs=VMEM,
        out_shape=jax.ShapeDtypeStruct(vec.shape, F32),
        compiler_params=params(),
        cost_estimate=cost(2 * size * size * k, 6 * size * size),
    )(vec, diag, after)


def finish_kernel(odd, part, low, one, ahead_a, ahead_b, pair_a, pair_b, out, upper):
    acc = jnp.dot(low[...], one[...].astype(BF16), preferred_element_type=F32) + part[...]
    half = upper.shape[0]
    for place, (straight, pair) in enumerate(((ahead_a, pair_a), (ahead_b, pair_b))):
        rows = slice(place * half, (place + 1) * half)
        out[rows] = acc[rows] + straight[...] + jnp.where(odd[0] > 0, 0.0, pair[...])
    upper[...] = out[:half]


def finish(odd, part, low, *arrived):
    size, k = part.shape
    return pl.pallas_call(
        finish_kernel,
        in_specs=[SMEM] + [VMEM] * 7,
        out_specs=[VMEM] * 2,
        out_shape=[jax.ShapeDtypeStruct(part.shape, F32), jax.ShapeDtypeStruct((size // 2, k), F32)],
        compiler_params=params(),
        cost_estimate=cost(2 * size * size * k, 2 * size * size),
    )(odd, part, low, *arrived)


def two_kernel(own, low, two, product):
    product[...] = own[...] + jnp.dot(low[...], two[...].astype(BF16), preferred_element_type=F32)


def add_two(own, low, two):
    size, k = two.shape
    return pl.pallas_call(
        two_kernel,
        in_specs=[VMEM] * 3,
        out_specs=VMEM,
        out_shape=jax.ShapeDtypeStruct(two.shape, F32),
        compiler_params=params(),
        cost_estimate=cost(2 * size * size * k, 2 * size * size),
    )(own, low, two)


def lower_kernel(vec, low_one, low_two, one, far):
    across = vec[...].T.astype(BF16)
    half = one.shape[0]
    one[...] = jnp.dot(across, low_one[:, half:], preferred_element_type=F32).T
    far[...] = jnp.dot(across, low_two[:, half:], preferred_element_type=F32).T


def lower_coupling(vec, low_one, low_two):
    size, k = vec.shape
    return pl.pallas_call(
        lower_kernel,
        in_specs=[VMEM] * 3,
        out_specs=[VMEM] * 2,
        out_shape=[jax.ShapeDtypeStruct((size // 2, k), F32)] * 2,
        compiler_params=params(),
        cost_estimate=cost(2 * size * size * k, 2 * size * size),
    )(vec, low_one, low_two)


def own_kernel(v0, v1, v2, diag, after, moments):
    image = jnp.dot(diag[...], v2[...].astype(BF16), preferred_element_type=F32)
    pairs = [(v0, v0), (v0, v1), (v1, v1), (v1, v2), (v2, v2)]
    for row, (a, b) in enumerate(pairs):
        moments[row : row + 1] = jnp.sum(a[...] * b[...], axis=0, keepdims=True)
    moments[5:6] = jnp.sum(v2[...] * image, axis=0, keepdims=True)
    moments[6:8] = jnp.zeros_like(moments[6:8])


def own_moments(v0, v1, v2, diag, after):
    size, k = v0.shape
    return pl.pallas_call(
        own_kernel,
        in_specs=[VMEM] * 4 + [ANY],
        out_specs=VMEM,
        out_shape=jax.ShapeDtypeStruct((8, k), F32),
        compiler_params=params(),
        cost_estimate=cost(2 * size * size * k, 6 * size * size),
    )(v0, v1, v2, diag, after)


def last_kernel(odd, low_one, low_two, one_a, one_b, two, v2, up, pair, moments, out):
    quarter, half = one_a.shape[0], two.shape[0]
    below = jnp.dot(low_two[:, :half], two[...].astype(BF16), preferred_element_type=F32)
    below = below + jnp.dot(low_one[:, :quarter], one_a[...].astype(BF16), preferred_element_type=F32)
    below = below + jnp.dot(low_one[:, quarter:half], one_b[...].astype(BF16), preferred_element_type=F32)
    above = up[...] + jnp.where(odd[0] > 0, 0.0, pair[...])
    coupled = jnp.sum(v2[...] * below, axis=0, keepdims=True) + jnp.sum(v2[half:] * above, axis=0, keepdims=True)
    out[...] = moments[...]
    out[5:6] = moments[5:6] + 2.0 * coupled


def last(odd, low_one, low_two, one_a, one_b, two, v2, up, pair, moments):
    size, k = v2.shape
    return pl.pallas_call(
        last_kernel,
        in_specs=[SMEM] + [VMEM] * 9,
        out_specs=VMEM,
        out_shape=jax.ShapeDtypeStruct((8, k), F32),
        compiler_params=params(),
        cost_estimate=cost(2 * size * size * k, 2 * size * size),
    )(odd, low_one, low_two, one_a, one_b, two, v2, up, pair, moments)


def group_rows(genotypes, groups, group):
    rows = genotypes.shape[0] // groups
    return genotypes[pl.ds(pl.multiple_of(group * rows, rows), rows)]


def send_kernel(groups, row, pieces, penalty, v0, v1, v2, genotypes, effects, rounded, send):
    sums = pieces[0]
    for piece in range(1, pieces.shape[0]):
        sums = sums + pieces[piece]
    moments = [sums[m : m + 1] for m in range(6)]
    c0, c1, c2 = coefficients(moments, penalty[...])
    value = c0 * v0[...] + c1 * v1[...] + c2 * v2[...]
    effects[...] = value
    narrow = value.astype(BF16)
    rounded[...] = narrow
    other = 1 - row[0] % 2
    for g in range(groups // 2):
        send[g] = jnp.dot(group_rows(genotypes, groups, 2 * g + other), narrow, preferred_element_type=F32)


def keep_kernel(groups, row, rounded, genotypes, keep):
    mine = row[0] % 2
    for g in range(groups // 2):
        keep[g] = jnp.dot(group_rows(genotypes, groups, 2 * g + mine), rounded[...], preferred_element_type=F32)


def partial_scores(row, groups, pieces, penalty, v0, v1, v2, genotypes):
    people, size = genotypes.shape
    k = v0.shape[1]
    half = jax.ShapeDtypeStruct((groups // 2, people // groups, k), F32)
    effects, rounded, send = pl.pallas_call(
        functools.partial(send_kernel, groups),
        in_specs=[SMEM] + [VMEM] * 6,
        out_specs=[VMEM] * 3,
        out_shape=[jax.ShapeDtypeStruct(v0.shape, F32), jax.ShapeDtypeStruct(v0.shape, BF16), half],
        compiler_params=params(),
        cost_estimate=cost(people * size * k, 2 * people * size),
    )(row, pieces, penalty, v0, v1, v2, genotypes)
    keep = pl.pallas_call(
        functools.partial(keep_kernel, groups),
        in_specs=[SMEM, VMEM, VMEM],
        out_specs=VMEM,
        out_shape=half,
        compiler_params=params(),
        cost_estimate=cost(people * size * k, 2 * people * size),
    )(row, rounded, genotypes)
    return effects, send, keep


def pick_kernel(index, keep, received, mine, other):
    mine[...] = keep[index[0]] + received[index[0]]
    other[...] = keep[1 - index[0]] + received[1 - index[0]]


def pick(index, keep, received):
    half = jax.ShapeDtypeStruct(keep.shape[1:], F32)
    return pl.pallas_call(
        pick_kernel,
        in_specs=[SMEM, VMEM, VMEM],
        out_specs=[VMEM] * 2,
        out_shape=[half] * 2,
        compiler_params=params(),
        cost_estimate=cost(keep.size, 12 * keep.size),
    )(index, keep, received)


def scattered_over(values, axis):
    n = lax.axis_size(axis)
    pieces = values.reshape((n, values.shape[0] // n) + values.shape[1:])
    return jnp.sum(lax.all_to_all(pieces, axis, 0, 0, tiled=True), axis=0)


def routed(block, pairs):
    return lax.ppermute(block, AXES, pairs)


def coefficients(moments, penalty):
    def inner(u, v):
        return sum(a * b * moments[i + j] for i, a in enumerate(u) for j, b in enumerate(v))

    n0 = moments[0]
    a0 = n0 / (moments[1] + penalty * n0)
    r1 = [1.0 - a0 * penalty, -a0]
    n1 = inner(r1, r1)
    b0 = n1 / n0
    d1 = [r1[0] + b0, r1[1]]
    ad1 = [penalty * d1[0], d1[0] + penalty * d1[1], d1[1]]
    a1 = n1 / inner(d1, ad1)
    e1 = [a0 + a1 * d1[0], a1 * d1[1]]
    r2 = [r1[0] - a1 * ad1[0], r1[1] - a1 * ad1[1], -a1 * ad1[2]]
    n2 = inner(r2, r2)
    b1 = n2 / n1
    d2 = [r2[0] + b1 * d1[0], r2[1] + b1 * d1[1], r2[2]]
    ad2 = [penalty * d2[0], d2[0] + penalty * d2[1], d2[1] + penalty * d2[2], d2[2]]
    a2 = n2 / inner(d2, ad2)
    return e1[0] + a2 * d2[0], e1[1] + a2 * d2[1], a2 * d2[2]


def swapped(block, bit):
    return routed(block, [(i, i ^ bit) for i in range(lax.axis_size(AXES))])


def body(marginal, penalty, ld_diag, ld_low, band, genotypes):
    n = lax.axis_size(AXES)
    rows, cols = lax.axis_size("row"), lax.axis_size("col")
    position = lax.axis_index(AXES)
    row = lax.axis_index("row")
    site = position.astype(jnp.int32)[None]
    odd = (position % 2).astype(jnp.int32)[None]
    half = marginal.shape[0] // 2

    def halos(vec, two, first, second):
        one_a, one_b = first()
        pair_a, pair_b = swapped(one_a, 1), swapped(one_b, 1)
        far_a, far_b = second(one_b)
        sum_a = relay(odd, far_a, pair_a, far_b)
        up_a = shifted(sum_a, -2)
        [chosen] = choose(odd, vec, two, sum_a, 1)
        one = swapped(chosen, 1)
        sum_b = relay(odd, far_b, pair_b, chosen)
        return sum_b, (one, up_a, shifted(sum_b, -2), pair_a, pair_b)

    v0 = marginal
    two = shifted(v0, 2)

    lows = []

    def second_tile(after):
        vec, _ = lax.optimization_barrier((v0, after))
        *products, low_one, low_two = from_tiles(second_kernel, 2, 2, 46, band, site, vec, ld_low[0])
        lows.extend((low_one, low_two))
        return products

    last_sum, arrived = halos(
        v0, two, lambda: from_tiles(first_kernel, 1, 0, 58, band, site, v0, ld_low[0]), second_tile
    )
    low_one, low_two = lows
    diag, own = first_diag(v0, ld_diag[0], last_sum)
    v1, _ = finish(odd, add_two(own, low_two, two), low_one, *arrived)

    two = shifted(v1, 2)
    products = coupling(v1, low_one, low_two)
    last_sum, arrived = halos(v1, two, lambda: products[:2], lambda after: products[2:])
    own = diag_times(v1, diag, last_sum)
    v2, upper = finish(odd, add_two(own, low_two, two), low_one, *arrived)

    two = shifted(upper, 2)
    one, far = lower_coupling(v2, low_one, low_two)
    pair = swapped(one, 1)
    above = relay(odd, far, pair, far)
    up = shifted(above, -2)
    chosen_a, chosen_b = choose(odd, upper, two, above, 2)
    moments = own_moments(v0, v1, v2, diag, chosen_b)
    one_a, one_b = swapped(chosen_a, 1), swapped(chosen_b, 1)
    moments = last(odd, low_one, low_two, one_a, one_b, two, v2, up, pair, moments)
    pieces = lax.all_to_all(jnp.broadcast_to(moments[None], (n,) + moments.shape), AXES, 0, 0, tiled=True)

    effects, send, keep = partial_scores(row.astype(jnp.int32)[None], rows, pieces, penalty[None], v0, v1, v2, genotypes)
    received = swapped(send, cols)
    bit = rows // 4
    while bit:
        mine = (row // (2 * bit)) % 2
        keep = keep.reshape((2, -1) + keep.shape[1:])
        received = received.reshape((2, -1) + received.shape[1:])

        keep, send = pick(mine.astype(jnp.int32)[None], keep, received)
        received = swapped(send, 2 * bit * cols)
        bit //= 2
    return effects, scattered_over((keep + received)[0], "col")


def solution(mesh):
    placed = (
        P(AXES, None),
        P(),
        P(AXES, None, None),
        P(AXES, None, None, None),
        P(AXES),
        P(None, AXES),
    )
    return jax.shard_map(
        body,
        mesh=mesh,
        in_specs=placed,
        out_specs=(P(AXES, None), P(AXES, None)),
        check_vma=False,
    )
```

profile of v0, /device:TPU:0, one launch (start us, length us, event | category | flops | bytes accessed | tf_op | source)
XLA Modules:
  0.0 121.9 jit_solution(6949979972251444819)
XLA Ops:
  0.6 5.0 %collective-permute-start.1 = (f32[1024,128]{1,0:T(8,128)}, f32[1024,128]{1,0:T(8,128)S(1)}, u32[]{:S(2)}, u32[]{:S(2)}) collective-permute-start(f32[1024,128]{1,0:T(8,128)} %v0.3), channel_id=1, source_target_pairs={{0,2},{1,3},{2,4},{3,5},{4,6},{5,7},{6,8},{7,9},{8,10},{9,11},{10,... | collective-permute-start | bytes 1572872 | tf_op jit(solution)/shard_map/ppermute | solution.py:30
  6.3 3.6 %shard_map.77 = (f32[512,128]{1,0:T(8,128)}, f32[512,128]{1,0:T(8,128)}) custom-call(s32[1]{0:T(128)S(6)} %copy.8.band, s32[1]{0:T(128)} %bitcast.2.position, f32[1024,128]{1,0:T(8,128)} %v0.3, f32[2,1024,1024]{2,1,0:T(8,128)} %bitcast.14), custom_call_target="tpu_custom_call" | custom-call | flops 268435456 | bytes 4194304 | tf_op jit(solution)/shard_map/pallas_call | solution.py:103
  9.9 1.6 %collective-permute-start.2 = (f32[512,128]{1,0:T(8,128)}, f32[512,128]{1,0:T(8,128)S(1)}, u32[]{:S(2)}, u32[]{:S(2)}) collective-permute-start(f32[512,128]{1,0:T(8,128)} %get-tuple-element.33), channel_id=1, source_target_pairs={{0,1},{1,0},{2,3},{3,2},{4,5},{5,4},{6,7},{7,6},{8,9},{9,8},{10,11... | collective-permute-start | bytes 786440 | tf_op jit(solution)/shard_map/ppermute | solution.py:379
  12.0 3.7 %shard_map.78 = (f32[512,128]{1,0:T(8,128)S(1)}, f32[512,128]{1,0:T(8,128)S(1)}, bf16[1024,1024]{1,0:T(8,128)(2,1)S(1)}, bf16[1024,1024]{1,0:T(8,128)(2,1)S(1)}) custom-call(s32[1]{0:T(128)S(6)} %copy.8.band, s32[1]{0:T(128)} %bitcast.2.position, f32[1024,128]{1,0:T(8,128)S(1)} %copy-done, f32[2,1024,1024]{2,1,0:T(8,128)} %bitcast.15), custom_call_target="tpu_custom_call" | custom-call | flops 268435456 | bytes 8388608 | tf_op jit(solution)/shard_map/pallas_call | solution.py:103
  15.7 3.7 %collective-permute-done.2.pair.pair_a = f32[512,128]{1,0:T(8,128)S(1)} collective-permute-done((f32[512,128]{1,0:T(8,128)}, f32[512,128]{1,0:T(8,128)S(1)}, u32[]{:S(2)}, u32[]{:S(2)}) %collective-permute-start.2) | collective-permute-done | bytes 262176 | tf_op jit(solution)/shard_map/ppermute | solution.py:379
  19.5 1.6 %collective-permute-start.3 = (f32[1024,128]{1,0:T(8,128)S(1)}, f32[1024,128]{1,0:T(8,128)S(1)}, u32[]{:S(2)}, u32[]{:S(2)}) collective-permute-start(f32[1024,128]{1,0:T(8,128)S(1)} %shard_map.80.after), channel_id=1, source_target_pairs={{0,1},{1,0},{2,3},{3,2},{4,5},{5,4},{6,7},{7,6},{8,9},{9,8},{10,11... | collective-permute-start | bytes 1572872 | tf_op jit(solution)/shard_map/ppermute | solution.py:379
  21.1 1.3 %collective-permute-start.4 = (f32[512,128]{1,0:T(8,128)S(1)}, f32[512,128]{1,0:T(8,128)S(1)}, u32[]{:S(2)}, u32[]{:S(2)}) collective-permute-start(f32[512,128]{1,0:T(8,128)S(1)} %shard_map.79.after), channel_id=1, source_target_pairs={{2,0},{3,1},{4,2},{5,3},{6,4},{7,5},{8,6},{9,7},{10,8},{11,9},{12,... | collective-permute-start | bytes 786440 | tf_op jit(solution)/shard_map/ppermute | solution.py:30
  22.4 2.0 %collective-permute-done.pair.pair_b = f32[512,128]{1,0:T(8,128)S(1)} collective-permute-done((f32[512,128]{1,0:T(8,128)}, f32[512,128]{1,0:T(8,128)S(1)}, u32[]{:S(2)}, u32[]{:S(2)}) %collective-permute-start) | collective-permute-done | bytes 262176 | tf_op jit(solution)/shard_map/ppermute | solution.py:379
  24.4 1.3 %collective-permute-start.5 = (f32[512,128]{1,0:T(8,128)S(1)}, f32[512,128]{1,0:T(8,128)S(1)}, u32[]{:S(2)}, u32[]{:S(2)}) collective-permute-start(f32[512,128]{1,0:T(8,128)S(1)} %shard_map.81.after), channel_id=1, source_target_pairs={{2,0},{3,1},{4,2},{5,3},{6,4},{7,5},{8,6},{9,7},{10,8},{11,9},{12,... | collective-permute-start | bytes 786440 | tf_op jit(solution)/shard_map/ppermute | solution.py:30
  25.7 1.4 %shard_map.82 = (bf16[1024,1024]{1,0:T(8,128)(2,1)S(1)}, f32[1024,128]{1,0:T(8,128)S(1)}) custom-call(f32[1024,128]{1,0:T(8,128)S(1)} %copy-done, f32[1024,1024]{1,0:T(8,128)S(1)} %bitcast.10, f32[512,128]{1,0:T(8,128)S(1)} %shard_map.81.after), custom_call_target="tpu_custom_call" | custom-call | flops 268435456 | bytes 6291456 | tf_op jit(solution)/shard_map/pallas_call | solution.py:179
  27.8 4.3 %collective-permute-done.4.ahead_a = f32[512,128]{1,0:T(8,128)S(1)} collective-permute-done((f32[512,128]{1,0:T(8,128)S(1)}, f32[512,128]{1,0:T(8,128)S(1)}, u32[]{:S(2)}, u32[]{:S(2)}) %collective-permute-start.4) | collective-permute-done | bytes 262176 | tf_op jit(solution)/shard_map/ppermute | solution.py:30
  32.1 4.8 %collective-permute-done.5.ahead_b = f32[512,128]{1,0:T(8,128)S(1)} collective-permute-done((f32[512,128]{1,0:T(8,128)S(1)}, f32[512,128]{1,0:T(8,128)S(1)}, u32[]{:S(2)}, u32[]{:S(2)}) %collective-permute-start.5) | collective-permute-done | bytes 262176 | tf_op jit(solution)/shard_map/ppermute | solution.py:30
  36.9 1.3 %shard_map.84 = (f32[1024,128]{1,0:T(8,128)S(1)}, f32[512,128]{1,0:T(8,128)}) custom-call(s32[1]{0:T(128)} %bitcast.1.odd, f32[1024,128]{1,0:T(8,128)S(1)} %shard_map.83.part, bf16[1024,1024]{1,0:T(8,128)(2,1)S(1)} %get-tuple-element.29.low.low_one, f32[1024,128]{1,0:T(8,128)S(1)} %collective-permute-done.3.one, ...), custom_call_target="tpu_custom_call" | custom-call | flops 268435456 | bytes 2097152 | tf_op jit(solution)/shard_map/pallas_call | solution.py:217
  38.2 1.5 %collective-permute-start.7 = (f32[1024,128]{1,0:T(8,128)S(1)}, f32[1024,128]{1,0:T(8,128)S(1)}, u32[]{:S(2)}, u32[]{:S(2)}) collective-permute-start(f32[1024,128]{1,0:T(8,128)S(1)} %get-tuple-element.35.vec.v1), channel_id=1, source_target_pairs={{0,2},{1,3},{2,4},{3,5},{4,6},{5,7},{6,8},{7,9},{8,10},{9,11},{10,... | collective-permute-start | bytes 1572872 | tf_op jit(solution)/shard_map/ppermute | solution.py:30
  40.6 1.4 %collective-permute-start.8 = (f32[512,128]{1,0:T(8,128)S(1)}, f32[512,128]{1,0:T(8,128)S(1)}, u32[]{:S(2)}, u32[]{:S(2)}) collective-permute-start(f32[512,128]{1,0:T(8,128)S(1)} %get-tuple-element.40), channel_id=1, source_target_pairs={{0,1},{1,0},{2,3},{3,2},{4,5},{5,4},{6,7},{7,6},{8,9},{9,8},{10,11... | collective-permute-start | bytes 786440 | tf_op jit(solution)/shard_map/ppermute | solution.py:379
  42.7 7.2 %collective-permute-done.8.pair.pair_a = f32[512,128]{1,0:T(8,128)S(1)} collective-permute-done((f32[512,128]{1,0:T(8,128)S(1)}, f32[512,128]{1,0:T(8,128)S(1)}, u32[]{:S(2)}, u32[]{:S(2)}) %collective-permute-start.8) | collective-permute-done | bytes 262176 | tf_op jit(solution)/shard_map/ppermute | solution.py:379
  51.7 1.3 %collective-permute-start.10 = (f32[512,128]{1,0:T(8,128)S(1)}, f32[512,128]{1,0:T(8,128)S(1)}, u32[]{:S(2)}, u32[]{:S(2)}) collective-permute-start(f32[512,128]{1,0:T(8,128)S(1)} %shard_map.86.after), channel_id=1, source_target_pairs={{2,0},{3,1},{4,2},{5,3},{6,4},{7,5},{8,6},{9,7},{10,8},{11,9},{12,... | collective-permute-start | bytes 786440 | tf_op jit(solution)/shard_map/ppermute | solution.py:30
  54.3 1.3 %collective-permute-start.11 = (f32[512,128]{1,0:T(8,128)S(1)}, f32[512,128]{1,0:T(8,128)S(1)}, u32[]{:S(2)}, u32[]{:S(2)}) collective-permute-start(f32[512,128]{1,0:T(8,128)S(1)} %shard_map.88.after), channel_id=1, source_target_pairs={{2,0},{3,1},{4,2},{5,3},{6,4},{7,5},{8,6},{9,7},{10,8},{11,9},{12,... | collective-permute-start | bytes 786440 | tf_op jit(solution)/shard_map/ppermute | solution.py:30
  57.0 5.0 %collective-permute-done.10.ahead_a = f32[512,128]{1,0:T(8,128)S(1)} collective-permute-done((f32[512,128]{1,0:T(8,128)S(1)}, f32[512,128]{1,0:T(8,128)S(1)}, u32[]{:S(2)}, u32[]{:S(2)}) %collective-permute-start.10) | collective-permute-done | bytes 262176 | tf_op jit(solution)/shard_map/ppermute | solution.py:30
  62.0 5.6 %collective-permute-done.11.ahead_b = f32[512,128]{1,0:T(8,128)S(1)} collective-permute-done((f32[512,128]{1,0:T(8,128)S(1)}, f32[512,128]{1,0:T(8,128)S(1)}, u32[]{:S(2)}, u32[]{:S(2)}) %collective-permute-start.11) | collective-permute-done | bytes 262176 | tf_op jit(solution)/shard_map/ppermute | solution.py:30
  68.9 1.6 %collective-permute-start.13 = (f32[512,128]{1,0:T(8,128)S(1)}, f32[512,128]{1,0:T(8,128)S(1)}, u32[]{:S(2)}, u32[]{:S(2)}) collective-permute-start(f32[512,128]{1,0:T(8,128)S(1)} %get-tuple-element.44), channel_id=1, source_target_pairs={{0,1},{1,0},{2,3},{3,2},{4,5},{5,4},{6,7},{7,6},{8,9},{9,8},{10,11... | collective-permute-start | bytes 786440 | tf_op jit(solution)/shard_map/ppermute | solution.py:379
  70.5 3.8 %collective-permute-start.12 = (f32[512,128]{1,0:T(8,128)S(1)}, f32[512,128]{1,0:T(8,128)S(1)}, u32[]{:S(2)}, u32[]{:S(2)}) collective-permute-start(f32[512,128]{1,0:T(8,128)S(1)} %get-tuple-element.41.vec), channel_id=1, source_target_pairs={{0,2},{1,3},{2,4},{3,5},{4,6},{5,7},{6,8},{7,9},{8,10},{9,11},{10,... | collective-permute-start | bytes 786440 | tf_op jit(solution)/shard_map/ppermute | solution.py:30
  74.4 3.7 %collective-permute-done.13.pair = f32[512,128]{1,0:T(8,128)S(1)} collective-permute-done((f32[512,128]{1,0:T(8,128)S(1)}, f32[512,128]{1,0:T(8,128)S(1)}, u32[]{:S(2)}, u32[]{:S(2)}) %collective-permute-start.13) | collective-permute-done | bytes 262176 | tf_op jit(solution)/shard_map/ppermute | solution.py:379
  78.1 1.3 %collective-permute-start.16 = (f32[512,128]{1,0:T(8,128)S(1)}, f32[512,128]{1,0:T(8,128)S(1)}, u32[]{:S(2)}, u32[]{:S(2)}) collective-permute-start(f32[512,128]{1,0:T(8,128)S(1)} %shard_map.93.after), channel_id=1, source_target_pairs={{2,0},{3,1},{4,2},{5,3},{6,4},{7,5},{8,6},{9,7},{10,8},{11,9},{12,... | collective-permute-start | bytes 786440 | tf_op jit(solution)/shard_map/ppermute | solution.py:30
  79.5 1.6 %collective-permute-start.14 = (f32[256,128]{1,0:T(8,128)S(1)}, f32[256,128]{1,0:T(8,128)S(1)}, u32[]{:S(2)}, u32[]{:S(2)}) collective-permute-start(f32[256,128]{1,0:T(8,128)S(1)} %get-tuple-element.45), channel_id=1, source_target_pairs={{0,1},{1,0},{2,3},{3,2},{4,5},{5,4},{6,7},{7,6},{8,9},{9,8},{10,11... | collective-permute-start | bytes 393224 | tf_op jit(solution)/shard_map/ppermute | solution.py:379
  82.4 2.1 %collective-permute-done.14.one_a = f32[256,128]{1,0:T(8,128)S(1)} collective-permute-done((f32[256,128]{1,0:T(8,128)S(1)}, f32[256,128]{1,0:T(8,128)S(1)}, u32[]{:S(2)}, u32[]{:S(2)}) %collective-permute-start.14) | collective-permute-done | bytes 131104 | tf_op jit(solution)/shard_map/ppermute | solution.py:379
  84.5 2.6 %collective-permute-done.15.one_b = f32[256,128]{1,0:T(8,128)S(1)} collective-permute-done((f32[256,128]{1,0:T(8,128)S(1)}, f32[256,128]{1,0:T(8,128)S(1)}, u32[]{:S(2)}, u32[]{:S(2)}) %collective-permute-start.15) | collective-permute-done | bytes 131104 | tf_op jit(solution)/shard_map/ppermute | solution.py:379
  87.2 2.2 %collective-permute-done.16.up = f32[512,128]{1,0:T(8,128)S(1)} collective-permute-done((f32[512,128]{1,0:T(8,128)S(1)}, f32[512,128]{1,0:T(8,128)S(1)}, u32[]{:S(2)}, u32[]{:S(2)}) %collective-permute-start.16) | collective-permute-done | bytes 262176 | tf_op jit(solution)/shard_map/ppermute | solution.py:30
  90.1 10.9 %all_to_all.10.pieces = f32[32,8,128]{2,1,0:T(8,128)S(1)} all-to-all(f32[32,8,128]{2,1,0:T(8,128)S(1)} %broadcast_in_dim.24), channel_id=1, replica_groups=mesh['row'=4,'col'=8] {'row','col'}, dimensions={0} | all-to-all | bytes 262144 | tf_op jit(solution)/shard_map/all_to_all | solution.py:461
  101.0 1.4 %shard_map.97 = (f32[1024,128]{1,0:T(8,128)}, bf16[1024,128]{1,0:T(8,128)(2,1)S(1)}, f32[2,320,128]{2,1,0:T(8,128)}) custom-call(s32[1]{0:T(128)} %bitcast.row, f32[32,8,128]{2,1,0:T(8,128)S(1)} %all_to_all.10.pieces, f32[1,128]{1,0:T(1,128)S(1)} %bitcast.13, f32[1024,128]{1,0:T(8,128)S(1)} %copy-done, f32[1024,128]{1,0:T(8,128)S(1)} %get-tuple-element.35.vec.v1, ...), custom_call_target="tpu_custom_call" | custom-call | flops 167772160 | bytes 2621440 | tf_op jit(solution)/shard_map/pallas_call | solution.py:336
  105.4 5.2 %collective-permute-done.18 = f32[1,320,128]{2,1,0:T(8,128)S(1)} collective-permute-done((f32[1,320,128]{2,1,0:T(8,128)S(1)}, f32[1,320,128]{2,1,0:T(8,128)S(1)}, u32[]{:S(2)}, u32[]{:S(2)}) %collective-permute-start.18) | collective-permute-done | bytes 163872 | tf_op jit(solution)/shard_map/ppermute | solution.py:379
  110.6 10.7 %all_to_all.11 = f32[8,40,128]{2,1,0:T(8,128)S(1)} all-to-all(f32[8,40,128]{2,1,0:T(8,128)S(1)} %bitcast.16), channel_id=1, replica_groups=mesh['row'=4,'col'=8] {'col'}, dimensions={0} | all-to-all | bytes 327680 | tf_op jit(solution)/shard_map/all_to_all | solution.py:375
  (42 shorter events, 14.6 us)
Async XLA Ops:
  0.6 18.8 %collective-permute-start.1 = (f32[1024,128]{1,0:T(8,128)}, f32[1024,128]{1,0:T(8,128)S(1)}, u32[]{:S(2)}, u32[]{:S(2)}) collective-permute-start(f32[1024,128]{1,0:T(8,128)} %v0.3), channel_id=1, source_target_pairs={{0,2},{1,3},{2,4},{3,5},{4,6},{5,7},{6,8},{7,9},{8,10},{9,11},{10,... | collective-permute-start | bytes 1572872 | tf_op jit(solution)/shard_map/ppermute | solution.py:30
  6.3 5.7 %copy-start = (f32[1024,128]{1,0:T(8,128)S(1)}, f32[1024,128]{1,0:T(8,128)}, u32[]{:S(2)}) copy-start(f32[1024,128]{1,0:T(8,128)} %v0.3) | copy-start | bytes 1572868
  9.9 9.5 %collective-permute-start.2 = (f32[512,128]{1,0:T(8,128)}, f32[512,128]{1,0:T(8,128)S(1)}, u32[]{:S(2)}, u32[]{:S(2)}) collective-permute-start(f32[512,128]{1,0:T(8,128)} %get-tuple-element.33), channel_id=1, source_target_pairs={{0,1},{1,0},{2,3},{3,2},{4,5},{5,4},{6,7},{7,6},{8,9},{9,8},{10,11... | collective-permute-start | bytes 786440 | tf_op jit(solution)/shard_map/ppermute | solution.py:379
  11.4 12.9 %collective-permute-start = (f32[512,128]{1,0:T(8,128)}, f32[512,128]{1,0:T(8,128)S(1)}, u32[]{:S(2)}, u32[]{:S(2)}) collective-permute-start(f32[512,128]{1,0:T(8,128)} %get-tuple-element.27), channel_id=1, source_target_pairs={{0,1},{1,0},{2,3},{3,2},{4,5},{5,4},{6,7},{7,6},{8,9},{9,8},{10,11... | collective-permute-start | bytes 786440 | tf_op jit(solution)/shard_map/ppermute | solution.py:379
  15.7 10.0 %copy-start.2 = (f32[1,1024,1024]{2,1,0:T(8,128)S(1)}, f32[1,1024,1024]{2,1,0:T(8,128)}, u32[]{:S(2)}) copy-start(f32[1,1024,1024]{2,1,0:T(8,128)} %param.8) | copy-start | bytes 12582916
  19.5 17.4 %collective-permute-start.3 = (f32[1024,128]{1,0:T(8,128)S(1)}, f32[1024,128]{1,0:T(8,128)S(1)}, u32[]{:S(2)}, u32[]{:S(2)}) collective-permute-start(f32[1024,128]{1,0:T(8,128)S(1)} %shard_map.80.after), channel_id=1, source_target_pairs={{0,1},{1,0},{2,3},{3,2},{4,5},{5,4},{6,7},{7,6},{8,9},{9,8},{10,11... | collective-permute-start | bytes 1572872 | tf_op jit(solution)/shard_map/ppermute | solution.py:379
  21.1 11.0 %collective-permute-start.4 = (f32[512,128]{1,0:T(8,128)S(1)}, f32[512,128]{1,0:T(8,128)S(1)}, u32[]{:S(2)}, u32[]{:S(2)}) collective-permute-start(f32[512,128]{1,0:T(8,128)S(1)} %shard_map.79.after), channel_id=1, source_target_pairs={{2,0},{3,1},{4,2},{5,3},{6,4},{7,5},{8,6},{9,7},{10,8},{11,9},{12,... | collective-permute-start | bytes 786440 | tf_op jit(solution)/shard_map/ppermute | solution.py:30
  24.4 12.6 %collective-permute-start.5 = (f32[512,128]{1,0:T(8,128)S(1)}, f32[512,128]{1,0:T(8,128)S(1)}, u32[]{:S(2)}, u32[]{:S(2)}) collective-permute-start(f32[512,128]{1,0:T(8,128)S(1)} %shard_map.81.after), channel_id=1, source_target_pairs={{2,0},{3,1},{4,2},{5,3},{6,4},{7,5},{8,6},{9,7},{10,8},{11,9},{12,... | collective-permute-start | bytes 786440 | tf_op jit(solution)/shard_map/ppermute | solution.py:30
  38.2 12.8 %collective-permute-start.7 = (f32[1024,128]{1,0:T(8,128)S(1)}, f32[1024,128]{1,0:T(8,128)S(1)}, u32[]{:S(2)}, u32[]{:S(2)}) collective-permute-start(f32[1024,128]{1,0:T(8,128)S(1)} %get-tuple-element.35.vec.v1), channel_id=1, source_target_pairs={{0,2},{1,3},{2,4},{3,5},{4,6},{5,7},{6,8},{7,9},{8,10},{9,11},{10,... | collective-permute-start | bytes 1572872 | tf_op jit(solution)/shard_map/ppermute | solution.py:30
  40.6 9.3 %collective-permute-start.8 = (f32[512,128]{1,0:T(8,128)S(1)}, f32[512,128]{1,0:T(8,128)S(1)}, u32[]{:S(2)}, u32[]{:S(2)}) collective-permute-start(f32[512,128]{1,0:T(8,128)S(1)} %get-tuple-element.40), channel_id=1, source_target_pairs={{0,1},{1,0},{2,3},{3,2},{4,5},{5,4},{6,7},{7,6},{8,9},{9,8},{10,11... | collective-permute-start | bytes 786440 | tf_op jit(solution)/shard_map/ppermute | solution.py:379
  42.0 12.3 %collective-permute-start.6 = (f32[512,128]{1,0:T(8,128)S(1)}, f32[512,128]{1,0:T(8,128)S(1)}, u32[]{:S(2)}, u32[]{:S(2)}) collective-permute-start(f32[512,128]{1,0:T(8,128)S(1)} %get-tuple-element.38), channel_id=1, source_target_pairs={{0,1},{1,0},{2,3},{3,2},{4,5},{5,4},{6,7},{7,6},{8,9},{9,8},{10,11... | collective-permute-start | bytes 786440 | tf_op jit(solution)/shard_map/ppermute | solution.py:379
  51.1 16.5 %collective-permute-start.9 = (f32[1024,128]{1,0:T(8,128)S(1)}, f32[1024,128]{1,0:T(8,128)S(1)}, u32[]{:S(2)}, u32[]{:S(2)}) collective-permute-start(f32[1024,128]{1,0:T(8,128)S(1)} %shard_map.87.after), channel_id=1, source_target_pairs={{0,1},{1,0},{2,3},{3,2},{4,5},{5,4},{6,7},{7,6},{8,9},{9,8},{10,11... | collective-permute-start | bytes 1572872 | tf_op jit(solution)/shard_map/ppermute | solution.py:379
  51.7 10.3 %collective-permute-start.10 = (f32[512,128]{1,0:T(8,128)S(1)}, f32[512,128]{1,0:T(8,128)S(1)}, u32[]{:S(2)}, u32[]{:S(2)}) collective-permute-start(f32[512,128]{1,0:T(8,128)S(1)} %shard_map.86.after), channel_id=1, source_target_pairs={{2,0},{3,1},{4,2},{5,3},{6,4},{7,5},{8,6},{9,7},{10,8},{11,9},{12,... | collective-permute-start | bytes 786440 | tf_op jit(solution)/shard_map/ppermute | solution.py:30
  54.3 13.3 %collective-permute-start.11 = (f32[512,128]{1,0:T(8,128)S(1)}, f32[512,128]{1,0:T(8,128)S(1)}, u32[]{:S(2)}, u32[]{:S(2)}) collective-permute-start(f32[512,128]{1,0:T(8,128)S(1)} %shard_map.88.after), channel_id=1, source_target_pairs={{2,0},{3,1},{4,2},{5,3},{6,4},{7,5},{8,6},{9,7},{10,8},{11,9},{12,... | collective-permute-start | bytes 786440 | tf_op jit(solution)/shard_map/ppermute | solution.py:30
  68.9 9.2 %collective-permute-start.13 = (f32[512,128]{1,0:T(8,128)S(1)}, f32[512,128]{1,0:T(8,128)S(1)}, u32[]{:S(2)}, u32[]{:S(2)}) collective-permute-start(f32[512,128]{1,0:T(8,128)S(1)} %get-tuple-element.44), channel_id=1, source_target_pairs={{0,1},{1,0},{2,3},{3,2},{4,5},{5,4},{6,7},{7,6},{8,9},{9,8},{10,11... | collective-permute-start | bytes 786440 | tf_op jit(solution)/shard_map/ppermute | solution.py:379
  70.5 8.9 %collective-permute-start.12 = (f32[512,128]{1,0:T(8,128)S(1)}, f32[512,128]{1,0:T(8,128)S(1)}, u32[]{:S(2)}, u32[]{:S(2)}) collective-permute-start(f32[512,128]{1,0:T(8,128)S(1)} %get-tuple-element.41.vec), channel_id=1, source_target_pairs={{0,2},{1,3},{2,4},{3,5},{4,6},{5,7},{6,8},{7,9},{8,10},{9,11},{10,... | collective-permute-start | bytes 786440 | tf_op jit(solution)/shard_map/ppermute | solution.py:30
  78.1 11.2 %collective-permute-start.16 = (f32[512,128]{1,0:T(8,128)S(1)}, f32[512,128]{1,0:T(8,128)S(1)}, u32[]{:S(2)}, u32[]{:S(2)}) collective-permute-start(f32[512,128]{1,0:T(8,128)S(1)} %shard_map.93.after), channel_id=1, source_target_pairs={{2,0},{3,1},{4,2},{5,3},{6,4},{7,5},{8,6},{9,7},{10,8},{11,9},{12,... | collective-permute-start | bytes 786440 | tf_op jit(solution)/shard_map/ppermute | solution.py:30
  79.5 5.0 %collective-permute-start.14 = (f32[256,128]{1,0:T(8,128)S(1)}, f32[256,128]{1,0:T(8,128)S(1)}, u32[]{:S(2)}, u32[]{:S(2)}) collective-permute-start(f32[256,128]{1,0:T(8,128)S(1)} %get-tuple-element.45), channel_id=1, source_target_pairs={{0,1},{1,0},{2,3},{3,2},{4,5},{5,4},{6,7},{7,6},{8,9},{9,8},{10,11... | collective-permute-start | bytes 393224 | tf_op jit(solution)/shard_map/ppermute | solution.py:379
  81.1 6.1 %collective-permute-start.15 = (f32[256,128]{1,0:T(8,128)S(1)}, f32[256,128]{1,0:T(8,128)S(1)}, u32[]{:S(2)}, u32[]{:S(2)}) collective-permute-start(f32[256,128]{1,0:T(8,128)S(1)} %get-tuple-element.46.after), channel_id=1, source_target_pairs={{0,1},{1,0},{2,3},{3,2},{4,5},{5,4},{6,7},{7,6},{8,9},{9,8},{10,11... | collective-permute-start | bytes 393224 | tf_op jit(solution)/shard_map/ppermute | solution.py:379
  82.4 18.6 %copy-start.1 = (bf16[1280,1024]{1,0:T(8,128)(2,1)S(1)}, bf16[1280,1024]{1,0:T(8,128)(2,1)}, u32[]{:S(2)}) copy-start(bf16[1280,1024]{1,0:T(8,128)(2,1)} %genotypes.3) | copy-start | bytes 7864324
  82.4 18.6 %copy-start.3 = (f32[128]{0:T(128)S(1)}, f32[128]{0:T(128)}, u32[]{:S(2)}) copy-start(f32[128]{0:T(128)} %param.7) | copy-start | bytes 1540
  102.4 1.8 %collective-permute-start.17 = (f32[2,320,128]{2,1,0:T(8,128)}, f32[2,320,128]{2,1,0:T(8,128)S(1)}, u32[]{:S(2)}, u32[]{:S(2)}) collective-permute-start(f32[2,320,128]{2,1,0:T(8,128)} %get-tuple-element.49), channel_id=1, source_target_pairs={{0,8},{1,9},{2,10},{3,11},{4,12},{5,13},{6,14},{7,15},{8,0},{9,1},... | collective-permute-start | bytes 983048 | tf_op jit(solution)/shard_map/ppermute | solution.py:379
  104.3 6.3 %collective-permute-start.18 = (f32[1,320,128]{2,1,0:T(8,128)S(1)}, f32[1,320,128]{2,1,0:T(8,128)S(1)}, u32[]{:S(2)}, u32[]{:S(2)}) collective-permute-start(f32[1,320,128]{2,1,0:T(8,128)S(1)} %get-tuple-element.51), channel_id=1, source_target_pairs={{0,16},{1,17},{2,18},{3,19},{4,20},{5,21},{6,22},{7,23},{8,24},{9,... | collective-permute-start | bytes 491528 | tf_op jit(solution)/shard_map/ppermute | solution.py:379
where the time goes:
time: 122 us
  waiting for transfers between devices  52 us (43%)
  starting transfers between devices  28 us (23%)
  blocking collectives  21.6 us (18%)
  Pallas kernels  18.1 us (15%)
  between operations  1.54 us (1%)
    ppermute x11, waiting for transfers between devices, routed(): return lax.ppermute(block, AXES, pairs)  28.9 us
    ppermute x8, waiting for transfers between devices, shifted(): return lax.ppermute(block, AXES, route)  23.1 us
    ppermute x8, starting transfers between devices, shifted(): return lax.ppermute(block, AXES, route)  16.7 us
    ppermute x11, starting transfers between devices, routed(): return lax.ppermute(block, AXES, pairs)  11.2 us
    all_to_all x1, blocking collectives, body(): lax.all_to_all(jnp.broadcast_to(moments[None], (n,) + moments.shape), AXE...  10.9 us
    all_to_all x1, blocking collectives, scattered_over(): return jnp.sum(lax.all_to_all(pieces, axis, 0, 0, tiled=True), axis=0)  10.7 us
    pallas_call x2, Pallas kernels, from_tiles(): pl.pallas_call(kernel, in_specs=[SMEM] * 2 + [pl.BlockSpec(memory_space=p...  7.32 us
  transfers between devices with their start and end apart: 19, of which 15 were waited for; matrix products, arithmetic and copies ran while one was open for 0% of the time, Pallas kernels for 11%

commit v1 on v0

--- a/solution.py
+++ b/solution.py
@@ -369,10 +369,69 @@
     )(index, keep, received)
 
 
-def scattered_over(values, axis):
-    n = lax.axis_size(axis)
-    pieces = values.reshape((n, values.shape[0] // n) + values.shape[1:])
-    return jnp.sum(lax.all_to_all(pieces, axis, 0, 0, tiled=True), axis=0)
+def local(kernel, outs, operands, scalars=0, after=None, scratch=()):
+    count = len(operands)
+
+    def run(*refs):
+        kernel(*refs[:count], *refs[count + (after is not None) :])
+
+    specs = [SMEM] * scalars + [VMEM] * (count - scalars)
+    return pl.pallas_call(
+        run,
+        in_specs=specs + ([ANY] if after is not None else []),
+        out_specs=[VMEM] * len(outs),
+        out_shape=outs,
+        scratch_shapes=scratch,
+        compiler_params=params(),
+        cost_estimate=cost(1, 1),
+    )(*operands, *([after] if after is not None else []))
+
+
+def reduced_over_chips(site, keep, received):
+    cols = lax.axis_size("col")
+    rows, k = keep.shape[1] // cols, keep.shape[2]
+    deep = cols // 2
+    half = deep // 2
+    keep, received = [value.reshape(2, deep, 2, rows, k) for value in (keep, received)]
+
+    def shape(*lead):
+        return jax.ShapeDtypeStruct((*lead, rows, k), F32)
+
+    def spread_kernel(site, keep, received, a_mine, a_other, b_mine, b_other):
+        y, x = site[0], site[1]
+        for z in range(half):
+            for there in range(2):
+                a_mine[z, there] = keep[y, z, there] + received[y, z, there]
+                a_other[z, there] = keep[1 - y, z, there] + received[1 - y, z, there]
+                b_mine[there, z] = keep[there, half + z, x] + received[there, half + z, x]
+                b_other[there, z] = keep[there, half + z, 1 - x] + received[there, half + z, 1 - x]
+
+    def cross_kernel(site, a, a_in, b, b_in, a_mine, a_other, b_mine, b_other):
+        y, x = site[0], site[1]
+        for z in range(half):
+            a_mine[z] = a[z, x] + a_in[z, x]
+            a_other[z] = a[z, 1 - x] + a_in[z, 1 - x]
+            b_mine[z] = b[y, z] + b_in[y, z]
+            b_other[z] = b[1 - y, z] + b_in[1 - y, z]
+
+    def along_kernel(site, a, a_in, b, b_in, mine, *rest):
+        *others, total = rest
+        total[:half] = a[...] + a_in[...]
+        total[half:] = b[...] + b_in[...]
+        mine[...] = total[site[2]]
+        for step, other in enumerate(others):
+            other[...] = total[jnp.bitwise_xor(site[2], step + 1)]
+
+    outs = [shape(half, 2)] * 2 + [shape(2, half)] * 2
+    a, a_other, b, b_other = local(spread_kernel, outs, [site, keep, received], 1)
+    a_in, b_in = swapped(a_other, 2 * cols), swapped(b_other, 1)
+    a, a_other, b, b_other = local(cross_kernel, [shape(half)] * 4, [site, a, a_in, b, b_in], 1)
+    a_in, b_in = swapped(a_other, 1), swapped(b_other, 2 * cols)
+    scratch = [pltpu.VMEM((deep, rows, k), F32)]
+    mine, *others = local(along_kernel, [shape()] * deep, [site, a, a_in, b, b_in], 1, scratch=scratch)
+    for step, other in enumerate(others):
+        mine = mine + swapped(other, 2 * (step + 1))
+    return mine
 
 
 def routed(block, pairs):
@@ -463,15 +522,14 @@
     effects, send, keep = partial_scores(row.astype(jnp.int32)[None], rows, pieces, penalty[None], v0, v1, v2, genotypes)
     received = swapped(send, cols)
     bit = rows // 4
-    while bit:
-        mine = (row // (2 * bit)) % 2
-        keep = keep.reshape((2, -1) + keep.shape[1:])
-        received = received.reshape((2, -1) + received.shape[1:])
-
-        keep, send = pick(mine.astype(jnp.int32)[None], keep, received)
+    while bit > 1:
+        keep, received = [value.reshape((2, -1) + value.shape[1:]) for value in (keep, received)]
+        keep, send = pick((row // (2 * bit) % 2).astype(jnp.int32)[None], keep, received)
         received = swapped(send, 2 * bit * cols)
         bit //= 2
-    return effects, scattered_over((keep + received)[0], "col")
+    col = lax.axis_index("col")
+    chip = jnp.stack([row // 2 % 2, col % 2, col // 2]).astype(jnp.int32)
+    return effects, reduced_over_chips(chip, keep, received)
 
 
 def solution(mesh):

time: 122 us -> 125 us (1.025)
  blocking collectives: 21.6 us -> 10.9 us
  starting transfers between devices: 28 us -> 35.6 us
  waiting for transfers between devices: 52 us -> 55.8 us
  Pallas kernels: 18.1 us -> 19.8 us
    all_to_all x1 -> x0, blocking collectives: 10.7 us -> none  [scattered_over(): return jnp.sum(lax.all_to_all(pieces, axis, 0, 0, tiled=True), axis=0)]
    ppermute x11 -> x17, starting transfers between devices: 11.2 us -> 18.9 us  [routed(): return lax.ppermute(block, AXES, pairs)]
    ppermute x11 -> x17, waiting for transfers between devices: 28.9 us -> 32.7 us  [routed(): return lax.ppermute(block, AXES, pairs)]
    pallas_call x1 -> x3, Pallas kernels: 0.03 us -> 1.71 us  [local(): pl.pallas_call(run, in_specs=specs + ([ANY] if after is not None else [])...]
  transfers between devices with their start and end apart: 19 -> 25, of which waited for: 15 -> 20; matrix products, arithmetic and copies ran while one was open for 0% -> 0% of each run, Pallas kernels for 11% -> 11%
where the time goes in v1:
time: 125 us; the launch traced here: 124 us
  waiting for transfers between devices  55.8 us (45%)
  starting transfers between devices  35.6 us (28%)
  Pallas kernels  19.8 us (16%)
  blocking collectives  10.9 us (9%)
  between operations  1.56 us (1%)
    ppermute x17, waiting for transfers between devices, routed(): return lax.ppermute(block, AXES, pairs)  32.7 us
    ppermute x8, waiting for transfers between devices, shifted(): return lax.ppermute(block, AXES, route)  23.1 us
    ppermute x17, starting transfers between devices, routed(): return lax.ppermute(block, AXES, pairs)  18.9 us
    ppermute x8, starting transfers between devices, shifted(): return lax.ppermute(block, AXES, route)  16.7 us
    all_to_all x1, blocking collectives, body(): lax.all_to_all(jnp.broadcast_to(moments[None], (n,) + moments.shape), AXE...  10.9 us
    pallas_call x2, Pallas kernels, from_tiles(): pl.pallas_call(kernel, in_specs=[SMEM] * 2 + [pl.BlockSpec(memory_space=p...  7.33 us
  transfers between devices with their start and end apart: 25, of which 20 were waited for; matrix products, arithmetic and copies ran while one was open for 0% of the time, Pallas kernels for 11%

profile of v1, /device:TPU:0, one launch (start us, length us, event | category | flops | bytes accessed | tf_op | source)
XLA Modules:
  0.0 124.5 jit_solution(5841346920051693711)
XLA Ops:
  0.6 5.0 %collective-permute-start.1 = (f32[1024,128]{1,0:T(8,128)}, f32[1024,128]{1,0:T(8,128)S(1)}, u32[]{:S(2)}, u32[]{:S(2)}) collective-permute-start(f32[1024,128]{1,0:T(8,128)} %v0.3), channel_id=1, source_target_pairs={{0,2},{1,3},{2,4},{3,5},{4,6},{5,7},{6,8},{7,9},{8,10},{9,11},{10,... | collective-permute-start | bytes 1572872 | tf_op jit(solution)/shard_map/ppermute | solution.py:30
  6.3 3.6 %shard_map.77 = (f32[512,128]{1,0:T(8,128)}, f32[512,128]{1,0:T(8,128)}) custom-call(s32[1]{0:T(128)S(6)} %copy.8.band, s32[1]{0:T(128)} %bitcast.2.position, f32[1024,128]{1,0:T(8,128)} %v0.3, f32[2,1024,1024]{2,1,0:T(8,128)} %bitcast.15), custom_call_target="tpu_custom_call" | custom-call | flops 268435456 | bytes 4194304 | tf_op jit(solution)/shard_map/pallas_call | solution.py:103
  9.9 1.6 %collective-permute-start.2 = (f32[512,128]{1,0:T(8,128)}, f32[512,128]{1,0:T(8,128)S(1)}, u32[]{:S(2)}, u32[]{:S(2)}) collective-permute-start(f32[512,128]{1,0:T(8,128)} %get-tuple-element.43), channel_id=1, source_target_pairs={{0,1},{1,0},{2,3},{3,2},{4,5},{5,4},{6,7},{7,6},{8,9},{9,8},{10,11... | collective-permute-start | bytes 786440 | tf_op jit(solution)/shard_map/ppermute | solution.py:438
  12.0 3.7 %shard_map.78 = (f32[512,128]{1,0:T(8,128)S(1)}, f32[512,128]{1,0:T(8,128)S(1)}, bf16[1024,1024]{1,0:T(8,128)(2,1)S(1)}, bf16[1024,1024]{1,0:T(8,128)(2,1)S(1)}) custom-call(s32[1]{0:T(128)S(6)} %copy.8.band, s32[1]{0:T(128)} %bitcast.2.position, f32[1024,128]{1,0:T(8,128)S(1)} %copy-done, f32[2,1024,1024]{2,1,0:T(8,128)} %bitcast.16), custom_call_target="tpu_custom_call" | custom-call | flops 268435456 | bytes 8388608 | tf_op jit(solution)/shard_map/pallas_call | solution.py:103
  15.7 3.7 %collective-permute-done.2.pair.pair_a = f32[512,128]{1,0:T(8,128)S(1)} collective-permute-done((f32[512,128]{1,0:T(8,128)}, f32[512,128]{1,0:T(8,128)S(1)}, u32[]{:S(2)}, u32[]{:S(2)}) %collective-permute-start.2) | collective-permute-done | bytes 262176 | tf_op jit(solution)/shard_map/ppermute | solution.py:438
  19.5 1.6 %collective-permute-start.3 = (f32[1024,128]{1,0:T(8,128)S(1)}, f32[1024,128]{1,0:T(8,128)S(1)}, u32[]{:S(2)}, u32[]{:S(2)}) collective-permute-start(f32[1024,128]{1,0:T(8,128)S(1)} %shard_map.80.after), channel_id=1, source_target_pairs={{0,1},{1,0},{2,3},{3,2},{4,5},{5,4},{6,7},{7,6},{8,9},{9,8},{10,11... | collective-permute-start | bytes 1572872 | tf_op jit(solution)/shard_map/ppermute | solution.py:438
  22.4 2.0 %collective-permute-done.pair.pair_b = f32[512,128]{1,0:T(8,128)S(1)} collective-permute-done((f32[512,128]{1,0:T(8,128)}, f32[512,128]{1,0:T(8,128)S(1)}, u32[]{:S(2)}, u32[]{:S(2)}) %collective-permute-start) | collective-permute-done | bytes 262176 | tf_op jit(solution)/shard_map/ppermute | solution.py:438
  24.4 1.3 %collective-permute-start.5 = (f32[512,128]{1,0:T(8,128)S(1)}, f32[512,128]{1,0:T(8,128)S(1)}, u32[]{:S(2)}, u32[]{:S(2)}) collective-permute-start(f32[512,128]{1,0:T(8,128)S(1)} %shard_map.81.after), channel_id=1, source_target_pairs={{2,0},{3,1},{4,2},{5,3},{6,4},{7,5},{8,6},{9,7},{10,8},{11,9},{12,... | collective-permute-start | bytes 786440 | tf_op jit(solution)/shard_map/ppermute | solution.py:30
  25.7 1.4 %shard_map.82 = (bf16[1024,1024]{1,0:T(8,128)(2,1)S(1)}, f32[1024,128]{1,0:T(8,128)S(1)}) custom-call(f32[1024,128]{1,0:T(8,128)S(1)} %copy-done, f32[1024,1024]{1,0:T(8,128)S(1)} %bitcast.11, f32[512,128]{1,0:T(8,128)S(1)} %shard_map.81.after), custom_call_target="tpu_custom_call" | custom-call | flops 268435456 | bytes 6291456 | tf_op jit(solution)/shard_map/pallas_call | solution.py:179
  27.8 4.3 %collective-permute-done.4.ahead_a = f32[512,128]{1,0:T(8,128)S(1)} collective-permute-done((f32[512,128]{1,0:T(8,128)S(1)}, f32[512,128]{1,0:T(8,128)S(1)}, u32[]{:S(2)}, u32[]{:S(2)}) %collective-permute-start.4) | collective-permute-done | bytes 262176 | tf_op jit(solution)/shard_map/ppermute | solution.py:30
  32.1 4.8 %collective-permute-done.5.ahead_b = f32[512,128]{1,0:T(8,128)S(1)} collective-permute-done((f32[512,128]{1,0:T(8,128)S(1)}, f32[512,128]{1,0:T(8,128)S(1)}, u32[]{:S(2)}, u32[]{:S(2)}) %collective-permute-start.5) | collective-permute-done | bytes 262176 | tf_op jit(solution)/shard_map/ppermute | solution.py:30
  36.9 1.3 %shard_map.84 = (f32[1024,128]{1,0:T(8,128)S(1)}, f32[512,128]{1,0:T(8,128)}) custom-call(s32[1]{0:T(128)} %bitcast.1.odd, f32[1024,128]{1,0:T(8,128)S(1)} %shard_map.83.part, bf16[1024,1024]{1,0:T(8,128)(2,1)S(1)} %get-tuple-element.39.low.low_one, f32[1024,128]{1,0:T(8,128)S(1)} %collective-permute-done.3.one, ...), custom_call_target="tpu_custom_call" | custom-call | flops 268435456 | bytes 2097152 | tf_op jit(solution)/shard_map/pallas_call | solution.py:217
  38.2 1.5 %collective-permute-start.7 = (f32[1024,128]{1,0:T(8,128)S(1)}, f32[1024,128]{1,0:T(8,128)S(1)}, u32[]{:S(2)}, u32[]{:S(2)}) collective-permute-start(f32[1024,128]{1,0:T(8,128)S(1)} %get-tuple-element.45.vec.v1), channel_id=1, source_target_pairs={{0,2},{1,3},{2,4},{3,5},{4,6},{5,7},{6,8},{7,9},{8,10},{9,11},{10,... | collective-permute-start | bytes 1572872 | tf_op jit(solution)/shard_map/ppermute | solution.py:30
  40.6 1.4 %collective-permute-start.8 = (f32[512,128]{1,0:T(8,128)S(1)}, f32[512,128]{1,0:T(8,128)S(1)}, u32[]{:S(2)}, u32[]{:S(2)}) collective-permute-start(f32[512,128]{1,0:T(8,128)S(1)} %get-tuple-element.50), channel_id=1, source_target_pairs={{0,1},{1,0},{2,3},{3,2},{4,5},{5,4},{6,7},{7,6},{8,9},{9,8},{10,11... | collective-permute-start | bytes 786440 | tf_op jit(solution)/shard_map/ppermute | solution.py:438
  42.7 7.2 %collective-permute-done.8.pair.pair_a = f32[512,128]{1,0:T(8,128)S(1)} collective-permute-done((f32[512,128]{1,0:T(8,128)S(1)}, f32[512,128]{1,0:T(8,128)S(1)}, u32[]{:S(2)}, u32[]{:S(2)}) %collective-permute-start.8) | collective-permute-done | bytes 262176 | tf_op jit(solution)/shard_map/ppermute | solution.py:438
  54.3 1.3 %collective-permute-start.11 = (f32[512,128]{1,0:T(8,128)S(1)}, f32[512,128]{1,0:T(8,128)S(1)}, u32[]{:S(2)}, u32[]{:S(2)}) collective-permute-start(f32[512,128]{1,0:T(8,128)S(1)} %shard_map.88.after), channel_id=1, source_target_pairs={{2,0},{3,1},{4,2},{5,3},{6,4},{7,5},{8,6},{9,7},{10,8},{11,9},{12,... | collective-permute-start | bytes 786440 | tf_op jit(solution)/shard_map/ppermute | solution.py:30
  57.0 5.0 %collective-permute-done.10.ahead_a = f32[512,128]{1,0:T(8,128)S(1)} collective-permute-done((f32[512,128]{1,0:T(8,128)S(1)}, f32[512,128]{1,0:T(8,128)S(1)}, u32[]{:S(2)}, u32[]{:S(2)}) %collective-permute-start.10) | collective-permute-done | bytes 262176 | tf_op jit(solution)/shard_map/ppermute | solution.py:30
  62.0 5.6 %collective-permute-done.11.ahead_b = f32[512,128]{1,0:T(8,128)S(1)} collective-permute-done((f32[512,128]{1,0:T(8,128)S(1)}, f32[512,128]{1,0:T(8,128)S(1)}, u32[]{:S(2)}, u32[]{:S(2)}) %collective-permute-start.11) | collective-permute-done | bytes 262176 | tf_op jit(solution)/shard_map/ppermute | solution.py:30
  68.9 1.6 %collective-permute-start.13 = (f32[512,128]{1,0:T(8,128)S(1)}, f32[512,128]{1,0:T(8,128)S(1)}, u32[]{:S(2)}, u32[]{:S(2)}) collective-permute-start(f32[512,128]{1,0:T(8,128)S(1)} %get-tuple-element.54), channel_id=1, source_target_pairs={{0,1},{1,0},{2,3},{3,2},{4,5},{5,4},{6,7},{7,6},{8,9},{9,8},{10,11... | collective-permute-start | bytes 786440 | tf_op jit(solution)/shard_map/ppermute | solution.py:438
  70.5 3.8 %collective-permute-start.12 = (f32[512,128]{1,0:T(8,128)S(1)}, f32[512,128]{1,0:T(8,128)S(1)}, u32[]{:S(2)}, u32[]{:S(2)}) collective-permute-start(f32[512,128]{1,0:T(8,128)S(1)} %get-tuple-element.51.vec), channel_id=1, source_target_pairs={{0,2},{1,3},{2,4},{3,5},{4,6},{5,7},{6,8},{7,9},{8,10},{9,11},{10,... | collective-permute-start | bytes 786440 | tf_op jit(solution)/shard_map/ppermute | solution.py:30
  74.4 3.7 %collective-permute-done.13.pair = f32[512,128]{1,0:T(8,128)S(1)} collective-permute-done((f32[512,128]{1,0:T(8,128)S(1)}, f32[512,128]{1,0:T(8,128)S(1)}, u32[]{:S(2)}, u32[]{:S(2)}) %collective-permute-start.13) | collective-permute-done | bytes 262176 | tf_op jit(solution)/shard_map/ppermute | solution.py:438
  78.1 1.3 %collective-permute-start.16 = (f32[512,128]{1,0:T(8,128)S(1)}, f32[512,128]{1,0:T(8,128)S(1)}, u32[]{:S(2)}, u32[]{:S(2)}) collective-permute-start(f32[512,128]{1,0:T(8,128)S(1)} %shard_map.93.after), channel_id=1, source_target_pairs={{2,0},{3,1},{4,2},{5,3},{6,4},{7,5},{8,6},{9,7},{10,8},{11,9},{12,... | collective-permute-start | bytes 786440 | tf_op jit(solution)/shard_map/ppermute | solution.py:30
  79.5 1.6 %collective-permute-start.14 = (f32[256,128]{1,0:T(8,128)S(1)}, f32[256,128]{1,0:T(8,128)S(1)}, u32[]{:S(2)}, u32[]{:S(2)}) collective-permute-start(f32[256,128]{1,0:T(8,128)S(1)} %get-tuple-element.55), channel_id=1, source_target_pairs={{0,1},{1,0},{2,3},{3,2},{4,5},{5,4},{6,7},{7,6},{8,9},{9,8},{10,11... | collective-permute-start | bytes 393224 | tf_op jit(solution)/shard_map/ppermute | solution.py:438
  82.4 2.1 %collective-permute-done.14.one_a = f32[256,128]{1,0:T(8,128)S(1)} collective-permute-done((f32[256,128]{1,0:T(8,128)S(1)}, f32[256,128]{1,0:T(8,128)S(1)}, u32[]{:S(2)}, u32[]{:S(2)}) %collective-permute-start.14) | collective-permute-done | bytes 131104 | tf_op jit(solution)/shard_map/ppermute | solution.py:438
  84.5 2.6 %collective-permute-done.15.one_b = f32[256,128]{1,0:T(8,128)S(1)} collective-permute-done((f32[256,128]{1,0:T(8,128)S(1)}, f32[256,128]{1,0:T(8,128)S(1)}, u32[]{:S(2)}, u32[]{:S(2)}) %collective-permute-start.15) | collective-permute-done | bytes 131104 | tf_op jit(solution)/shard_map/ppermute | solution.py:438
  87.1 2.2 %collective-permute-done.16.up = f32[512,128]{1,0:T(8,128)S(1)} collective-permute-done((f32[512,128]{1,0:T(8,128)S(1)}, f32[512,128]{1,0:T(8,128)S(1)}, u32[]{:S(2)}, u32[]{:S(2)}) %collective-permute-start.16) | collective-permute-done | bytes 262176 | tf_op jit(solution)/shard_map/ppermute | solution.py:30
  90.1 10.9 %all_to_all.5.pieces = f32[32,8,128]{2,1,0:T(8,128)S(1)} all-to-all(f32[32,8,128]{2,1,0:T(8,128)S(1)} %broadcast_in_dim.21), channel_id=1, replica_groups=mesh['row'=4,'col'=8] {'row','col'}, dimensions={0} | all-to-all | bytes 262144 | tf_op jit(solution)/shard_map/all_to_all | solution.py:520
  101.1 1.4 %shard_map.97 = (f32[1024,128]{1,0:T(8,128)}, bf16[1024,128]{1,0:T(8,128)(2,1)S(1)}, f32[2,320,128]{2,1,0:T(8,128)}) custom-call(s32[1]{0:T(128)} %bitcast.row, f32[32,8,128]{2,1,0:T(8,128)S(1)} %all_to_all.5.pieces, f32[1,128]{1,0:T(1,128)S(1)} %bitcast.14, f32[1024,128]{1,0:T(8,128)S(1)} %copy-done, f32[1024,128]{1,0:T(8,128)S(1)} %get-tuple-element.45.vec.v1, ...), custom_call_target="tpu_custom_call" | custom-call | flops 167772160 | bytes 2621440 | tf_op jit(solution)/shard_map/pallas_call | solution.py:336
  106.9 2.5 %collective-permute-done.18.refs_2_ = f32[2,2,40,128]{3,2,1,0:T(8,128)S(1)} collective-permute-done((f32[2,2,40,128]{3,2,1,0:T(8,128)S(1)}, f32[2,2,40,128]{3,2,1,0:T(8,128)S(1)}, u32[]{:S(2)}, u32[]{:S(2)}) %collective-permute-start.18) | collective-permute-done | bytes 81952 | tf_op jit(solution)/shard_map/ppermute | solution.py:438
  113.3 1.8 %collective-permute-done.20.refs_2_ = f32[2,40,128]{2,1,0:T(8,128)S(1)} collective-permute-done((f32[2,40,128]{2,1,0:T(8,128)S(1)}, f32[2,40,128]{2,1,0:T(8,128)S(1)}, u32[]{:S(2)}, u32[]{:S(2)}) %collective-permute-start.20) | collective-permute-done | bytes 40992 | tf_op jit(solution)/shard_map/ppermute | solution.py:438
  118.3 2.7 %collective-permute-start.24 = (f32[40,128]{1,0:T(8,128)S(1)}, f32[40,128]{1,0:T(8,128)S(1)}, u32[]{:S(2)}, u32[]{:S(2)}) collective-permute-start(f32[40,128]{1,0:T(8,128)S(1)} %get-tuple-element.71), channel_id=1, source_target_pairs={{0,6},{1,7},{2,4},{3,5},{4,2},{5,3},{6,0},{7,1},{8,14},{9,15},{10,... | collective-permute-start | bytes 61448 | tf_op jit(solution)/shard_map/ppermute | solution.py:438
  121.8 2.1 %collective-permute-done.24 = f32[40,128]{1,0:T(8,128)S(1)} collective-permute-done((f32[40,128]{1,0:T(8,128)S(1)}, f32[40,128]{1,0:T(8,128)S(1)}, u32[]{:S(2)}, u32[]{:S(2)}) %collective-permute-start.24) | collective-permute-done | bytes 20512 | tf_op jit(solution)/shard_map/ppermute | solution.py:438
  (55 shorter events, 26.4 us)
Async XLA Ops:
  0.6 18.8 %collective-permute-start.1 = (f32[1024,128]{1,0:T(8,128)}, f32[1024,128]{1,0:T(8,128)S(1)}, u32[]{:S(2)}, u32[]{:S(2)}) collective-permute-start(f32[1024,128]{1,0:T(8,128)} %v0.3), channel_id=1, source_target_pairs={{0,2},{1,3},{2,4},{3,5},{4,6},{5,7},{6,8},{7,9},{8,10},{9,11},{10,... | collective-permute-start | bytes 1572872 | tf_op jit(solution)/shard_map/ppermute | solution.py:30
  6.3 5.7 %copy-start = (f32[1024,128]{1,0:T(8,128)S(1)}, f32[1024,128]{1,0:T(8,128)}, u32[]{:S(2)}) copy-start(f32[1024,128]{1,0:T(8,128)} %v0.3) | copy-start | bytes 1572868
  9.9 9.5 %collective-permute-start.2 = (f32[512,128]{1,0:T(8,128)}, f32[512,128]{1,0:T(8,128)S(1)}, u32[]{:S(2)}, u32[]{:S(2)}) collective-permute-start(f32[512,128]{1,0:T(8,128)} %get-tuple-element.43), channel_id=1, source_target_pairs={{0,1},{1,0},{2,3},{3,2},{4,5},{5,4},{6,7},{7,6},{8,9},{9,8},{10,11... | collective-permute-start | bytes 786440 | tf_op jit(solution)/shard_map/ppermute | solution.py:438
  11.4 12.9 %collective-permute-start = (f32[512,128]{1,0:T(8,128)}, f32[512,128]{1,0:T(8,128)S(1)}, u32[]{:S(2)}, u32[]{:S(2)}) collective-permute-start(f32[512,128]{1,0:T(8,128)} %get-tuple-element.37), channel_id=1, source_target_pairs={{0,1},{1,0},{2,3},{3,2},{4,5},{5,4},{6,7},{7,6},{8,9},{9,8},{10,11... | collective-permute-start | bytes 786440 | tf_op jit(solution)/shard_map/ppermute | solution.py:438
  15.7 10.0 %copy-start.2 = (f32[1,1024,1024]{2,1,0:T(8,128)S(1)}, f32[1,1024,1024]{2,1,0:T(8,128)}, u32[]{:S(2)}) copy-start(f32[1,1024,1024]{2,1,0:T(8,128)} %param.8) | copy-start | bytes 12582916
  19.5 17.4 %collective-permute-start.3 = (f32[1024,128]{1,0:T(8,128)S(1)}, f32[1024,128]{1,0:T(8,128)S(1)}, u32[]{:S(2)}, u32[]{:S(2)}) collective-permute-start(f32[1024,128]{1,0:T(8,128)S(1)} %shard_map.80.after), channel_id=1, source_target_pairs={{0,1},{1,0},{2,3},{3,2},{4,5},{5,4},{6,7},{7,6},{8,9},{9,8},{10,11... | collective-permute-start | bytes 1572872 | tf_op jit(solution)/shard_map/ppermute | solution.py:438
  21.1 11.0 %collective-permute-start.4 = (f32[512,128]{1,0:T(8,128)S(1)}, f32[512,128]{1,0:T(8,128)S(1)}, u32[]{:S(2)}, u32[]{:S(2)}) collective-permute-start(f32[512,128]{1,0:T(8,128)S(1)} %shard_map.79.after), channel_id=1, source_target_pairs={{2,0},{3,1},{4,2},{5,3},{6,4},{7,5},{8,6},{9,7},{10,8},{11,9},{12,... | collective-permute-start | bytes 786440 | tf_op jit(solution)/shard_map/ppermute | solution.py:30
  24.4 12.6 %collective-permute-start.5 = (f32[512,128]{1,0:T(8,128)S(1)}, f32[512,128]{1,0:T(8,128)S(1)}, u32[]{:S(2)}, u32[]{:S(2)}) collective-permute-start(f32[512,128]{1,0:T(8,128)S(1)} %shard_map.81.after), channel_id=1, source_target_pairs={{2,0},{3,1},{4,2},{5,3},{6,4},{7,5},{8,6},{9,7},{10,8},{11,9},{12,... | collective-permute-start | bytes 786440 | tf_op jit(solution)/shard_map/ppermute | solution.py:30
  38.2 12.8 %collective-permute-start.7 = (f32[1024,128]{1,0:T(8,128)S(1)}, f32[1024,128]{1,0:T(8,128)S(1)}, u32[]{:S(2)}, u32[]{:S(2)}) collective-permute-start(f32[1024,128]{1,0:T(8,128)S(1)} %get-tuple-element.45.vec.v1), channel_id=1, source_target_pairs={{0,2},{1,3},{2,4},{3,5},{4,6},{5,7},{6,8},{7,9},{8,10},{9,11},{10,... | collective-permute-start | bytes 1572872 | tf_op jit(solution)/shard_map/ppermute | solution.py:30
  40.6 9.3 %collective-permute-start.8 = (f32[512,128]{1,0:T(8,128)S(1)}, f32[512,128]{1,0:T(8,128)S(1)}, u32[]{:S(2)}, u32[]{:S(2)}) collective-permute-start(f32[512,128]{1,0:T(8,128)S(1)} %get-tuple-element.50), channel_id=1, source_target_pairs={{0,1},{1,0},{2,3},{3,2},{4,5},{5,4},{6,7},{7,6},{8,9},{9,8},{10,11... | collective-permute-start | bytes 786440 | tf_op jit(solution)/shard_map/ppermute | solution.py:438
  42.0 12.3 %collective-permute-start.6 = (f32[512,128]{1,0:T(8,128)S(1)}, f32[512,128]{1,0:T(8,128)S(1)}, u32[]{:S(2)}, u32[]{:S(2)}) collective-permute-start(f32[512,128]{1,0:T(8,128)S(1)} %get-tuple-element.48), channel_id=1, source_target_pairs={{0,1},{1,0},{2,3},{3,2},{4,5},{5,4},{6,7},{7,6},{8,9},{9,8},{10,11... | collective-permute-start | bytes 786440 | tf_op jit(solution)/shard_map/ppermute | solution.py:438
  51.1 16.5 %collective-permute-start.9 = (f32[1024,128]{1,0:T(8,128)S(1)}, f32[1024,128]{1,0:T(8,128)S(1)}, u32[]{:S(2)}, u32[]{:S(2)}) collective-permute-start(f32[1024,128]{1,0:T(8,128)S(1)} %shard_map.87.after), channel_id=1, source_target_pairs={{0,1},{1,0},{2,3},{3,2},{4,5},{5,4},{6,7},{7,6},{8,9},{9,8},{10,11... | collective-permute-start | bytes 1572872 | tf_op jit(solution)/shard_map/ppermute | solution.py:438
  51.7 10.3 %collective-permute-start.10 = (f32[512,128]{1,0:T(8,128)S(1)}, f32[512,128]{1,0:T(8,128)S(1)}, u32[]{:S(2)}, u32[]{:S(2)}) collective-permute-start(f32[512,128]{1,0:T(8,128)S(1)} %shard_map.86.after), channel_id=1, source_target_pairs={{2,0},{3,1},{4,2},{5,3},{6,4},{7,5},{8,6},{9,7},{10,8},{11,9},{12,... | collective-permute-start | bytes 786440 | tf_op jit(solution)/shard_map/ppermute | solution.py:30
  54.3 13.3 %collective-permute-start.11 = (f32[512,128]{1,0:T(8,128)S(1)}, f32[512,128]{1,0:T(8,128)S(1)}, u32[]{:S(2)}, u32[]{:S(2)}) collective-permute-start(f32[512,128]{1,0:T(8,128)S(1)} %shard_map.88.after), channel_id=1, source_target_pairs={{2,0},{3,1},{4,2},{5,3},{6,4},{7,5},{8,6},{9,7},{10,8},{11,9},{12,... | collective-permute-start | bytes 786440 | tf_op jit(solution)/shard_map/ppermute | solution.py:30
  68.9 9.2 %collective-permute-start.13 = (f32[512,128]{1,0:T(8,128)S(1)}, f32[512,128]{1,0:T(8,128)S(1)}, u32[]{:S(2)}, u32[]{:S(2)}) collective-permute-start(f32[512,128]{1,0:T(8,128)S(1)} %get-tuple-element.54), channel_id=1, source_target_pairs={{0,1},{1,0},{2,3},{3,2},{4,5},{5,4},{6,7},{7,6},{8,9},{9,8},{10,11... | collective-permute-start | bytes 786440 | tf_op jit(solution)/shard_map/ppermute | solution.py:438
  70.5 8.9 %collective-permute-start.12 = (f32[512,128]{1,0:T(8,128)S(1)}, f32[512,128]{1,0:T(8,128)S(1)}, u32[]{:S(2)}, u32[]{:S(2)}) collective-permute-start(f32[512,128]{1,0:T(8,128)S(1)} %get-tuple-element.51.vec), channel_id=1, source_target_pairs={{0,2},{1,3},{2,4},{3,5},{4,6},{5,7},{6,8},{7,9},{8,10},{9,11},{10,... | collective-permute-start | bytes 786440 | tf_op jit(solution)/shard_map/ppermute | solution.py:30
  78.1 11.2 %collective-permute-start.16 = (f32[512,128]{1,0:T(8,128)S(1)}, f32[512,128]{1,0:T(8,128)S(1)}, u32[]{:S(2)}, u32[]{:S(2)}) collective-permute-start(f32[512,128]{1,0:T(8,128)S(1)} %shard_map.93.after), channel_id=1, source_target_pairs={{2,0},{3,1},{4,2},{5,3},{6,4},{7,5},{8,6},{9,7},{10,8},{11,9},{12,... | collective-permute-start | bytes 786440 | tf_op jit(solution)/shard_map/ppermute | solution.py:30
  79.5 5.0 %collective-permute-start.14 = (f32[256,128]{1,0:T(8,128)S(1)}, f32[256,128]{1,0:T(8,128)S(1)}, u32[]{:S(2)}, u32[]{:S(2)}) collective-permute-start(f32[256,128]{1,0:T(8,128)S(1)} %get-tuple-element.55), channel_id=1, source_target_pairs={{0,1},{1,0},{2,3},{3,2},{4,5},{5,4},{6,7},{7,6},{8,9},{9,8},{10,11... | collective-permute-start | bytes 393224 | tf_op jit(solution)/shard_map/ppermute | solution.py:438
  81.1 6.0 %collective-permute-start.15 = (f32[256,128]{1,0:T(8,128)S(1)}, f32[256,128]{1,0:T(8,128)S(1)}, u32[]{:S(2)}, u32[]{:S(2)}) collective-permute-start(f32[256,128]{1,0:T(8,128)S(1)} %get-tuple-element.56.after), channel_id=1, source_target_pairs={{0,1},{1,0},{2,3},{3,2},{4,5},{5,4},{6,7},{7,6},{8,9},{9,8},{10,11... | collective-permute-start | bytes 393224 | tf_op jit(solution)/shard_map/ppermute | solution.py:438
  82.4 18.6 %copy-start.1 = (bf16[1280,1024]{1,0:T(8,128)(2,1)S(1)}, bf16[1280,1024]{1,0:T(8,128)(2,1)}, u32[]{:S(2)}) copy-start(bf16[1280,1024]{1,0:T(8,128)(2,1)} %genotypes.3) | copy-start | bytes 7864324
  82.4 18.6 %copy-start.3 = (f32[128]{0:T(128)S(1)}, f32[128]{0:T(128)}, u32[]{:S(2)}) copy-start(f32[128]{0:T(128)} %param.7) | copy-start | bytes 1540
  102.4 1.8 %collective-permute-start.17 = (f32[2,320,128]{2,1,0:T(8,128)}, f32[2,320,128]{2,1,0:T(8,128)S(1)}, u32[]{:S(2)}, u32[]{:S(2)}) collective-permute-start(f32[2,320,128]{2,1,0:T(8,128)} %get-tuple-element.59), channel_id=1, source_target_pairs={{0,8},{1,9},{2,10},{3,11},{4,12},{5,13},{6,14},{7,15},{8,0},{9,1},... | collective-permute-start | bytes 983048 | tf_op jit(solution)/shard_map/ppermute | solution.py:438
  104.9 4.6 %collective-permute-start.18 = (f32[2,2,40,128]{3,2,1,0:T(8,128)S(1)}, f32[2,2,40,128]{3,2,1,0:T(8,128)S(1)}, u32[]{:S(2)}, u32[]{:S(2)}) collective-permute-start(f32[2,2,40,128]{3,2,1,0:T(8,128)S(1)} %get-tuple-element.61), channel_id=1, source_target_pairs={{0,16},{1,17},{2,18},{3,19},{4,20},{5,21},{6,22},{7,23},{8,24},{9,... | collective-permute-start | bytes 245768 | tf_op jit(solution)/shard_map/ppermute | solution.py:438
  106.0 4.4 %collective-permute-start.19 = (f32[2,2,40,128]{3,2,1,0:T(8,128)S(1)}, f32[2,2,40,128]{3,2,1,0:T(8,128)S(1)}, u32[]{:S(2)}, u32[]{:S(2)}) collective-permute-start(f32[2,2,40,128]{3,2,1,0:T(8,128)S(1)} %get-tuple-element.63), channel_id=1, source_target_pairs={{0,1},{1,0},{2,3},{3,2},{4,5},{5,4},{6,7},{7,6},{8,9},{9,8},{10,11... | collective-permute-start | bytes 245768 | tf_op jit(solution)/shard_map/ppermute | solution.py:438
  111.0 4.1 %collective-permute-start.20 = (f32[2,40,128]{2,1,0:T(8,128)S(1)}, f32[2,40,128]{2,1,0:T(8,128)S(1)}, u32[]{:S(2)}, u32[]{:S(2)}) collective-permute-start(f32[2,40,128]{2,1,0:T(8,128)S(1)} %get-tuple-element.65), channel_id=1, source_target_pairs={{0,1},{1,0},{2,3},{3,2},{4,5},{5,4},{6,7},{7,6},{8,9},{9,8},{10,11... | collective-permute-start | bytes 122888 | tf_op jit(solution)/shard_map/ppermute | solution.py:438
  112.0 4.0 %collective-permute-start.21 = (f32[2,40,128]{2,1,0:T(8,128)S(1)}, f32[2,40,128]{2,1,0:T(8,128)S(1)}, u32[]{:S(2)}, u32[]{:S(2)}) collective-permute-start(f32[2,40,128]{2,1,0:T(8,128)S(1)} %get-tuple-element.67), channel_id=1, source_target_pairs={{0,16},{1,17},{2,18},{3,19},{4,20},{5,21},{6,22},{7,23},{8,24},{9,... | collective-permute-start | bytes 122888 | tf_op jit(solution)/shard_map/ppermute | solution.py:438
  116.5 4.5 %collective-permute-start.22 = (f32[40,128]{1,0:T(8,128)S(1)}, f32[40,128]{1,0:T(8,128)S(1)}, u32[]{:S(2)}, u32[]{:S(2)}) collective-permute-start(f32[40,128]{1,0:T(8,128)S(1)} %get-tuple-element.69), channel_id=1, source_target_pairs={{0,2},{1,3},{2,0},{3,1},{4,6},{5,7},{6,4},{7,5},{8,10},{9,11},{10,... | collective-permute-start | bytes 61448 | tf_op jit(solution)/shard_map/ppermute | solution.py:438
  117.1 4.7 %collective-permute-start.23 = (f32[40,128]{1,0:T(8,128)S(1)}, f32[40,128]{1,0:T(8,128)S(1)}, u32[]{:S(2)}, u32[]{:S(2)}) collective-permute-start(f32[40,128]{1,0:T(8,128)S(1)} %get-tuple-element.70), channel_id=1, source_target_pairs={{0,4},{1,5},{2,6},{3,7},{4,0},{5,1},{6,2},{7,3},{8,12},{9,13},{10,... | collective-permute-start | bytes 61448 | tf_op jit(solution)/shard_map/ppermute | solution.py:438
  118.3 5.6 %collective-permute-start.24 = (f32[40,128]{1,0:T(8,128)S(1)}, f32[40,128]{1,0:T(8,128)S(1)}, u32[]{:S(2)}, u32[]{:S(2)}) collective-permute-start(f32[40,128]{1,0:T(8,128)S(1)} %get-tuple-element.71), channel_id=1, source_target_pairs={{0,6},{1,7},{2,4},{3,5},{4,2},{5,3},{6,0},{7,1},{8,14},{9,15},{10,... | collective-permute-start | bytes 61448 | tf_op jit(solution)/shard_map/ppermute | solution.py:438

commit v2 on v0

--- a/solution.py
+++ b/solution.py
@@ -169,8 +169,14 @@
 
 def first_diag_kernel(vec, diag, after, narrow, product):
     tile = diag[...].astype(BF16)
+    rest = (diag[...] - tile.astype(F32)).astype(BF16)
     narrow[...] = tile
-    product[...] = jnp.dot(tile, vec[...].astype(BF16), preferred_element_type=F32)
+    value = vec[...]
+    high = value.astype(BF16)
+    low = (value - high.astype(F32)).astype(BF16)
+    both = jnp.dot(tile, jnp.concatenate([high, low], axis=1), preferred_element_type=F32)
+    k = value.shape[1]
+    product[...] = both[:, :k] + both[:, k:] + jnp.dot(rest, high, preferred_element_type=F32)
 
 
 def first_diag(vec, diag, after):
@@ -203,22 +209,23 @@
     )(vec, diag, after)
 
 
-def finish_kernel(odd, part, low, one, ahead_a, ahead_b, pair_a, pair_b, out, upper):
+def finish_kernel(odd, part, low, one, ahead_a, ahead_b, pair_a, pair_b, out, *upper):
     acc = jnp.dot(low[...], one[...].astype(BF16), preferred_element_type=F32) + part[...]
-    half = upper.shape[0]
+    half = ahead_a.shape[0]
     for place, (straight, pair) in enumerate(((ahead_a, pair_a), (ahead_b, pair_b))):
         rows = slice(place * half, (place + 1) * half)
         out[rows] = acc[rows] + straight[...] + jnp.where(odd[0] > 0, 0.0, pair[...])
-    upper[...] = out[:half]
-
-
-def finish(odd, part, low, *arrived):
+    for copy in upper:
+        copy[...] = out[:half]
+
+
+def finish(odd, uppers, part, low, *arrived):
     size, k = part.shape
     return pl.pallas_call(
         finish_kernel,
         in_specs=[SMEM] + [VMEM] * 7,
-        out_specs=[VMEM] * 2,
-        out_shape=[jax.ShapeDtypeStruct(part.shape, F32), jax.ShapeDtypeStruct((size // 2, k), F32)],
+        out_specs=[VMEM] * (1 + uppers),
+        out_shape=[jax.ShapeDtypeStruct(part.shape, F32)] + [jax.ShapeDtypeStruct((size // 2, k), F32)] * uppers,
         compiler_params=params(),
         cost_estimate=cost(2 * size * size * k, 2 * size * size),
     )(odd, part, low, *arrived)
@@ -320,19 +327,22 @@
     rounded[...] = narrow
     other = 1 - row[0] % 2
     for g in range(groups // 2):
-        send[g] = jnp.dot(group_rows(genotypes, groups, 2 * g + other), narrow, preferred_element_type=F32)
+        value = jnp.dot(group_rows(genotypes, groups, 2 * g + other), narrow, preferred_element_type=F32)
+        send[:, g] = value.reshape(send.shape[0], send.shape[2], send.shape[3])
 
 
 def keep_kernel(groups, row, rounded, genotypes, keep):
     mine = row[0] % 2
     for g in range(groups // 2):
-        keep[g] = jnp.dot(group_rows(genotypes, groups, 2 * g + mine), rounded[...], preferred_element_type=F32)
+        value = jnp.dot(group_rows(genotypes, groups, 2 * g + mine), rounded[...], preferred_element_type=F32)
+        keep[:, g] = value.reshape(keep.shape[0], keep.shape[2], keep.shape[3])
 
 
 def partial_scores(row, groups, pieces, penalty, v0, v1, v2, genotypes):
     people, size = genotypes.shape
     k = v0.shape[1]
-    half = jax.ShapeDtypeStruct((groups // 2, people // groups, k), F32)
+    cols = lax.axis_size("col")
+    half = jax.ShapeDtypeStruct((cols, groups // 2, people // groups // cols, k), F32)
     effects, rounded, send = pl.pallas_call(
         functools.partial(send_kernel, groups),
         in_specs=[SMEM] + [VMEM] * 6,
@@ -441,13 +451,13 @@
     )
     low_one, low_two = lows
     diag, own = first_diag(v0, ld_diag[0], last_sum)
-    v1, _ = finish(odd, add_two(own, low_two, two), low_one, *arrived)
+    [v1] = finish(odd, 0, add_two(own, low_two, two), low_one, *arrived)
 
     two = shifted(v1, 2)
     products = coupling(v1, low_one, low_two)
     last_sum, arrived = halos(v1, two, lambda: products[:2], lambda after: products[2:])
     own = diag_times(v1, diag, last_sum)
-    v2, upper = finish(odd, add_two(own, low_two, two), low_one, *arrived)
+    v2, upper = finish(odd, 1, add_two(own, low_two, two), low_one, *arrived)
 
     two = shifted(upper, 2)
     one, far = lower_coupling(v2, low_one, low_two)
@@ -462,16 +472,15 @@
 
     effects, send, keep = partial_scores(row.astype(jnp.int32)[None], rows, pieces, penalty[None], v0, v1, v2, genotypes)
     received = swapped(send, cols)
+    total = jnp.sum(lax.all_to_all(keep + received, "col", 0, 0, tiled=True), axis=0)
     bit = rows // 4
     while bit:
-        mine = (row // (2 * bit)) % 2
-        keep = keep.reshape((2, -1) + keep.shape[1:])
-        received = received.reshape((2, -1) + received.shape[1:])
-
-        keep, send = pick(mine.astype(jnp.int32)[None], keep, received)
-        received = swapped(send, 2 * bit * cols)
+        index = (row // (2 * bit)) % 2
+        total = total.reshape((2, -1) + total.shape[1:])
+        send = lax.dynamic_index_in_dim(total, 1 - index, 0, False)
+        total = lax.dynamic_index_in_dim(total, index, 0, False) + swapped(send, 2 * bit * cols)
         bit //= 2
-    return effects, scattered_over((keep + received)[0], "col")
+    return effects, total[0]
 
 
 def solution(mesh):

time: 122 us -> 123 us (level)
  blocking collectives: 21.6 us -> 10.9 us
  waiting for transfers between devices: 52 us -> 59.6 us
  starting transfers between devices: 28 us -> 31.4 us
    all_to_all x0 -> x1, waiting for transfers between devices: none -> 10.7 us  [body(): lax.all_to_all(keep + received, 'col', 0, 0, tiled=True)]
    all_to_all x1 -> x0, blocking collectives: 10.7 us -> none  [scattered_over(): return jnp.sum(lax.all_to_all(pieces, axis, 0, 0, tiled=True), axis=0)]
    all_to_all x0 -> x1, starting transfers between devices: none -> 3.43 us  [body(): lax.all_to_all(keep + received, 'col', 0, 0, tiled=True)]
    ppermute x11, waiting for transfers between devices: 28.9 us -> 26.3 us  [routed(): return lax.ppermute(block, AXES, pairs)]
  transfers between devices with their start and end apart: 19 -> 20, of which waited for: 15 -> 16; matrix products, arithmetic and copies ran while one was open for 0% -> 0% of each run, Pallas kernels for 11% -> 11%
where the time goes in v2:
time: 123 us
  waiting for transfers between devices  59.6 us (48%)
  starting transfers between devices  31.4 us (26%)
  Pallas kernels  17.8 us (14%)
  blocking collectives  10.9 us (9%)
  between operations  1.59 us (1%)
  other arithmetic  1.39 us (1%)
    ppermute x11, waiting for transfers between devices, routed(): return lax.ppermute(block, AXES, pairs)  26.3 us
    ppermute x8, waiting for transfers between devices, shifted(): return lax.ppermute(block, AXES, route)  22.6 us
    ppermute x8, starting transfers between devices, shifted(): return lax.ppermute(block, AXES, route)  16.7 us
    ppermute x11, starting transfers between devices, routed(): return lax.ppermute(block, AXES, pairs)  11.3 us
    all_to_all x1, blocking collectives, body(): lax.all_to_all(jnp.broadcast_to(moments[None], (n,) + moments.shape), AXE...  10.9 us
    all_to_all x1, waiting for transfers between devices, body(): lax.all_to_all(keep + received, 'col', 0, 0, tiled=True)  10.7 us
    pallas_call x2, Pallas kernels, from_tiles(): pl.pallas_call(kernel, in_specs=[SMEM] * 2 + [pl.BlockSpec(memory_space=p...  7.32 us
    all_to_all x1, starting transfers between devices, body(): lax.all_to_all(keep + received, 'col', 0, 0, tiled=True)  3.43 us
  transfers between devices with their start and end apart: 20, of which 16 were waited for; matrix products, arithmetic and copies ran while one was open for 0% of the time, Pallas kernels for 11%

profile of v2, /device:TPU:0, one launch (start us, length us, event | category | flops | bytes accessed | tf_op | source)
XLA Modules:
  0.0 122.8 jit_solution(7207755997386522695)
XLA Ops:
  0.6 5.0 %collective-permute-start.1 = (f32[1024,128]{1,0:T(8,128)}, f32[1024,128]{1,0:T(8,128)S(1)}, u32[]{:S(2)}, u32[]{:S(2)}) collective-permute-start(f32[1024,128]{1,0:T(8,128)} %v0.3), channel_id=1, source_target_pairs={{0,2},{1,3},{2,4},{3,5},{4,6},{5,7},{6,8},{7,9},{8,10},{9,11},{10,... | collective-permute-start | bytes 1572872 | tf_op jit(solution)/shard_map/ppermute | solution.py:30
  6.3 3.6 %shard_map.77 = (f32[512,128]{1,0:T(8,128)}, f32[512,128]{1,0:T(8,128)}) custom-call(s32[1]{0:T(128)S(6)} %copy.8.band, s32[1]{0:T(128)} %bitcast.2.position, f32[1024,128]{1,0:T(8,128)} %v0.3, f32[2,1024,1024]{2,1,0:T(8,128)} %bitcast.10), custom_call_target="tpu_custom_call" | custom-call | flops 268435456 | bytes 4194304 | tf_op jit(solution)/shard_map/pallas_call | solution.py:103
  9.9 1.6 %collective-permute-start.2 = (f32[512,128]{1,0:T(8,128)}, f32[512,128]{1,0:T(8,128)S(1)}, u32[]{:S(2)}, u32[]{:S(2)}) collective-permute-start(f32[512,128]{1,0:T(8,128)} %get-tuple-element.30), channel_id=1, source_target_pairs={{0,1},{1,0},{2,3},{3,2},{4,5},{5,4},{6,7},{7,6},{8,9},{9,8},{10,11... | collective-permute-start | bytes 786440 | tf_op jit(solution)/shard_map/ppermute | solution.py:389
  12.0 3.7 %shard_map.78 = (f32[512,128]{1,0:T(8,128)S(1)}, f32[512,128]{1,0:T(8,128)S(1)}, bf16[1024,1024]{1,0:T(8,128)(2,1)S(1)}, bf16[1024,1024]{1,0:T(8,128)(2,1)S(1)}) custom-call(s32[1]{0:T(128)S(6)} %copy.8.band, s32[1]{0:T(128)} %bitcast.2.position, f32[1024,128]{1,0:T(8,128)S(1)} %copy-done, f32[2,1024,1024]{2,1,0:T(8,128)} %bitcast.11), custom_call_target="tpu_custom_call" | custom-call | flops 268435456 | bytes 8388608 | tf_op jit(solution)/shard_map/pallas_call | solution.py:103
  15.7 3.7 %collective-permute-done.2.pair.pair_a = f32[512,128]{1,0:T(8,128)S(1)} collective-permute-done((f32[512,128]{1,0:T(8,128)}, f32[512,128]{1,0:T(8,128)S(1)}, u32[]{:S(2)}, u32[]{:S(2)}) %collective-permute-start.2) | collective-permute-done | bytes 262176 | tf_op jit(solution)/shard_map/ppermute | solution.py:389
  19.5 1.6 %collective-permute-start.3 = (f32[1024,128]{1,0:T(8,128)S(1)}, f32[1024,128]{1,0:T(8,128)S(1)}, u32[]{:S(2)}, u32[]{:S(2)}) collective-permute-start(f32[1024,128]{1,0:T(8,128)S(1)} %shard_map.80.after), channel_id=1, source_target_pairs={{0,1},{1,0},{2,3},{3,2},{4,5},{5,4},{6,7},{7,6},{8,9},{9,8},{10,11... | collective-permute-start | bytes 1572872 | tf_op jit(solution)/shard_map/ppermute | solution.py:389
  21.1 1.3 %collective-permute-start.4 = (f32[512,128]{1,0:T(8,128)S(1)}, f32[512,128]{1,0:T(8,128)S(1)}, u32[]{:S(2)}, u32[]{:S(2)}) collective-permute-start(f32[512,128]{1,0:T(8,128)S(1)} %shard_map.79.after), channel_id=1, source_target_pairs={{2,0},{3,1},{4,2},{5,3},{6,4},{7,5},{8,6},{9,7},{10,8},{11,9},{12,... | collective-permute-start | bytes 786440 | tf_op jit(solution)/shard_map/ppermute | solution.py:30
  22.4 2.0 %collective-permute-done.pair.pair_b = f32[512,128]{1,0:T(8,128)S(1)} collective-permute-done((f32[512,128]{1,0:T(8,128)}, f32[512,128]{1,0:T(8,128)S(1)}, u32[]{:S(2)}, u32[]{:S(2)}) %collective-permute-start) | collective-permute-done | bytes 262176 | tf_op jit(solution)/shard_map/ppermute | solution.py:389
  24.4 1.3 %collective-permute-start.5 = (f32[512,128]{1,0:T(8,128)S(1)}, f32[512,128]{1,0:T(8,128)S(1)}, u32[]{:S(2)}, u32[]{:S(2)}) collective-permute-start(f32[512,128]{1,0:T(8,128)S(1)} %shard_map.81.after), channel_id=1, source_target_pairs={{2,0},{3,1},{4,2},{5,3},{6,4},{7,5},{8,6},{9,7},{10,8},{11,9},{12,... | collective-permute-start | bytes 786440 | tf_op jit(solution)/shard_map/ppermute | solution.py:30
  25.7 1.9 %shard_map.82 = (bf16[1024,1024]{1,0:T(8,128)(2,1)S(1)}, f32[1024,128]{1,0:T(8,128)S(1)}) custom-call(f32[1024,128]{1,0:T(8,128)S(1)} %copy-done, f32[1024,1024]{1,0:T(8,128)S(1)} %bitcast.8, f32[512,128]{1,0:T(8,128)S(1)} %shard_map.81.after), custom_call_target="tpu_custom_call" | custom-call | flops 268435456 | bytes 6291456 | tf_op jit(solution)/shard_map/pallas_call | solution.py:185
  28.3 3.8 %collective-permute-done.4.ahead_a = f32[512,128]{1,0:T(8,128)S(1)} collective-permute-done((f32[512,128]{1,0:T(8,128)S(1)}, f32[512,128]{1,0:T(8,128)S(1)}, u32[]{:S(2)}, u32[]{:S(2)}) %collective-permute-start.4) | collective-permute-done | bytes 262176 | tf_op jit(solution)/shard_map/ppermute | solution.py:30
  32.1 4.8 %collective-permute-done.5.ahead_b = f32[512,128]{1,0:T(8,128)S(1)} collective-permute-done((f32[512,128]{1,0:T(8,128)S(1)}, f32[512,128]{1,0:T(8,128)S(1)}, u32[]{:S(2)}, u32[]{:S(2)}) %collective-permute-start.5) | collective-permute-done | bytes 262176 | tf_op jit(solution)/shard_map/ppermute | solution.py:30
  37.7 1.5 %collective-permute-start.7 = (f32[1024,128]{1,0:T(8,128)S(1)}, f32[1024,128]{1,0:T(8,128)S(1)}, u32[]{:S(2)}, u32[]{:S(2)}) collective-permute-start(f32[1024,128]{1,0:T(8,128)S(1)} %shard_map.84.vec.v1), channel_id=1, source_target_pairs={{0,2},{1,3},{2,4},{3,5},{4,6},{5,7},{6,8},{7,9},{8,10},{9,11},{10,... | collective-permute-start | bytes 1572872 | tf_op jit(solution)/shard_map/ppermute | solution.py:30
  40.1 1.4 %collective-permute-start.8 = (f32[512,128]{1,0:T(8,128)S(1)}, f32[512,128]{1,0:T(8,128)S(1)}, u32[]{:S(2)}, u32[]{:S(2)}) collective-permute-start(f32[512,128]{1,0:T(8,128)S(1)} %get-tuple-element.36), channel_id=1, source_target_pairs={{0,1},{1,0},{2,3},{3,2},{4,5},{5,4},{6,7},{7,6},{8,9},{9,8},{10,11... | collective-permute-start | bytes 786440 | tf_op jit(solution)/shard_map/ppermute | solution.py:389
  42.2 7.2 %collective-permute-done.8.pair.pair_a = f32[512,128]{1,0:T(8,128)S(1)} collective-permute-done((f32[512,128]{1,0:T(8,128)S(1)}, f32[512,128]{1,0:T(8,128)S(1)}, u32[]{:S(2)}, u32[]{:S(2)}) %collective-permute-start.8) | collective-permute-done | bytes 262176 | tf_op jit(solution)/shard_map/ppermute | solution.py:389
  51.2 1.3 %collective-permute-start.10 = (f32[512,128]{1,0:T(8,128)S(1)}, f32[512,128]{1,0:T(8,128)S(1)}, u32[]{:S(2)}, u32[]{:S(2)}) collective-permute-start(f32[512,128]{1,0:T(8,128)S(1)} %shard_map.86.after), channel_id=1, source_target_pairs={{2,0},{3,1},{4,2},{5,3},{6,4},{7,5},{8,6},{9,7},{10,8},{11,9},{12,... | collective-permute-start | bytes 786440 | tf_op jit(solution)/shard_map/ppermute | solution.py:30
  52.5 1.2 collective-permute-done.6.pair.pair_b
  53.7 1.3 %collective-permute-start.11 = (f32[512,128]{1,0:T(8,128)S(1)}, f32[512,128]{1,0:T(8,128)S(1)}, u32[]{:S(2)}, u32[]{:S(2)}) collective-permute-start(f32[512,128]{1,0:T(8,128)S(1)} %shard_map.88.after), channel_id=1, source_target_pairs={{2,0},{3,1},{4,2},{5,3},{6,4},{7,5},{8,6},{9,7},{10,8},{11,9},{12,... | collective-permute-start | bytes 786440 | tf_op jit(solution)/shard_map/ppermute | solution.py:30
  56.5 5.0 %collective-permute-done.10.ahead_a = f32[512,128]{1,0:T(8,128)S(1)} collective-permute-done((f32[512,128]{1,0:T(8,128)S(1)}, f32[512,128]{1,0:T(8,128)S(1)}, u32[]{:S(2)}, u32[]{:S(2)}) %collective-permute-start.10) | collective-permute-done | bytes 262176 | tf_op jit(solution)/shard_map/ppermute | solution.py:30
  61.5 5.6 %collective-permute-done.11.ahead_b = f32[512,128]{1,0:T(8,128)S(1)} collective-permute-done((f32[512,128]{1,0:T(8,128)S(1)}, f32[512,128]{1,0:T(8,128)S(1)}, u32[]{:S(2)}, u32[]{:S(2)}) %collective-permute-start.11) | collective-permute-done | bytes 262176 | tf_op jit(solution)/shard_map/ppermute | solution.py:30
  68.4 1.6 %collective-permute-start.13 = (f32[512,128]{1,0:T(8,128)S(1)}, f32[512,128]{1,0:T(8,128)S(1)}, u32[]{:S(2)}, u32[]{:S(2)}) collective-permute-start(f32[512,128]{1,0:T(8,128)S(1)} %get-tuple-element.40), channel_id=1, source_target_pairs={{0,1},{1,0},{2,3},{3,2},{4,5},{5,4},{6,7},{7,6},{8,9},{9,8},{10,11... | collective-permute-start | bytes 786440 | tf_op jit(solution)/shard_map/ppermute | solution.py:389
  70.0 3.8 %collective-permute-start.12 = (f32[512,128]{1,0:T(8,128)S(1)}, f32[512,128]{1,0:T(8,128)S(1)}, u32[]{:S(2)}, u32[]{:S(2)}) collective-permute-start(f32[512,128]{1,0:T(8,128)S(1)} %get-tuple-element.37.vec), channel_id=1, source_target_pairs={{0,2},{1,3},{2,4},{3,5},{4,6},{5,7},{6,8},{7,9},{8,10},{9,11},{10,... | collective-permute-start | bytes 786440 | tf_op jit(solution)/shard_map/ppermute | solution.py:30
  73.8 3.7 %collective-permute-done.13.pair = f32[512,128]{1,0:T(8,128)S(1)} collective-permute-done((f32[512,128]{1,0:T(8,128)S(1)}, f32[512,128]{1,0:T(8,128)S(1)}, u32[]{:S(2)}, u32[]{:S(2)}) %collective-permute-start.13) | collective-permute-done | bytes 262176 | tf_op jit(solution)/shard_map/ppermute | solution.py:389
  77.6 1.3 %collective-permute-start.16 = (f32[512,128]{1,0:T(8,128)S(1)}, f32[512,128]{1,0:T(8,128)S(1)}, u32[]{:S(2)}, u32[]{:S(2)}) collective-permute-start(f32[512,128]{1,0:T(8,128)S(1)} %shard_map.93.after), channel_id=1, source_target_pairs={{2,0},{3,1},{4,2},{5,3},{6,4},{7,5},{8,6},{9,7},{10,8},{11,9},{12,... | collective-permute-start | bytes 786440 | tf_op jit(solution)/shard_map/ppermute | solution.py:30
  79.0 1.6 %collective-permute-start.14 = (f32[256,128]{1,0:T(8,128)S(1)}, f32[256,128]{1,0:T(8,128)S(1)}, u32[]{:S(2)}, u32[]{:S(2)}) collective-permute-start(f32[256,128]{1,0:T(8,128)S(1)} %get-tuple-element.41), channel_id=1, source_target_pairs={{0,1},{1,0},{2,3},{3,2},{4,5},{5,4},{6,7},{7,6},{8,9},{9,8},{10,11... | collective-permute-start | bytes 393224 | tf_op jit(solution)/shard_map/ppermute | solution.py:389
  81.9 2.1 %collective-permute-done.14.one_a = f32[256,128]{1,0:T(8,128)S(1)} collective-permute-done((f32[256,128]{1,0:T(8,128)S(1)}, f32[256,128]{1,0:T(8,128)S(1)}, u32[]{:S(2)}, u32[]{:S(2)}) %collective-permute-start.14) | collective-permute-done | bytes 131104 | tf_op jit(solution)/shard_map/ppermute | solution.py:389
  84.0 2.7 %collective-permute-done.15.one_b = f32[256,128]{1,0:T(8,128)S(1)} collective-permute-done((f32[256,128]{1,0:T(8,128)S(1)}, f32[256,128]{1,0:T(8,128)S(1)}, u32[]{:S(2)}, u32[]{:S(2)}) %collective-permute-start.15) | collective-permute-done | bytes 131104 | tf_op jit(solution)/shard_map/ppermute | solution.py:389
  86.7 2.2 %collective-permute-done.16.up = f32[512,128]{1,0:T(8,128)S(1)} collective-permute-done((f32[512,128]{1,0:T(8,128)S(1)}, f32[512,128]{1,0:T(8,128)S(1)}, u32[]{:S(2)}, u32[]{:S(2)}) %collective-permute-start.16) | collective-permute-done | bytes 262176 | tf_op jit(solution)/shard_map/ppermute | solution.py:30
  89.6 10.9 %all_to_all.10.pieces = f32[32,8,128]{2,1,0:T(8,128)S(1)} all-to-all(f32[32,8,128]{2,1,0:T(8,128)S(1)} %broadcast_in_dim.21), channel_id=1, replica_groups=mesh['row'=4,'col'=8] {'row','col'}, dimensions={0} | all-to-all | bytes 262144 | tf_op jit(solution)/shard_map/all_to_all | solution.py:471
  104.1 3.4 %all-to-all-start.1 = ((f32[8,2,40,128]{3,2,1,0:T(8,128)}), f32[8,2,40,128]{3,2,1,0:T(8,128)S(1)}, u32[]{:S(2)}, u32[]{:S(2)}) async-start(f32[8,2,40,128]{3,2,1,0:T(8,128)} %add.27), calls=%async_computation.1 | async-start | bytes 655360 | tf_op jit(solution)/shard_map/all_to_all | solution.py:475
  107.6 10.7 %all-to-all-done.1 = f32[8,2,40,128]{3,2,1,0:T(8,128)S(1)} async-done(((f32[8,2,40,128]{3,2,1,0:T(8,128)}), f32[8,2,40,128]{3,2,1,0:T(8,128)S(1)}, u32[]{:S(2)}, u32[]{:S(2)}) %all-to-all-start.1) | async-done | bytes 327712 | tf_op jit(solution)/shard_map/all_to_all | solution.py:475
  119.5 2.7 %collective-permute-done.18 = f32[1,40,128]{2,1,0:T(8,128)S(1)} collective-permute-done((f32[1,40,128]{2,1,0:T(8,128)S(1)}, f32[1,40,128]{2,1,0:T(8,128)S(1)}, u32[]{:S(2)}, u32[]{:S(2)}) %collective-permute-start.18) | collective-permute-done | bytes 20512 | tf_op jit(solution)/shard_map/ppermute | solution.py:389
  (44 shorter events, 15.8 us)
Async XLA Ops:
  0.6 18.8 %collective-permute-start.1 = (f32[1024,128]{1,0:T(8,128)}, f32[1024,128]{1,0:T(8,128)S(1)}, u32[]{:S(2)}, u32[]{:S(2)}) collective-permute-start(f32[1024,128]{1,0:T(8,128)} %v0.3), channel_id=1, source_target_pairs={{0,2},{1,3},{2,4},{3,5},{4,6},{5,7},{6,8},{7,9},{8,10},{9,11},{10,... | collective-permute-start | bytes 1572872 | tf_op jit(solution)/shard_map/ppermute | solution.py:30
  6.3 5.7 %copy-start = (f32[1024,128]{1,0:T(8,128)S(1)}, f32[1024,128]{1,0:T(8,128)}, u32[]{:S(2)}) copy-start(f32[1024,128]{1,0:T(8,128)} %v0.3) | copy-start | bytes 1572868
  9.9 9.5 %collective-permute-start.2 = (f32[512,128]{1,0:T(8,128)}, f32[512,128]{1,0:T(8,128)S(1)}, u32[]{:S(2)}, u32[]{:S(2)}) collective-permute-start(f32[512,128]{1,0:T(8,128)} %get-tuple-element.30), channel_id=1, source_target_pairs={{0,1},{1,0},{2,3},{3,2},{4,5},{5,4},{6,7},{7,6},{8,9},{9,8},{10,11... | collective-permute-start | bytes 786440 | tf_op jit(solution)/shard_map/ppermute | solution.py:389
  11.4 12.9 %collective-permute-start = (f32[512,128]{1,0:T(8,128)}, f32[512,128]{1,0:T(8,128)S(1)}, u32[]{:S(2)}, u32[]{:S(2)}) collective-permute-start(f32[512,128]{1,0:T(8,128)} %get-tuple-element.24), channel_id=1, source_target_pairs={{0,1},{1,0},{2,3},{3,2},{4,5},{5,4},{6,7},{7,6},{8,9},{9,8},{10,11... | collective-permute-start | bytes 786440 | tf_op jit(solution)/shard_map/ppermute | solution.py:389
  15.7 10.0 %copy-start.2 = (f32[1,1024,1024]{2,1,0:T(8,128)S(1)}, f32[1,1024,1024]{2,1,0:T(8,128)}, u32[]{:S(2)}) copy-start(f32[1,1024,1024]{2,1,0:T(8,128)} %param.8) | copy-start | bytes 12582916
  19.5 17.4 %collective-permute-start.3 = (f32[1024,128]{1,0:T(8,128)S(1)}, f32[1024,128]{1,0:T(8,128)S(1)}, u32[]{:S(2)}, u32[]{:S(2)}) collective-permute-start(f32[1024,128]{1,0:T(8,128)S(1)} %shard_map.80.after), channel_id=1, source_target_pairs={{0,1},{1,0},{2,3},{3,2},{4,5},{5,4},{6,7},{7,6},{8,9},{9,8},{10,11... | collective-permute-start | bytes 1572872 | tf_op jit(solution)/shard_map/ppermute | solution.py:389
  21.1 11.0 %collective-permute-start.4 = (f32[512,128]{1,0:T(8,128)S(1)}, f32[512,128]{1,0:T(8,128)S(1)}, u32[]{:S(2)}, u32[]{:S(2)}) collective-permute-start(f32[512,128]{1,0:T(8,128)S(1)} %shard_map.79.after), channel_id=1, source_target_pairs={{2,0},{3,1},{4,2},{5,3},{6,4},{7,5},{8,6},{9,7},{10,8},{11,9},{12,... | collective-permute-start | bytes 786440 | tf_op jit(solution)/shard_map/ppermute | solution.py:30
  24.4 12.6 %collective-permute-start.5 = (f32[512,128]{1,0:T(8,128)S(1)}, f32[512,128]{1,0:T(8,128)S(1)}, u32[]{:S(2)}, u32[]{:S(2)}) collective-permute-start(f32[512,128]{1,0:T(8,128)S(1)} %shard_map.81.after), channel_id=1, source_target_pairs={{2,0},{3,1},{4,2},{5,3},{6,4},{7,5},{8,6},{9,7},{10,8},{11,9},{12,... | collective-permute-start | bytes 786440 | tf_op jit(solution)/shard_map/ppermute | solution.py:30
  37.7 12.8 %collective-permute-start.7 = (f32[1024,128]{1,0:T(8,128)S(1)}, f32[1024,128]{1,0:T(8,128)S(1)}, u32[]{:S(2)}, u32[]{:S(2)}) collective-permute-start(f32[1024,128]{1,0:T(8,128)S(1)} %shard_map.84.vec.v1), channel_id=1, source_target_pairs={{0,2},{1,3},{2,4},{3,5},{4,6},{5,7},{6,8},{7,9},{8,10},{9,11},{10,... | collective-permute-start | bytes 1572872 | tf_op jit(solution)/shard_map/ppermute | solution.py:30
  40.1 9.3 %collective-permute-start.8 = (f32[512,128]{1,0:T(8,128)S(1)}, f32[512,128]{1,0:T(8,128)S(1)}, u32[]{:S(2)}, u32[]{:S(2)}) collective-permute-start(f32[512,128]{1,0:T(8,128)S(1)} %get-tuple-element.36), channel_id=1, source_target_pairs={{0,1},{1,0},{2,3},{3,2},{4,5},{5,4},{6,7},{7,6},{8,9},{9,8},{10,11... | collective-permute-start | bytes 786440 | tf_op jit(solution)/shard_map/ppermute | solution.py:389
  41.4 12.3 %collective-permute-start.6 = (f32[512,128]{1,0:T(8,128)S(1)}, f32[512,128]{1,0:T(8,128)S(1)}, u32[]{:S(2)}, u32[]{:S(2)}) collective-permute-start(f32[512,128]{1,0:T(8,128)S(1)} %get-tuple-element.34), channel_id=1, source_target_pairs={{0,1},{1,0},{2,3},{3,2},{4,5},{5,4},{6,7},{7,6},{8,9},{9,8},{10,11... | collective-permute-start | bytes 786440 | tf_op jit(solution)/shard_map/ppermute | solution.py:389
  50.6 16.5 %collective-permute-start.9 = (f32[1024,128]{1,0:T(8,128)S(1)}, f32[1024,128]{1,0:T(8,128)S(1)}, u32[]{:S(2)}, u32[]{:S(2)}) collective-permute-start(f32[1024,128]{1,0:T(8,128)S(1)} %shard_map.87.after), channel_id=1, source_target_pairs={{0,1},{1,0},{2,3},{3,2},{4,5},{5,4},{6,7},{7,6},{8,9},{9,8},{10,11... | collective-permute-start | bytes 1572872 | tf_op jit(solution)/shard_map/ppermute | solution.py:389
  51.2 10.3 %collective-permute-start.10 = (f32[512,128]{1,0:T(8,128)S(1)}, f32[512,128]{1,0:T(8,128)S(1)}, u32[]{:S(2)}, u32[]{:S(2)}) collective-permute-start(f32[512,128]{1,0:T(8,128)S(1)} %shard_map.86.after), channel_id=1, source_target_pairs={{2,0},{3,1},{4,2},{5,3},{6,4},{7,5},{8,6},{9,7},{10,8},{11,9},{12,... | collective-permute-start | bytes 786440 | tf_op jit(solution)/shard_map/ppermute | solution.py:30
  53.7 13.4 %collective-permute-start.11 = (f32[512,128]{1,0:T(8,128)S(1)}, f32[512,128]{1,0:T(8,128)S(1)}, u32[]{:S(2)}, u32[]{:S(2)}) collective-permute-start(f32[512,128]{1,0:T(8,128)S(1)} %shard_map.88.after), channel_id=1, source_target_pairs={{2,0},{3,1},{4,2},{5,3},{6,4},{7,5},{8,6},{9,7},{10,8},{11,9},{12,... | collective-permute-start | bytes 786440 | tf_op jit(solution)/shard_map/ppermute | solution.py:30
  68.4 9.2 %collective-permute-start.13 = (f32[512,128]{1,0:T(8,128)S(1)}, f32[512,128]{1,0:T(8,128)S(1)}, u32[]{:S(2)}, u32[]{:S(2)}) collective-permute-start(f32[512,128]{1,0:T(8,128)S(1)} %get-tuple-element.40), channel_id=1, source_target_pairs={{0,1},{1,0},{2,3},{3,2},{4,5},{5,4},{6,7},{7,6},{8,9},{9,8},{10,11... | collective-permute-start | bytes 786440 | tf_op jit(solution)/shard_map/ppermute | solution.py:389
  70.0 8.9 %collective-permute-start.12 = (f32[512,128]{1,0:T(8,128)S(1)}, f32[512,128]{1,0:T(8,128)S(1)}, u32[]{:S(2)}, u32[]{:S(2)}) collective-permute-start(f32[512,128]{1,0:T(8,128)S(1)} %get-tuple-element.37.vec), channel_id=1, source_target_pairs={{0,2},{1,3},{2,4},{3,5},{4,6},{5,7},{6,8},{7,9},{8,10},{9,11},{10,... | collective-permute-start | bytes 786440 | tf_op jit(solution)/shard_map/ppermute | solution.py:30
  77.6 11.2 %collective-permute-start.16 = (f32[512,128]{1,0:T(8,128)S(1)}, f32[512,128]{1,0:T(8,128)S(1)}, u32[]{:S(2)}, u32[]{:S(2)}) collective-permute-start(f32[512,128]{1,0:T(8,128)S(1)} %shard_map.93.after), channel_id=1, source_target_pairs={{2,0},{3,1},{4,2},{5,3},{6,4},{7,5},{8,6},{9,7},{10,8},{11,9},{12,... | collective-permute-start | bytes 786440 | tf_op jit(solution)/shard_map/ppermute | solution.py:30
  79.0 5.0 %collective-permute-start.14 = (f32[256,128]{1,0:T(8,128)S(1)}, f32[256,128]{1,0:T(8,128)S(1)}, u32[]{:S(2)}, u32[]{:S(2)}) collective-permute-start(f32[256,128]{1,0:T(8,128)S(1)} %get-tuple-element.41), channel_id=1, source_target_pairs={{0,1},{1,0},{2,3},{3,2},{4,5},{5,4},{6,7},{7,6},{8,9},{9,8},{10,11... | collective-permute-start | bytes 393224 | tf_op jit(solution)/shard_map/ppermute | solution.py:389
  80.6 6.1 %collective-permute-start.15 = (f32[256,128]{1,0:T(8,128)S(1)}, f32[256,128]{1,0:T(8,128)S(1)}, u32[]{:S(2)}, u32[]{:S(2)}) collective-permute-start(f32[256,128]{1,0:T(8,128)S(1)} %get-tuple-element.42.after), channel_id=1, source_target_pairs={{0,1},{1,0},{2,3},{3,2},{4,5},{5,4},{6,7},{7,6},{8,9},{9,8},{10,11... | collective-permute-start | bytes 393224 | tf_op jit(solution)/shard_map/ppermute | solution.py:389
  81.9 18.6 %copy-start.1 = (bf16[1280,1024]{1,0:T(8,128)(2,1)S(1)}, bf16[1280,1024]{1,0:T(8,128)(2,1)}, u32[]{:S(2)}) copy-start(bf16[1280,1024]{1,0:T(8,128)(2,1)} %genotypes.3) | copy-start | bytes 7864324
  81.9 18.6 %copy-start.3 = (f32[128]{0:T(128)S(1)}, f32[128]{0:T(128)}, u32[]{:S(2)}) copy-start(f32[128]{0:T(128)} %param.7) | copy-start | bytes 1540
  101.7 1.6 %collective-permute-start.17 = (f32[8,2,40,128]{3,2,1,0:T(8,128)S(1)}, f32[8,2,40,128]{3,2,1,0:T(8,128)S(1)}, u32[]{:S(2)}, u32[]{:S(2)}) collective-permute-start(f32[8,2,40,128]{3,2,1,0:T(8,128)S(1)} %get-tuple-element.45), channel_id=1, source_target_pairs={{0,8},{1,9},{2,10},{3,11},{4,12},{5,13},{6,14},{7,15},{8,0},{9,1},... | collective-permute-start | bytes 983048 | tf_op jit(solution)/shard_map/ppermute | solution.py:389
  104.1 14.2 %all-to-all-start.1 = ((f32[8,2,40,128]{3,2,1,0:T(8,128)}), f32[8,2,40,128]{3,2,1,0:T(8,128)S(1)}, u32[]{:S(2)}, u32[]{:S(2)}) async-start(f32[8,2,40,128]{3,2,1,0:T(8,128)} %add.27), calls=%async_computation.1 | async-start | bytes 655360 | tf_op jit(solution)/shard_map/all_to_all | solution.py:475
  118.3 3.8 %collective-permute-start.18 = (f32[1,40,128]{2,1,0:T(8,128)S(1)}, f32[1,40,128]{2,1,0:T(8,128)S(1)}, u32[]{:S(2)}, u32[]{:S(2)}) collective-permute-start(f32[1,40,128]{2,1,0:T(8,128)S(1)} %constant_dynamic-slice_fusion), channel_id=1, source_target_pairs={{0,16},{1,17},{2,18},{3,19},{4,20},{5,21},{6,22},{7,23},{8,24},{9,... | collective-permute-start | bytes 61448 | tf_op jit(solution)/shard_map/ppermute | solution.py:389

commit v3 on v2

--- a/solution.py
+++ b/solution.py
@@ -327,22 +327,19 @@
     rounded[...] = narrow
     other = 1 - row[0] % 2
     for g in range(groups // 2):
-        value = jnp.dot(group_rows(genotypes, groups, 2 * g + other), narrow, preferred_element_type=F32)
-        send[:, g] = value.reshape(send.shape[0], send.shape[2], send.shape[3])
+        send[g] = jnp.dot(group_rows(genotypes, groups, 2 * g + other), narrow, preferred_element_type=F32)
 
 
 def keep_kernel(groups, row, rounded, genotypes, keep):
     mine = row[0] % 2
     for g in range(groups // 2):
-        value = jnp.dot(group_rows(genotypes, groups, 2 * g + mine), rounded[...], preferred_element_type=F32)
-        keep[:, g] = value.reshape(keep.shape[0], keep.shape[2], keep.shape[3])
+        keep[g] = jnp.dot(group_rows(genotypes, groups, 2 * g + mine), rounded[...], preferred_element_type=F32)
 
 
 def partial_scores(row, groups, pieces, penalty, v0, v1, v2, genotypes):
     people, size = genotypes.shape
     k = v0.shape[1]
-    cols = lax.axis_size("col")
-    half = jax.ShapeDtypeStruct((cols, groups // 2, people // groups // cols, k), F32)
+    half = jax.ShapeDtypeStruct((groups // 2, people // groups, k), F32)
     effects, rounded, send = pl.pallas_call(
         functools.partial(send_kernel, groups),
         in_specs=[SMEM] + [VMEM] * 6,
@@ -472,15 +469,16 @@
 
     effects, send, keep = partial_scores(row.astype(jnp.int32)[None], rows, pieces, penalty[None], v0, v1, v2, genotypes)
     received = swapped(send, cols)
-    total = jnp.sum(lax.all_to_all(keep + received, "col", 0, 0, tiled=True), axis=0)
     bit = rows // 4
     while bit:
-        index = (row // (2 * bit)) % 2
-        total = total.reshape((2, -1) + total.shape[1:])
-        send = lax.dynamic_index_in_dim(total, 1 - index, 0, False)
-        total = lax.dynamic_index_in_dim(total, index, 0, False) + swapped(send, 2 * bit * cols)
+        mine = (row // (2 * bit)) % 2
+        keep = keep.reshape((2, -1) + keep.shape[1:])
+        received = received.reshape((2, -1) + received.shape[1:])
+
+        keep, send = pick(mine.astype(jnp.int32)[None], keep, received)
+        received = swapped(send, 2 * bit * cols)
         bit //= 2
-    return effects, total[0]
+    return effects, scattered_over((keep + received)[0], "col")
 
 
 def solution(mesh):

time: 123 us -> 122 us (level)
  blocking collectives: 10.9 us -> 21.6 us
  waiting for transfers between devices: 59.6 us -> 51.5 us
  starting transfers between devices: 31.4 us -> 28 us
    all_to_all x1 -> x0, waiting for transfers between devices: 10.7 us -> none  [body(): lax.all_to_all(keep + received, 'col', 0, 0, tiled=True)]
    all_to_all x0 -> x1, blocking collectives: none -> 10.7 us  [scattered_over(): return jnp.sum(lax.all_to_all(pieces, axis, 0, 0, tiled=True), axis=0)]
    all_to_all x1 -> x0, starting transfers between devices: 3.43 us -> none  [body(): lax.all_to_all(keep + received, 'col', 0, 0, tiled=True)]
    ppermute x11, waiting for transfers between devices: 26.3 us -> 28.9 us  [routed(): return lax.ppermute(block, AXES, pairs)]
  transfers between devices with their start and end apart: 20 -> 19, of which waited for: 16 -> 15; matrix products, arithmetic and copies ran while one was open for 0% -> 0% of each run, Pallas kernels for 11% -> 11%
where the time goes in v3:
time: 122 us; the launch traced here: 121 us
  waiting for transfers between devices  51.5 us (42%)
  starting transfers between devices  28 us (23%)
  blocking collectives  21.6 us (18%)
  Pallas kernels  18 us (15%)
  between operations  1.55 us (1%)
    ppermute x11, waiting for transfers between devices, routed(): return lax.ppermute(block, AXES, pairs)  28.9 us
    ppermute x8, waiting for transfers between devices, shifted(): return lax.ppermute(block, AXES, route)  22.6 us
    ppermute x8, starting transfers between devices, shifted(): return lax.ppermute(block, AXES, route)  16.7 us
    ppermute x11, starting transfers between devices, routed(): return lax.ppermute(block, AXES, pairs)  11.3 us
    all_to_all x1, blocking collectives, body(): lax.all_to_all(jnp.broadcast_to(moments[None], (n,) + moments.shape), AXE...  10.9 us
    all_to_all x1, blocking collectives, scattered_over(): return jnp.sum(lax.all_to_all(pieces, axis, 0, 0, tiled=True), axis=0)  10.7 us
    pallas_call x2, Pallas kernels, from_tiles(): pl.pallas_call(kernel, in_specs=[SMEM] * 2 + [pl.BlockSpec(memory_space=p...  7.32 us
  transfers between devices with their start and end apart: 19, of which 15 were waited for; matrix products, arithmetic and copies ran while one was open for 0% of the time, Pallas kernels for 11%

profile of v3, /device:TPU:0, one launch (start us, length us, event | category | flops | bytes accessed | tf_op | source)
XLA Modules:
  0.0 121.4 jit_solution(10659751683404298222)
XLA Ops:
  0.6 5.0 %collective-permute-start.1 = (f32[1024,128]{1,0:T(8,128)}, f32[1024,128]{1,0:T(8,128)S(1)}, u32[]{:S(2)}, u32[]{:S(2)}) collective-permute-start(f32[1024,128]{1,0:T(8,128)} %v0.3), channel_id=1, source_target_pairs={{0,2},{1,3},{2,4},{3,5},{4,6},{5,7},{6,8},{7,9},{8,10},{9,11},{10,... | collective-permute-start | bytes 1572872 | tf_op jit(solution)/shard_map/ppermute | solution.py:30
  6.3 3.6 %shard_map.77 = (f32[512,128]{1,0:T(8,128)}, f32[512,128]{1,0:T(8,128)}) custom-call(s32[1]{0:T(128)S(6)} %copy.8.band, s32[1]{0:T(128)} %bitcast.2.position, f32[1024,128]{1,0:T(8,128)} %v0.3, f32[2,1024,1024]{2,1,0:T(8,128)} %bitcast.14), custom_call_target="tpu_custom_call" | custom-call | flops 268435456 | bytes 4194304 | tf_op jit(solution)/shard_map/pallas_call | solution.py:103
  9.9 1.6 %collective-permute-start.2 = (f32[512,128]{1,0:T(8,128)}, f32[512,128]{1,0:T(8,128)S(1)}, u32[]{:S(2)}, u32[]{:S(2)}) collective-permute-start(f32[512,128]{1,0:T(8,128)} %get-tuple-element.32), channel_id=1, source_target_pairs={{0,1},{1,0},{2,3},{3,2},{4,5},{5,4},{6,7},{7,6},{8,9},{9,8},{10,11... | collective-permute-start | bytes 786440 | tf_op jit(solution)/shard_map/ppermute | solution.py:386
  12.0 3.7 %shard_map.78 = (f32[512,128]{1,0:T(8,128)S(1)}, f32[512,128]{1,0:T(8,128)S(1)}, bf16[1024,1024]{1,0:T(8,128)(2,1)S(1)}, bf16[1024,1024]{1,0:T(8,128)(2,1)S(1)}) custom-call(s32[1]{0:T(128)S(6)} %copy.8.band, s32[1]{0:T(128)} %bitcast.2.position, f32[1024,128]{1,0:T(8,128)S(1)} %copy-done, f32[2,1024,1024]{2,1,0:T(8,128)} %bitcast.15), custom_call_target="tpu_custom_call" | custom-call | flops 268435456 | bytes 8388608 | tf_op jit(solution)/shard_map/pallas_call | solution.py:103
  15.7 3.7 %collective-permute-done.2.pair.pair_a = f32[512,128]{1,0:T(8,128)S(1)} collective-permute-done((f32[512,128]{1,0:T(8,128)}, f32[512,128]{1,0:T(8,128)S(1)}, u32[]{:S(2)}, u32[]{:S(2)}) %collective-permute-start.2) | collective-permute-done | bytes 262176 | tf_op jit(solution)/shard_map/ppermute | solution.py:386
  19.5 1.6 %collective-permute-start.3 = (f32[1024,128]{1,0:T(8,128)S(1)}, f32[1024,128]{1,0:T(8,128)S(1)}, u32[]{:S(2)}, u32[]{:S(2)}) collective-permute-start(f32[1024,128]{1,0:T(8,128)S(1)} %shard_map.80.after), channel_id=1, source_target_pairs={{0,1},{1,0},{2,3},{3,2},{4,5},{5,4},{6,7},{7,6},{8,9},{9,8},{10,11... | collective-permute-start | bytes 1572872 | tf_op jit(solution)/shard_map/ppermute | solution.py:386
  21.1 1.3 %collective-permute-start.4 = (f32[512,128]{1,0:T(8,128)S(1)}, f32[512,128]{1,0:T(8,128)S(1)}, u32[]{:S(2)}, u32[]{:S(2)}) collective-permute-start(f32[512,128]{1,0:T(8,128)S(1)} %shard_map.79.after), channel_id=1, source_target_pairs={{2,0},{3,1},{4,2},{5,3},{6,4},{7,5},{8,6},{9,7},{10,8},{11,9},{12,... | collective-permute-start | bytes 786440 | tf_op jit(solution)/shard_map/ppermute | solution.py:30
  22.3 2.0 %collective-permute-done.pair.pair_b = f32[512,128]{1,0:T(8,128)S(1)} collective-permute-done((f32[512,128]{1,0:T(8,128)}, f32[512,128]{1,0:T(8,128)S(1)}, u32[]{:S(2)}, u32[]{:S(2)}) %collective-permute-start) | collective-permute-done | bytes 262176 | tf_op jit(solution)/shard_map/ppermute | solution.py:386
  24.3 1.3 %collective-permute-start.5 = (f32[512,128]{1,0:T(8,128)S(1)}, f32[512,128]{1,0:T(8,128)S(1)}, u32[]{:S(2)}, u32[]{:S(2)}) collective-permute-start(f32[512,128]{1,0:T(8,128)S(1)} %shard_map.81.after), channel_id=1, source_target_pairs={{2,0},{3,1},{4,2},{5,3},{6,4},{7,5},{8,6},{9,7},{10,8},{11,9},{12,... | collective-permute-start | bytes 786440 | tf_op jit(solution)/shard_map/ppermute | solution.py:30
  25.7 1.9 %shard_map.82 = (bf16[1024,1024]{1,0:T(8,128)(2,1)S(1)}, f32[1024,128]{1,0:T(8,128)S(1)}) custom-call(f32[1024,128]{1,0:T(8,128)S(1)} %copy-done, f32[1024,1024]{1,0:T(8,128)S(1)} %bitcast.10, f32[512,128]{1,0:T(8,128)S(1)} %shard_map.81.after), custom_call_target="tpu_custom_call" | custom-call | flops 268435456 | bytes 6291456 | tf_op jit(solution)/shard_map/pallas_call | solution.py:185
  28.3 3.8 %collective-permute-done.4.ahead_a = f32[512,128]{1,0:T(8,128)S(1)} collective-permute-done((f32[512,128]{1,0:T(8,128)S(1)}, f32[512,128]{1,0:T(8,128)S(1)}, u32[]{:S(2)}, u32[]{:S(2)}) %collective-permute-start.4) | collective-permute-done | bytes 262176 | tf_op jit(solution)/shard_map/ppermute | solution.py:30
  32.1 4.8 %collective-permute-done.5.ahead_b = f32[512,128]{1,0:T(8,128)S(1)} collective-permute-done((f32[512,128]{1,0:T(8,128)S(1)}, f32[512,128]{1,0:T(8,128)S(1)}, u32[]{:S(2)}, u32[]{:S(2)}) %collective-permute-start.5) | collective-permute-done | bytes 262176 | tf_op jit(solution)/shard_map/ppermute | solution.py:30
  37.6 1.5 %collective-permute-start.7 = (f32[1024,128]{1,0:T(8,128)S(1)}, f32[1024,128]{1,0:T(8,128)S(1)}, u32[]{:S(2)}, u32[]{:S(2)}) collective-permute-start(f32[1024,128]{1,0:T(8,128)S(1)} %shard_map.84.vec.v1), channel_id=1, source_target_pairs={{0,2},{1,3},{2,4},{3,5},{4,6},{5,7},{6,8},{7,9},{8,10},{9,11},{10,... | collective-permute-start | bytes 1572872 | tf_op jit(solution)/shard_map/ppermute | solution.py:30
  40.0 1.4 %collective-permute-start.8 = (f32[512,128]{1,0:T(8,128)S(1)}, f32[512,128]{1,0:T(8,128)S(1)}, u32[]{:S(2)}, u32[]{:S(2)}) collective-permute-start(f32[512,128]{1,0:T(8,128)S(1)} %get-tuple-element.38), channel_id=1, source_target_pairs={{0,1},{1,0},{2,3},{3,2},{4,5},{5,4},{6,7},{7,6},{8,9},{9,8},{10,11... | collective-permute-start | bytes 786440 | tf_op jit(solution)/shard_map/ppermute | solution.py:386
  42.1 7.2 %collective-permute-done.8.pair.pair_a = f32[512,128]{1,0:T(8,128)S(1)} collective-permute-done((f32[512,128]{1,0:T(8,128)S(1)}, f32[512,128]{1,0:T(8,128)S(1)}, u32[]{:S(2)}, u32[]{:S(2)}) %collective-permute-start.8) | collective-permute-done | bytes 262176 | tf_op jit(solution)/shard_map/ppermute | solution.py:386
  51.2 1.3 %collective-permute-start.10 = (f32[512,128]{1,0:T(8,128)S(1)}, f32[512,128]{1,0:T(8,128)S(1)}, u32[]{:S(2)}, u32[]{:S(2)}) collective-permute-start(f32[512,128]{1,0:T(8,128)S(1)} %shard_map.86.after), channel_id=1, source_target_pairs={{2,0},{3,1},{4,2},{5,3},{6,4},{7,5},{8,6},{9,7},{10,8},{11,9},{12,... | collective-permute-start | bytes 786440 | tf_op jit(solution)/shard_map/ppermute | solution.py:30
  53.7 1.3 %collective-permute-start.11 = (f32[512,128]{1,0:T(8,128)S(1)}, f32[512,128]{1,0:T(8,128)S(1)}, u32[]{:S(2)}, u32[]{:S(2)}) collective-permute-start(f32[512,128]{1,0:T(8,128)S(1)} %shard_map.88.after), channel_id=1, source_target_pairs={{2,0},{3,1},{4,2},{5,3},{6,4},{7,5},{8,6},{9,7},{10,8},{11,9},{12,... | collective-permute-start | bytes 786440 | tf_op jit(solution)/shard_map/ppermute | solution.py:30
  56.5 5.0 %collective-permute-done.10.ahead_a = f32[512,128]{1,0:T(8,128)S(1)} collective-permute-done((f32[512,128]{1,0:T(8,128)S(1)}, f32[512,128]{1,0:T(8,128)S(1)}, u32[]{:S(2)}, u32[]{:S(2)}) %collective-permute-start.10) | collective-permute-done | bytes 262176 | tf_op jit(solution)/shard_map/ppermute | solution.py:30
  61.5 5.6 %collective-permute-done.11.ahead_b = f32[512,128]{1,0:T(8,128)S(1)} collective-permute-done((f32[512,128]{1,0:T(8,128)S(1)}, f32[512,128]{1,0:T(8,128)S(1)}, u32[]{:S(2)}, u32[]{:S(2)}) %collective-permute-start.11) | collective-permute-done | bytes 262176 | tf_op jit(solution)/shard_map/ppermute | solution.py:30
  68.4 1.6 %collective-permute-start.13 = (f32[512,128]{1,0:T(8,128)S(1)}, f32[512,128]{1,0:T(8,128)S(1)}, u32[]{:S(2)}, u32[]{:S(2)}) collective-permute-start(f32[512,128]{1,0:T(8,128)S(1)} %get-tuple-element.42), channel_id=1, source_target_pairs={{0,1},{1,0},{2,3},{3,2},{4,5},{5,4},{6,7},{7,6},{8,9},{9,8},{10,11... | collective-permute-start | bytes 786440 | tf_op jit(solution)/shard_map/ppermute | solution.py:386
  70.0 3.8 %collective-permute-start.12 = (f32[512,128]{1,0:T(8,128)S(1)}, f32[512,128]{1,0:T(8,128)S(1)}, u32[]{:S(2)}, u32[]{:S(2)}) collective-permute-start(f32[512,128]{1,0:T(8,128)S(1)} %get-tuple-element.39.vec), channel_id=1, source_target_pairs={{0,2},{1,3},{2,4},{3,5},{4,6},{5,7},{6,8},{7,9},{8,10},{9,11},{10,... | collective-permute-start | bytes 786440 | tf_op jit(solution)/shard_map/ppermute | solution.py:30
  73.8 3.7 %collective-permute-done.13.pair = f32[512,128]{1,0:T(8,128)S(1)} collective-permute-done((f32[512,128]{1,0:T(8,128)S(1)}, f32[512,128]{1,0:T(8,128)S(1)}, u32[]{:S(2)}, u32[]{:S(2)}) %collective-permute-start.13) | collective-permute-done | bytes 262176 | tf_op jit(solution)/shard_map/ppermute | solution.py:386
  77.6 1.3 %collective-permute-start.16 = (f32[512,128]{1,0:T(8,128)S(1)}, f32[512,128]{1,0:T(8,128)S(1)}, u32[]{:S(2)}, u32[]{:S(2)}) collective-permute-start(f32[512,128]{1,0:T(8,128)S(1)} %shard_map.93.after), channel_id=1, source_target_pairs={{2,0},{3,1},{4,2},{5,3},{6,4},{7,5},{8,6},{9,7},{10,8},{11,9},{12,... | collective-permute-start | bytes 786440 | tf_op jit(solution)/shard_map/ppermute | solution.py:30
  78.9 1.6 %collective-permute-start.14 = (f32[256,128]{1,0:T(8,128)S(1)}, f32[256,128]{1,0:T(8,128)S(1)}, u32[]{:S(2)}, u32[]{:S(2)}) collective-permute-start(f32[256,128]{1,0:T(8,128)S(1)} %get-tuple-element.43), channel_id=1, source_target_pairs={{0,1},{1,0},{2,3},{3,2},{4,5},{5,4},{6,7},{7,6},{8,9},{9,8},{10,11... | collective-permute-start | bytes 393224 | tf_op jit(solution)/shard_map/ppermute | solution.py:386
  81.9 2.1 %collective-permute-done.14.one_a = f32[256,128]{1,0:T(8,128)S(1)} collective-permute-done((f32[256,128]{1,0:T(8,128)S(1)}, f32[256,128]{1,0:T(8,128)S(1)}, u32[]{:S(2)}, u32[]{:S(2)}) %collective-permute-start.14) | collective-permute-done | bytes 131104 | tf_op jit(solution)/shard_map/ppermute | solution.py:386
  84.0 2.7 %collective-permute-done.15.one_b = f32[256,128]{1,0:T(8,128)S(1)} collective-permute-done((f32[256,128]{1,0:T(8,128)S(1)}, f32[256,128]{1,0:T(8,128)S(1)}, u32[]{:S(2)}, u32[]{:S(2)}) %collective-permute-start.15) | collective-permute-done | bytes 131104 | tf_op jit(solution)/shard_map/ppermute | solution.py:386
  86.6 2.2 %collective-permute-done.16.up = f32[512,128]{1,0:T(8,128)S(1)} collective-permute-done((f32[512,128]{1,0:T(8,128)S(1)}, f32[512,128]{1,0:T(8,128)S(1)}, u32[]{:S(2)}, u32[]{:S(2)}) %collective-permute-start.16) | collective-permute-done | bytes 262176 | tf_op jit(solution)/shard_map/ppermute | solution.py:30
  89.5 10.9 %all_to_all.10.pieces = f32[32,8,128]{2,1,0:T(8,128)S(1)} all-to-all(f32[32,8,128]{2,1,0:T(8,128)S(1)} %broadcast_in_dim.24), channel_id=1, replica_groups=mesh['row'=4,'col'=8] {'row','col'}, dimensions={0} | all-to-all | bytes 262144 | tf_op jit(solution)/shard_map/all_to_all | solution.py:468
  100.5 1.4 %shard_map.97 = (f32[1024,128]{1,0:T(8,128)}, bf16[1024,128]{1,0:T(8,128)(2,1)S(1)}, f32[2,320,128]{2,1,0:T(8,128)}) custom-call(s32[1]{0:T(128)} %bitcast.row, f32[32,8,128]{2,1,0:T(8,128)S(1)} %all_to_all.10.pieces, f32[1,128]{1,0:T(1,128)S(1)} %bitcast.13, f32[1024,128]{1,0:T(8,128)S(1)} %copy-done, f32[1024,128]{1,0:T(8,128)S(1)} %shard_map.84.vec.v1, ...), custom_call_target="tpu_custom_call" | custom-call | flops 167772160 | bytes 2621440 | tf_op jit(solution)/shard_map/pallas_call | solution.py:343
  102.5 1.2 %collective-permute-done.17 = f32[2,320,128]{2,1,0:T(8,128)S(1)} collective-permute-done((f32[2,320,128]{2,1,0:T(8,128)}, f32[2,320,128]{2,1,0:T(8,128)S(1)}, u32[]{:S(2)}, u32[]{:S(2)}) %collective-permute-start.17) | collective-permute-done | bytes 327712 | tf_op jit(solution)/shard_map/ppermute | solution.py:386
  104.8 5.2 %collective-permute-done.18 = f32[1,320,128]{2,1,0:T(8,128)S(1)} collective-permute-done((f32[1,320,128]{2,1,0:T(8,128)S(1)}, f32[1,320,128]{2,1,0:T(8,128)S(1)}, u32[]{:S(2)}, u32[]{:S(2)}) %collective-permute-start.18) | collective-permute-done | bytes 163872 | tf_op jit(solution)/shard_map/ppermute | solution.py:386
  110.1 10.7 %all_to_all.11 = f32[8,40,128]{2,1,0:T(8,128)S(1)} all-to-all(f32[8,40,128]{2,1,0:T(8,128)S(1)} %bitcast.16), channel_id=1, replica_groups=mesh['row'=4,'col'=8] {'col'}, dimensions={0} | all-to-all | bytes 327680 | tf_op jit(solution)/shard_map/all_to_all | solution.py:382
  (42 shorter events, 14.1 us)
Async XLA Ops:
  0.6 18.8 %collective-permute-start.1 = (f32[1024,128]{1,0:T(8,128)}, f32[1024,128]{1,0:T(8,128)S(1)}, u32[]{:S(2)}, u32[]{:S(2)}) collective-permute-start(f32[1024,128]{1,0:T(8,128)} %v0.3), channel_id=1, source_target_pairs={{0,2},{1,3},{2,4},{3,5},{4,6},{5,7},{6,8},{7,9},{8,10},{9,11},{10,... | collective-permute-start | bytes 1572872 | tf_op jit(solution)/shard_map/ppermute | solution.py:30
  6.3 5.7 %copy-start = (f32[1024,128]{1,0:T(8,128)S(1)}, f32[1024,128]{1,0:T(8,128)}, u32[]{:S(2)}) copy-start(f32[1024,128]{1,0:T(8,128)} %v0.3) | copy-start | bytes 1572868
  9.9 9.5 %collective-permute-start.2 = (f32[512,128]{1,0:T(8,128)}, f32[512,128]{1,0:T(8,128)S(1)}, u32[]{:S(2)}, u32[]{:S(2)}) collective-permute-start(f32[512,128]{1,0:T(8,128)} %get-tuple-element.32), channel_id=1, source_target_pairs={{0,1},{1,0},{2,3},{3,2},{4,5},{5,4},{6,7},{7,6},{8,9},{9,8},{10,11... | collective-permute-start | bytes 786440 | tf_op jit(solution)/shard_map/ppermute | solution.py:386
  11.4 12.9 %collective-permute-start = (f32[512,128]{1,0:T(8,128)}, f32[512,128]{1,0:T(8,128)S(1)}, u32[]{:S(2)}, u32[]{:S(2)}) collective-permute-start(f32[512,128]{1,0:T(8,128)} %get-tuple-element.26), channel_id=1, source_target_pairs={{0,1},{1,0},{2,3},{3,2},{4,5},{5,4},{6,7},{7,6},{8,9},{9,8},{10,11... | collective-permute-start | bytes 786440 | tf_op jit(solution)/shard_map/ppermute | solution.py:386
  15.7 10.0 %copy-start.2 = (f32[1,1024,1024]{2,1,0:T(8,128)S(1)}, f32[1,1024,1024]{2,1,0:T(8,128)}, u32[]{:S(2)}) copy-start(f32[1,1024,1024]{2,1,0:T(8,128)} %param.8) | copy-start | bytes 12582916
  19.5 17.4 %collective-permute-start.3 = (f32[1024,128]{1,0:T(8,128)S(1)}, f32[1024,128]{1,0:T(8,128)S(1)}, u32[]{:S(2)}, u32[]{:S(2)}) collective-permute-start(f32[1024,128]{1,0:T(8,128)S(1)} %shard_map.80.after), channel_id=1, source_target_pairs={{0,1},{1,0},{2,3},{3,2},{4,5},{5,4},{6,7},{7,6},{8,9},{9,8},{10,11... | collective-permute-start | bytes 1572872 | tf_op jit(solution)/shard_map/ppermute | solution.py:386
  21.1 11.0 %collective-permute-start.4 = (f32[512,128]{1,0:T(8,128)S(1)}, f32[512,128]{1,0:T(8,128)S(1)}, u32[]{:S(2)}, u32[]{:S(2)}) collective-permute-start(f32[512,128]{1,0:T(8,128)S(1)} %shard_map.79.after), channel_id=1, source_target_pairs={{2,0},{3,1},{4,2},{5,3},{6,4},{7,5},{8,6},{9,7},{10,8},{11,9},{12,... | collective-permute-start | bytes 786440 | tf_op jit(solution)/shard_map/ppermute | solution.py:30
  24.3 12.6 %collective-permute-start.5 = (f32[512,128]{1,0:T(8,128)S(1)}, f32[512,128]{1,0:T(8,128)S(1)}, u32[]{:S(2)}, u32[]{:S(2)}) collective-permute-start(f32[512,128]{1,0:T(8,128)S(1)} %shard_map.81.after), channel_id=1, source_target_pairs={{2,0},{3,1},{4,2},{5,3},{6,4},{7,5},{8,6},{9,7},{10,8},{11,9},{12,... | collective-permute-start | bytes 786440 | tf_op jit(solution)/shard_map/ppermute | solution.py:30
  37.6 12.8 %collective-permute-start.7 = (f32[1024,128]{1,0:T(8,128)S(1)}, f32[1024,128]{1,0:T(8,128)S(1)}, u32[]{:S(2)}, u32[]{:S(2)}) collective-permute-start(f32[1024,128]{1,0:T(8,128)S(1)} %shard_map.84.vec.v1), channel_id=1, source_target_pairs={{0,2},{1,3},{2,4},{3,5},{4,6},{5,7},{6,8},{7,9},{8,10},{9,11},{10,... | collective-permute-start | bytes 1572872 | tf_op jit(solution)/shard_map/ppermute | solution.py:30
  40.0 9.3 %collective-permute-start.8 = (f32[512,128]{1,0:T(8,128)S(1)}, f32[512,128]{1,0:T(8,128)S(1)}, u32[]{:S(2)}, u32[]{:S(2)}) collective-permute-start(f32[512,128]{1,0:T(8,128)S(1)} %get-tuple-element.38), channel_id=1, source_target_pairs={{0,1},{1,0},{2,3},{3,2},{4,5},{5,4},{6,7},{7,6},{8,9},{9,8},{10,11... | collective-permute-start | bytes 786440 | tf_op jit(solution)/shard_map/ppermute | solution.py:386
  41.4 12.3 %collective-permute-start.6 = (f32[512,128]{1,0:T(8,128)S(1)}, f32[512,128]{1,0:T(8,128)S(1)}, u32[]{:S(2)}, u32[]{:S(2)}) collective-permute-start(f32[512,128]{1,0:T(8,128)S(1)} %get-tuple-element.36), channel_id=1, source_target_pairs={{0,1},{1,0},{2,3},{3,2},{4,5},{5,4},{6,7},{7,6},{8,9},{9,8},{10,11... | collective-permute-start | bytes 786440 | tf_op jit(solution)/shard_map/ppermute | solution.py:386
  50.6 16.5 %collective-permute-start.9 = (f32[1024,128]{1,0:T(8,128)S(1)}, f32[1024,128]{1,0:T(8,128)S(1)}, u32[]{:S(2)}, u32[]{:S(2)}) collective-permute-start(f32[1024,128]{1,0:T(8,128)S(1)} %shard_map.87.after), channel_id=1, source_target_pairs={{0,1},{1,0},{2,3},{3,2},{4,5},{5,4},{6,7},{7,6},{8,9},{9,8},{10,11... | collective-permute-start | bytes 1572872 | tf_op jit(solution)/shard_map/ppermute | solution.py:386
  51.2 10.3 %collective-permute-start.10 = (f32[512,128]{1,0:T(8,128)S(1)}, f32[512,128]{1,0:T(8,128)S(1)}, u32[]{:S(2)}, u32[]{:S(2)}) collective-permute-start(f32[512,128]{1,0:T(8,128)S(1)} %shard_map.86.after), channel_id=1, source_target_pairs={{2,0},{3,1},{4,2},{5,3},{6,4},{7,5},{8,6},{9,7},{10,8},{11,9},{12,... | collective-permute-start | bytes 786440 | tf_op jit(solution)/shard_map/ppermute | solution.py:30
  53.7 13.3 %collective-permute-start.11 = (f32[512,128]{1,0:T(8,128)S(1)}, f32[512,128]{1,0:T(8,128)S(1)}, u32[]{:S(2)}, u32[]{:S(2)}) collective-permute-start(f32[512,128]{1,0:T(8,128)S(1)} %shard_map.88.after), channel_id=1, source_target_pairs={{2,0},{3,1},{4,2},{5,3},{6,4},{7,5},{8,6},{9,7},{10,8},{11,9},{12,... | collective-permute-start | bytes 786440 | tf_op jit(solution)/shard_map/ppermute | solution.py:30
  68.4 9.1 %collective-permute-start.13 = (f32[512,128]{1,0:T(8,128)S(1)}, f32[512,128]{1,0:T(8,128)S(1)}, u32[]{:S(2)}, u32[]{:S(2)}) collective-permute-start(f32[512,128]{1,0:T(8,128)S(1)} %get-tuple-element.42), channel_id=1, source_target_pairs={{0,1},{1,0},{2,3},{3,2},{4,5},{5,4},{6,7},{7,6},{8,9},{9,8},{10,11... | collective-permute-start | bytes 786440 | tf_op jit(solution)/shard_map/ppermute | solution.py:386
  70.0 8.9 %collective-permute-start.12 = (f32[512,128]{1,0:T(8,128)S(1)}, f32[512,128]{1,0:T(8,128)S(1)}, u32[]{:S(2)}, u32[]{:S(2)}) collective-permute-start(f32[512,128]{1,0:T(8,128)S(1)} %get-tuple-element.39.vec), channel_id=1, source_target_pairs={{0,2},{1,3},{2,4},{3,5},{4,6},{5,7},{6,8},{7,9},{8,10},{9,11},{10,... | collective-permute-start | bytes 786440 | tf_op jit(solution)/shard_map/ppermute | solution.py:30
  77.6 11.2 %collective-permute-start.16 = (f32[512,128]{1,0:T(8,128)S(1)}, f32[512,128]{1,0:T(8,128)S(1)}, u32[]{:S(2)}, u32[]{:S(2)}) collective-permute-start(f32[512,128]{1,0:T(8,128)S(1)} %shard_map.93.after), channel_id=1, source_target_pairs={{2,0},{3,1},{4,2},{5,3},{6,4},{7,5},{8,6},{9,7},{10,8},{11,9},{12,... | collective-permute-start | bytes 786440 | tf_op jit(solution)/shard_map/ppermute | solution.py:30
  78.9 5.0 %collective-permute-start.14 = (f32[256,128]{1,0:T(8,128)S(1)}, f32[256,128]{1,0:T(8,128)S(1)}, u32[]{:S(2)}, u32[]{:S(2)}) collective-permute-start(f32[256,128]{1,0:T(8,128)S(1)} %get-tuple-element.43), channel_id=1, source_target_pairs={{0,1},{1,0},{2,3},{3,2},{4,5},{5,4},{6,7},{7,6},{8,9},{9,8},{10,11... | collective-permute-start | bytes 393224 | tf_op jit(solution)/shard_map/ppermute | solution.py:386
  80.6 6.1 %collective-permute-start.15 = (f32[256,128]{1,0:T(8,128)S(1)}, f32[256,128]{1,0:T(8,128)S(1)}, u32[]{:S(2)}, u32[]{:S(2)}) collective-permute-start(f32[256,128]{1,0:T(8,128)S(1)} %get-tuple-element.44.after), channel_id=1, source_target_pairs={{0,1},{1,0},{2,3},{3,2},{4,5},{5,4},{6,7},{7,6},{8,9},{9,8},{10,11... | collective-permute-start | bytes 393224 | tf_op jit(solution)/shard_map/ppermute | solution.py:386
  81.9 18.6 %copy-start.1 = (bf16[1280,1024]{1,0:T(8,128)(2,1)S(1)}, bf16[1280,1024]{1,0:T(8,128)(2,1)}, u32[]{:S(2)}) copy-start(bf16[1280,1024]{1,0:T(8,128)(2,1)} %genotypes.3) | copy-start | bytes 7864324
  81.9 18.6 %copy-start.3 = (f32[128]{0:T(128)S(1)}, f32[128]{0:T(128)}, u32[]{:S(2)}) copy-start(f32[128]{0:T(128)} %param.7) | copy-start | bytes 1540
  101.8 1.8 %collective-permute-start.17 = (f32[2,320,128]{2,1,0:T(8,128)}, f32[2,320,128]{2,1,0:T(8,128)S(1)}, u32[]{:S(2)}, u32[]{:S(2)}) collective-permute-start(f32[2,320,128]{2,1,0:T(8,128)} %get-tuple-element.47), channel_id=1, source_target_pairs={{0,8},{1,9},{2,10},{3,11},{4,12},{5,13},{6,14},{7,15},{8,0},{9,1},... | collective-permute-start | bytes 983048 | tf_op jit(solution)/shard_map/ppermute | solution.py:386
  103.7 6.3 %collective-permute-start.18 = (f32[1,320,128]{2,1,0:T(8,128)S(1)}, f32[1,320,128]{2,1,0:T(8,128)S(1)}, u32[]{:S(2)}, u32[]{:S(2)}) collective-permute-start(f32[1,320,128]{2,1,0:T(8,128)S(1)} %get-tuple-element.49), channel_id=1, source_target_pairs={{0,16},{1,17},{2,18},{3,19},{4,20},{5,21},{6,22},{7,23},{8,24},{9,... | collective-permute-start | bytes 491528 | tf_op jit(solution)/shard_map/ppermute | solution.py:386

commit v4 on v3

--- a/solution.py
+++ b/solution.py
@@ -294,8 +294,11 @@
     below = below + jnp.dot(low_one[:, quarter:half], one_b[...].astype(BF16), preferred_element_type=F32)
     above = up[...] + jnp.where(odd[0] > 0, 0.0, pair[...])
     coupled = jnp.sum(v2[...] * below, axis=0, keepdims=True) + jnp.sum(v2[half:] * above, axis=0, keepdims=True)
-    out[...] = moments[...]
-    out[5:6] = moments[5:6] + 2.0 * coupled
+    whole = moments[...]
+    row = lax.broadcasted_iota(jnp.int32, whole.shape, 0)
+    whole = jnp.where(row == 5, whole + 2.0 * coupled, whole)
+    for place in range(out.shape[0]):
+        out[place] = whole
 
 
 def last(odd, low_one, low_two, one_a, one_b, two, v2, up, pair, moments):
@@ -304,7 +307,7 @@
         last_kernel,
         in_specs=[SMEM] + [VMEM] * 9,
         out_specs=VMEM,
-        out_shape=jax.ShapeDtypeStruct((8, k), F32),
+        out_shape=jax.ShapeDtypeStruct((lax.axis_size(AXES), 8, k), F32),
         compiler_params=params(),
         cost_estimate=cost(2 * size * size * k, 2 * size * size),
     )(odd, low_one, low_two, one_a, one_b, two, v2, up, pair, moments)
@@ -315,14 +318,16 @@
     return genotypes[pl.ds(pl.multiple_of(group * rows, rows), rows)]
 
 
-def send_kernel(groups, row, pieces, penalty, v0, v1, v2, genotypes, effects, rounded, send):
+def send_kernel(groups, row, pieces, penalty, v0, v1, v2, genotypes, factors, rounded, send):
     sums = pieces[0]
     for piece in range(1, pieces.shape[0]):
         sums = sums + pieces[piece]
     moments = [sums[m : m + 1] for m in range(6)]
     c0, c1, c2 = coefficients(moments, penalty[...])
     value = c0 * v0[...] + c1 * v1[...] + c2 * v2[...]
-    effects[...] = value
+    for place, factor in enumerate((c0, c1, c2)):
+        factors[place : place + 1] = factor
+    factors[3:8] = jnp.zeros_like(factors[3:8])
     narrow = value.astype(BF16)
     rounded[...] = narrow
     other = 1 - row[0] % 2
@@ -340,11 +345,11 @@
     people, size = genotypes.shape
     k = v0.shape[1]
     half = jax.ShapeDtypeStruct((groups // 2, people // groups, k), F32)
-    effects, rounded, send = pl.pallas_call(
+    factors, rounded, send = pl.pallas_call(
         functools.partial(send_kernel, groups),
         in_specs=[SMEM] + [VMEM] * 6,
         out_specs=[VMEM] * 3,
-        out_shape=[jax.ShapeDtypeStruct(v0.shape, F32), jax.ShapeDtypeStruct(v0.shape, BF16), half],
+        out_shape=[jax.ShapeDtypeStruct((8, k), F32), jax.ShapeDtypeStruct(v0.shape, BF16), half],
         compiler_params=params(),
         cost_estimate=cost(people * size * k, 2 * people * size),
     )(row, pieces, penalty, v0, v1, v2, genotypes)
@@ -356,7 +361,22 @@
         compiler_params=params(),
         cost_estimate=cost(people * size * k, 2 * people * size),
     )(row, rounded, genotypes)
-    return effects, send, keep
+    return factors, send, keep
+
+
+def effects_kernel(factors, v0, v1, v2, after, effects):
+    effects[...] = factors[0:1] * v0[...] + factors[1:2] * v1[...] + factors[2:3] * v2[...]
+
+
+def combined(factors, v0, v1, v2, after):
+    return pl.pallas_call(
+        effects_kernel,
+        in_specs=[VMEM] * 4 + [ANY],
+        out_specs=VMEM,
+        out_shape=jax.ShapeDtypeStruct(v0.shape, F32),
+        compiler_params=params(),
+        cost_estimate=cost(5 * v0.size, 16 * v0.size),
+    )(factors, v0, v1, v2, after)
 
 
 def pick_kernel(index, keep, received, mine, other):
@@ -465,9 +485,9 @@
     moments = own_moments(v0, v1, v2, diag, chosen_b)
     one_a, one_b = swapped(chosen_a, 1), swapped(chosen_b, 1)
     moments = last(odd, low_one, low_two, one_a, one_b, two, v2, up, pair, moments)
-    pieces = lax.all_to_all(jnp.broadcast_to(moments[None], (n,) + moments.shape), AXES, 0, 0, tiled=True)
-
-    effects, send, keep = partial_scores(row.astype(jnp.int32)[None], rows, pieces, penalty[None], v0, v1, v2, genotypes)
+    pieces = lax.all_to_all(moments, AXES, 0, 0, tiled=True)
+
+    factors, send, keep = partial_scores(row.astype(jnp.int32)[None], rows, pieces, penalty[None], v0, v1, v2, genotypes)
     received = swapped(send, cols)
     bit = rows // 4
     while bit:
@@ -478,6 +498,7 @@
         keep, send = pick(mine.astype(jnp.int32)[None], keep, received)
         received = swapped(send, 2 * bit * cols)
         bit //= 2
+    effects = combined(factors, v0, v1, v2, send)
     return effects, scattered_over((keep + received)[0], "col")
 
 

time: 122 us -> 123 us (level)
  blocking collectives: 21.6 us -> 10.9 us
  waiting for transfers between devices: 51.5 us -> 57.3 us
  starting transfers between devices: 28 us -> 31.4 us
  local copies, waits for them, and re-layouts: 0.03 us -> 1.76 us
    all_to_all x2 -> x1, blocking collectives: 21.6 us -> 10.9 us  [body(): pieces = lax.all_to_all(moments, AXES, 0, 0, tiled=True)]
    all_to_all x0 -> x1, waiting for transfers between devices: none -> 6.62 us  [scattered_over(): return jnp.sum(lax.all_to_all(pieces, axis, 0, 0, tiled=True), axis=0)]
    all_to_all x0 -> x1, starting transfers between devices: none -> 3.38 us  [scattered_over(): return jnp.sum(lax.all_to_all(pieces, axis, 0, 0, tiled=True), axis=0)]
    unnamed x8 -> x10, local copies, waits for them, and re-layouts: 0.02 us -> 1.76 us
  transfers between devices with their start and end apart: 19 -> 20, of which waited for: 15 -> 15; matrix products, arithmetic and copies ran while one was open for 0% -> 0% of each run, Pallas kernels for 11% -> 12%
where the time goes in v4:
time: 123 us; the launch traced here: 122 us
  waiting for transfers between devices  57.3 us (47%)
  starting transfers between devices  31.4 us (26%)
  Pallas kernels  18.2 us (15%)
  blocking collectives  10.9 us (9%)
  local copies, waits for them, and re-layouts  1.76 us (1%)
  between operations  1.57 us (1%)
  other arithmetic  1.3 us (1%)
    ppermute x11, waiting for transfers between devices, routed(): return lax.ppermute(block, AXES, pairs)  28 us
    ppermute x8, waiting for transfers between devices, shifted(): return lax.ppermute(block, AXES, route)  22.6 us
    ppermute x8, starting transfers between devices, shifted(): return lax.ppermute(block, AXES, route)  16.7 us
    ppermute x11, starting transfers between devices, routed(): return lax.ppermute(block, AXES, pairs)  11.3 us
    all_to_all x1, blocking collectives, body(): pieces = lax.all_to_all(moments, AXES, 0, 0, tiled=True)  10.9 us
    pallas_call x2, Pallas kernels, from_tiles(): pl.pallas_call(kernel, in_specs=[SMEM] * 2 + [pl.BlockSpec(memory_space=p...  7.31 us
    all_to_all x1, waiting for transfers between devices, scattered_over(): return jnp.sum(lax.all_to_all(pieces, axis, 0, 0, tiled=True), axis=0)  6.62 us
    all_to_all x1, starting transfers between devices, scattered_over(): return jnp.sum(lax.all_to_all(pieces, axis, 0, 0, tiled=True), axis=0)  3.38 us
  transfers between devices with their start and end apart: 20, of which 15 were waited for; matrix products, arithmetic and copies ran while one was open for 0% of the time, Pallas kernels for 12%

profile of v4, /device:TPU:0, one launch (start us, length us, event | category | flops | bytes accessed | tf_op | source)
XLA Modules:
  0.0 122.4 jit_solution(2034612454025030784)
XLA Ops:
  0.6 5.0 %collective-permute-start.1 = (f32[1024,128]{1,0:T(8,128)}, f32[1024,128]{1,0:T(8,128)S(1)}, u32[]{:S(2)}, u32[]{:S(2)}) collective-permute-start(f32[1024,128]{1,0:T(8,128)} %v0.5), channel_id=1, source_target_pairs={{0,2},{1,3},{2,4},{3,5},{4,6},{5,7},{6,8},{7,9},{8,10},{9,11},{10,... | collective-permute-start | bytes 1572872 | tf_op jit(solution)/shard_map/ppermute | solution.py:30
  6.3 3.6 %shard_map.77 = (f32[512,128]{1,0:T(8,128)}, f32[512,128]{1,0:T(8,128)}) custom-call(s32[1]{0:T(128)S(6)} %copy.8.band, s32[1]{0:T(128)} %bitcast.2.position, f32[1024,128]{1,0:T(8,128)} %v0.5, f32[2,1024,1024]{2,1,0:T(8,128)} %bitcast.14), custom_call_target="tpu_custom_call" | custom-call | flops 268435456 | bytes 4194304 | tf_op jit(solution)/shard_map/pallas_call | solution.py:103
  9.9 1.6 %collective-permute-start.2 = (f32[512,128]{1,0:T(8,128)}, f32[512,128]{1,0:T(8,128)S(1)}, u32[]{:S(2)}, u32[]{:S(2)}) collective-permute-start(f32[512,128]{1,0:T(8,128)} %get-tuple-element.32), channel_id=1, source_target_pairs={{0,1},{1,0},{2,3},{3,2},{4,5},{5,4},{6,7},{7,6},{8,9},{9,8},{10,11... | collective-permute-start | bytes 786440 | tf_op jit(solution)/shard_map/ppermute | solution.py:406
  11.9 3.7 %shard_map.78 = (f32[512,128]{1,0:T(8,128)S(1)}, f32[512,128]{1,0:T(8,128)S(1)}, bf16[1024,1024]{1,0:T(8,128)(2,1)S(1)}, bf16[1024,1024]{1,0:T(8,128)(2,1)S(1)}) custom-call(s32[1]{0:T(128)S(6)} %copy.8.band, s32[1]{0:T(128)} %bitcast.2.position, f32[1024,128]{1,0:T(8,128)S(1)} %copy-done, f32[2,1024,1024]{2,1,0:T(8,128)} %bitcast.15), custom_call_target="tpu_custom_call" | custom-call | flops 268435456 | bytes 8388608 | tf_op jit(solution)/shard_map/pallas_call | solution.py:103
  15.7 3.7 %collective-permute-done.2.pair.pair_a = f32[512,128]{1,0:T(8,128)S(1)} collective-permute-done((f32[512,128]{1,0:T(8,128)}, f32[512,128]{1,0:T(8,128)S(1)}, u32[]{:S(2)}, u32[]{:S(2)}) %collective-permute-start.2) | collective-permute-done | bytes 262176 | tf_op jit(solution)/shard_map/ppermute | solution.py:406
  19.5 1.6 %collective-permute-start.3 = (f32[1024,128]{1,0:T(8,128)S(1)}, f32[1024,128]{1,0:T(8,128)S(1)}, u32[]{:S(2)}, u32[]{:S(2)}) collective-permute-start(f32[1024,128]{1,0:T(8,128)S(1)} %shard_map.80.after), channel_id=1, source_target_pairs={{0,1},{1,0},{2,3},{3,2},{4,5},{5,4},{6,7},{7,6},{8,9},{9,8},{10,11... | collective-permute-start | bytes 1572872 | tf_op jit(solution)/shard_map/ppermute | solution.py:406
  21.1 1.3 %collective-permute-start.4 = (f32[512,128]{1,0:T(8,128)S(1)}, f32[512,128]{1,0:T(8,128)S(1)}, u32[]{:S(2)}, u32[]{:S(2)}) collective-permute-start(f32[512,128]{1,0:T(8,128)S(1)} %shard_map.79.after), channel_id=1, source_target_pairs={{2,0},{3,1},{4,2},{5,3},{6,4},{7,5},{8,6},{9,7},{10,8},{11,9},{12,... | collective-permute-start | bytes 786440 | tf_op jit(solution)/shard_map/ppermute | solution.py:30
  22.3 2.0 %collective-permute-done.pair.pair_b = f32[512,128]{1,0:T(8,128)S(1)} collective-permute-done((f32[512,128]{1,0:T(8,128)}, f32[512,128]{1,0:T(8,128)S(1)}, u32[]{:S(2)}, u32[]{:S(2)}) %collective-permute-start) | collective-permute-done | bytes 262176 | tf_op jit(solution)/shard_map/ppermute | solution.py:406
  24.3 1.3 %collective-permute-start.5 = (f32[512,128]{1,0:T(8,128)S(1)}, f32[512,128]{1,0:T(8,128)S(1)}, u32[]{:S(2)}, u32[]{:S(2)}) collective-permute-start(f32[512,128]{1,0:T(8,128)S(1)} %shard_map.81.after), channel_id=1, source_target_pairs={{2,0},{3,1},{4,2},{5,3},{6,4},{7,5},{8,6},{9,7},{10,8},{11,9},{12,... | collective-permute-start | bytes 786440 | tf_op jit(solution)/shard_map/ppermute | solution.py:30
  25.6 1.9 %shard_map.82 = (bf16[1024,1024]{1,0:T(8,128)(2,1)S(1)}, f32[1024,128]{1,0:T(8,128)S(1)}) custom-call(f32[1024,128]{1,0:T(8,128)S(1)} %copy-done, f32[1024,1024]{1,0:T(8,128)S(1)} %bitcast.10, f32[512,128]{1,0:T(8,128)S(1)} %shard_map.81.after), custom_call_target="tpu_custom_call" | custom-call | flops 268435456 | bytes 6291456 | tf_op jit(solution)/shard_map/pallas_call | solution.py:185
  28.2 3.8 %collective-permute-done.4.ahead_a = f32[512,128]{1,0:T(8,128)S(1)} collective-permute-done((f32[512,128]{1,0:T(8,128)S(1)}, f32[512,128]{1,0:T(8,128)S(1)}, u32[]{:S(2)}, u32[]{:S(2)}) %collective-permute-start.4) | collective-permute-done | bytes 262176 | tf_op jit(solution)/shard_map/ppermute | solution.py:30
  32.1 4.8 %collective-permute-done.5.ahead_b = f32[512,128]{1,0:T(8,128)S(1)} collective-permute-done((f32[512,128]{1,0:T(8,128)S(1)}, f32[512,128]{1,0:T(8,128)S(1)}, u32[]{:S(2)}, u32[]{:S(2)}) %collective-permute-start.5) | collective-permute-done | bytes 262176 | tf_op jit(solution)/shard_map/ppermute | solution.py:30
  37.7 1.5 %collective-permute-start.7 = (f32[1024,128]{1,0:T(8,128)S(1)}, f32[1024,128]{1,0:T(8,128)S(1)}, u32[]{:S(2)}, u32[]{:S(2)}) collective-permute-start(f32[1024,128]{1,0:T(8,128)S(1)} %shard_map.84.vec.v1), channel_id=1, source_target_pairs={{0,2},{1,3},{2,4},{3,5},{4,6},{5,7},{6,8},{7,9},{8,10},{9,11},{10,... | collective-permute-start | bytes 1572872 | tf_op jit(solution)/shard_map/ppermute | solution.py:30
  40.1 1.4 %collective-permute-start.8 = (f32[512,128]{1,0:T(8,128)S(1)}, f32[512,128]{1,0:T(8,128)S(1)}, u32[]{:S(2)}, u32[]{:S(2)}) collective-permute-start(f32[512,128]{1,0:T(8,128)S(1)} %get-tuple-element.38), channel_id=1, source_target_pairs={{0,1},{1,0},{2,3},{3,2},{4,5},{5,4},{6,7},{7,6},{8,9},{9,8},{10,11... | collective-permute-start | bytes 786440 | tf_op jit(solution)/shard_map/ppermute | solution.py:406
  42.2 7.2 %collective-permute-done.8.pair.pair_a = f32[512,128]{1,0:T(8,128)S(1)} collective-permute-done((f32[512,128]{1,0:T(8,128)S(1)}, f32[512,128]{1,0:T(8,128)S(1)}, u32[]{:S(2)}, u32[]{:S(2)}) %collective-permute-start.8) | collective-permute-done | bytes 262176 | tf_op jit(solution)/shard_map/ppermute | solution.py:406
  51.2 1.3 %collective-permute-start.10 = (f32[512,128]{1,0:T(8,128)S(1)}, f32[512,128]{1,0:T(8,128)S(1)}, u32[]{:S(2)}, u32[]{:S(2)}) collective-permute-start(f32[512,128]{1,0:T(8,128)S(1)} %shard_map.86.after), channel_id=1, source_target_pairs={{2,0},{3,1},{4,2},{5,3},{6,4},{7,5},{8,6},{9,7},{10,8},{11,9},{12,... | collective-permute-start | bytes 786440 | tf_op jit(solution)/shard_map/ppermute | solution.py:30
  53.8 1.3 %collective-permute-start.11 = (f32[512,128]{1,0:T(8,128)S(1)}, f32[512,128]{1,0:T(8,128)S(1)}, u32[]{:S(2)}, u32[]{:S(2)}) collective-permute-start(f32[512,128]{1,0:T(8,128)S(1)} %shard_map.88.after), channel_id=1, source_target_pairs={{2,0},{3,1},{4,2},{5,3},{6,4},{7,5},{8,6},{9,7},{10,8},{11,9},{12,... | collective-permute-start | bytes 786440 | tf_op jit(solution)/shard_map/ppermute | solution.py:30
  56.5 5.0 %collective-permute-done.10.ahead_a = f32[512,128]{1,0:T(8,128)S(1)} collective-permute-done((f32[512,128]{1,0:T(8,128)S(1)}, f32[512,128]{1,0:T(8,128)S(1)}, u32[]{:S(2)}, u32[]{:S(2)}) %collective-permute-start.10) | collective-permute-done | bytes 262176 | tf_op jit(solution)/shard_map/ppermute | solution.py:30
  61.4 5.6 %collective-permute-done.11.ahead_b = f32[512,128]{1,0:T(8,128)S(1)} collective-permute-done((f32[512,128]{1,0:T(8,128)S(1)}, f32[512,128]{1,0:T(8,128)S(1)}, u32[]{:S(2)}, u32[]{:S(2)}) %collective-permute-start.11) | collective-permute-done | bytes 262176 | tf_op jit(solution)/shard_map/ppermute | solution.py:30
  68.4 1.6 %collective-permute-start.13 = (f32[512,128]{1,0:T(8,128)S(1)}, f32[512,128]{1,0:T(8,128)S(1)}, u32[]{:S(2)}, u32[]{:S(2)}) collective-permute-start(f32[512,128]{1,0:T(8,128)S(1)} %get-tuple-element.42), channel_id=1, source_target_pairs={{0,1},{1,0},{2,3},{3,2},{4,5},{5,4},{6,7},{7,6},{8,9},{9,8},{10,11... | collective-permute-start | bytes 786440 | tf_op jit(solution)/shard_map/ppermute | solution.py:406
  70.0 3.9 %collective-permute-start.12 = (f32[512,128]{1,0:T(8,128)S(1)}, f32[512,128]{1,0:T(8,128)S(1)}, u32[]{:S(2)}, u32[]{:S(2)}) collective-permute-start(f32[512,128]{1,0:T(8,128)S(1)} %get-tuple-element.39.vec), channel_id=1, source_target_pairs={{0,2},{1,3},{2,4},{3,5},{4,6},{5,7},{6,8},{7,9},{8,10},{9,11},{10,... | collective-permute-start | bytes 786440 | tf_op jit(solution)/shard_map/ppermute | solution.py:30
  73.9 3.7 %collective-permute-done.13.pair = f32[512,128]{1,0:T(8,128)S(1)} collective-permute-done((f32[512,128]{1,0:T(8,128)S(1)}, f32[512,128]{1,0:T(8,128)S(1)}, u32[]{:S(2)}, u32[]{:S(2)}) %collective-permute-start.13) | collective-permute-done | bytes 262176 | tf_op jit(solution)/shard_map/ppermute | solution.py:406
  77.6 1.3 %collective-permute-start.16 = (f32[512,128]{1,0:T(8,128)S(1)}, f32[512,128]{1,0:T(8,128)S(1)}, u32[]{:S(2)}, u32[]{:S(2)}) collective-permute-start(f32[512,128]{1,0:T(8,128)S(1)} %shard_map.93.after), channel_id=1, source_target_pairs={{2,0},{3,1},{4,2},{5,3},{6,4},{7,5},{8,6},{9,7},{10,8},{11,9},{12,... | collective-permute-start | bytes 786440 | tf_op jit(solution)/shard_map/ppermute | solution.py:30
  78.9 1.6 %collective-permute-start.14 = (f32[256,128]{1,0:T(8,128)S(1)}, f32[256,128]{1,0:T(8,128)S(1)}, u32[]{:S(2)}, u32[]{:S(2)}) collective-permute-start(f32[256,128]{1,0:T(8,128)S(1)} %get-tuple-element.43), channel_id=1, source_target_pairs={{0,1},{1,0},{2,3},{3,2},{4,5},{5,4},{6,7},{7,6},{8,9},{9,8},{10,11... | collective-permute-start | bytes 393224 | tf_op jit(solution)/shard_map/ppermute | solution.py:406
  81.9 2.1 %collective-permute-done.14.one_a = f32[256,128]{1,0:T(8,128)S(1)} collective-permute-done((f32[256,128]{1,0:T(8,128)S(1)}, f32[256,128]{1,0:T(8,128)S(1)}, u32[]{:S(2)}, u32[]{:S(2)}) %collective-permute-start.14) | collective-permute-done | bytes 131104 | tf_op jit(solution)/shard_map/ppermute | solution.py:406
  83.9 2.6 %collective-permute-done.15.one_b = f32[256,128]{1,0:T(8,128)S(1)} collective-permute-done((f32[256,128]{1,0:T(8,128)S(1)}, f32[256,128]{1,0:T(8,128)S(1)}, u32[]{:S(2)}, u32[]{:S(2)}) %collective-permute-start.15) | collective-permute-done | bytes 131104 | tf_op jit(solution)/shard_map/ppermute | solution.py:406
  86.6 2.3 %collective-permute-done.16.up = f32[512,128]{1,0:T(8,128)S(1)} collective-permute-done((f32[512,128]{1,0:T(8,128)S(1)}, f32[512,128]{1,0:T(8,128)S(1)}, u32[]{:S(2)}, u32[]{:S(2)}) %collective-permute-start.16) | collective-permute-done | bytes 262176 | tf_op jit(solution)/shard_map/ppermute | solution.py:30
  89.6 10.9 %all_to_all.10.pieces = f32[32,8,128]{2,1,0:T(8,128)S(1)} all-to-all(f32[32,8,128]{2,1,0:T(8,128)S(1)} %shard_map.96), channel_id=1, replica_groups=mesh['row'=4,'col'=8] {'row','col'}, dimensions={0} | all-to-all | bytes 262144 | tf_op jit(solution)/shard_map/all_to_all | solution.py:488
  101.3 1.7 %copy-done.2 = bf16[1280,1024]{1,0:T(8,128)(2,1)S(1)} copy-done((bf16[1280,1024]{1,0:T(8,128)(2,1)S(1)}, bf16[1280,1024]{1,0:T(8,128)(2,1)}, u32[]{:S(2)}) %copy-start.2) | copy-done | bytes 2621464
  104.7 5.5 %collective-permute-done.18 = f32[1,320,128]{2,1,0:T(8,128)S(1)} collective-permute-done((f32[1,320,128]{2,1,0:T(8,128)S(1)}, f32[1,320,128]{2,1,0:T(8,128)S(1)}, u32[]{:S(2)}, u32[]{:S(2)}) %collective-permute-start.18) | collective-permute-done | bytes 163872 | tf_op jit(solution)/shard_map/ppermute | solution.py:406
  110.9 3.4 %all-to-all-start.1 = ((f32[8,40,128]{2,1,0:T(8,128)}), f32[8,40,128]{2,1,0:T(8,128)S(1)}, u32[]{:S(2)}, u32[]{:S(2)}) async-start(f32[8,40,128]{2,1,0:T(8,128)} %bitcast.9), calls=%async_computation.1 | async-start | bytes 327680 | tf_op jit(solution)/shard_map/all_to_all | solution.py:402
  115.2 6.6 %all-to-all-done.1 = f32[8,40,128]{2,1,0:T(8,128)S(1)} async-done(((f32[8,40,128]{2,1,0:T(8,128)}), f32[8,40,128]{2,1,0:T(8,128)S(1)}, u32[]{:S(2)}, u32[]{:S(2)}) %all-to-all-start.1) | async-done | bytes 163872 | tf_op jit(solution)/shard_map/all_to_all | solution.py:402
  (45 shorter events, 16.3 us)
Async XLA Ops:
  0.6 18.8 %collective-permute-start.1 = (f32[1024,128]{1,0:T(8,128)}, f32[1024,128]{1,0:T(8,128)S(1)}, u32[]{:S(2)}, u32[]{:S(2)}) collective-permute-start(f32[1024,128]{1,0:T(8,128)} %v0.5), channel_id=1, source_target_pairs={{0,2},{1,3},{2,4},{3,5},{4,6},{5,7},{6,8},{7,9},{8,10},{9,11},{10,... | collective-permute-start | bytes 1572872 | tf_op jit(solution)/shard_map/ppermute | solution.py:30
  6.3 5.7 %copy-start = (f32[1024,128]{1,0:T(8,128)S(1)}, f32[1024,128]{1,0:T(8,128)}, u32[]{:S(2)}) copy-start(f32[1024,128]{1,0:T(8,128)} %v0.5) | copy-start | bytes 1572868
  9.9 9.5 %collective-permute-start.2 = (f32[512,128]{1,0:T(8,128)}, f32[512,128]{1,0:T(8,128)S(1)}, u32[]{:S(2)}, u32[]{:S(2)}) collective-permute-start(f32[512,128]{1,0:T(8,128)} %get-tuple-element.32), channel_id=1, source_target_pairs={{0,1},{1,0},{2,3},{3,2},{4,5},{5,4},{6,7},{7,6},{8,9},{9,8},{10,11... | collective-permute-start | bytes 786440 | tf_op jit(solution)/shard_map/ppermute | solution.py:406
  11.4 12.9 %collective-permute-start = (f32[512,128]{1,0:T(8,128)}, f32[512,128]{1,0:T(8,128)S(1)}, u32[]{:S(2)}, u32[]{:S(2)}) collective-permute-start(f32[512,128]{1,0:T(8,128)} %get-tuple-element.26), channel_id=1, source_target_pairs={{0,1},{1,0},{2,3},{3,2},{4,5},{5,4},{6,7},{7,6},{8,9},{9,8},{10,11... | collective-permute-start | bytes 786440 | tf_op jit(solution)/shard_map/ppermute | solution.py:406
  15.7 9.9 %copy-start.3 = (f32[1,1024,1024]{2,1,0:T(8,128)S(1)}, f32[1,1024,1024]{2,1,0:T(8,128)}, u32[]{:S(2)}) copy-start(f32[1,1024,1024]{2,1,0:T(8,128)} %param.8) | copy-start | bytes 12582916
  19.5 17.4 %collective-permute-start.3 = (f32[1024,128]{1,0:T(8,128)S(1)}, f32[1024,128]{1,0:T(8,128)S(1)}, u32[]{:S(2)}, u32[]{:S(2)}) collective-permute-start(f32[1024,128]{1,0:T(8,128)S(1)} %shard_map.80.after), channel_id=1, source_target_pairs={{0,1},{1,0},{2,3},{3,2},{4,5},{5,4},{6,7},{7,6},{8,9},{9,8},{10,11... | collective-permute-start | bytes 1572872 | tf_op jit(solution)/shard_map/ppermute | solution.py:406
  21.1 11.0 %collective-permute-start.4 = (f32[512,128]{1,0:T(8,128)S(1)}, f32[512,128]{1,0:T(8,128)S(1)}, u32[]{:S(2)}, u32[]{:S(2)}) collective-permute-start(f32[512,128]{1,0:T(8,128)S(1)} %shard_map.79.after), channel_id=1, source_target_pairs={{2,0},{3,1},{4,2},{5,3},{6,4},{7,5},{8,6},{9,7},{10,8},{11,9},{12,... | collective-permute-start | bytes 786440 | tf_op jit(solution)/shard_map/ppermute | solution.py:30
  24.3 12.6 %collective-permute-start.5 = (f32[512,128]{1,0:T(8,128)S(1)}, f32[512,128]{1,0:T(8,128)S(1)}, u32[]{:S(2)}, u32[]{:S(2)}) collective-permute-start(f32[512,128]{1,0:T(8,128)S(1)} %shard_map.81.after), channel_id=1, source_target_pairs={{2,0},{3,1},{4,2},{5,3},{6,4},{7,5},{8,6},{9,7},{10,8},{11,9},{12,... | collective-permute-start | bytes 786440 | tf_op jit(solution)/shard_map/ppermute | solution.py:30
  37.7 12.9 %collective-permute-start.7 = (f32[1024,128]{1,0:T(8,128)S(1)}, f32[1024,128]{1,0:T(8,128)S(1)}, u32[]{:S(2)}, u32[]{:S(2)}) collective-permute-start(f32[1024,128]{1,0:T(8,128)S(1)} %shard_map.84.vec.v1), channel_id=1, source_target_pairs={{0,2},{1,3},{2,4},{3,5},{4,6},{5,7},{6,8},{7,9},{8,10},{9,11},{10,... | collective-permute-start | bytes 1572872 | tf_op jit(solution)/shard_map/ppermute | solution.py:30
  40.1 9.3 %collective-permute-start.8 = (f32[512,128]{1,0:T(8,128)S(1)}, f32[512,128]{1,0:T(8,128)S(1)}, u32[]{:S(2)}, u32[]{:S(2)}) collective-permute-start(f32[512,128]{1,0:T(8,128)S(1)} %get-tuple-element.38), channel_id=1, source_target_pairs={{0,1},{1,0},{2,3},{3,2},{4,5},{5,4},{6,7},{7,6},{8,9},{9,8},{10,11... | collective-permute-start | bytes 786440 | tf_op jit(solution)/shard_map/ppermute | solution.py:406
  41.4 12.3 %collective-permute-start.6 = (f32[512,128]{1,0:T(8,128)S(1)}, f32[512,128]{1,0:T(8,128)S(1)}, u32[]{:S(2)}, u32[]{:S(2)}) collective-permute-start(f32[512,128]{1,0:T(8,128)S(1)} %get-tuple-element.36), channel_id=1, source_target_pairs={{0,1},{1,0},{2,3},{3,2},{4,5},{5,4},{6,7},{7,6},{8,9},{9,8},{10,11... | collective-permute-start | bytes 786440 | tf_op jit(solution)/shard_map/ppermute | solution.py:406
  50.6 16.5 %collective-permute-start.9 = (f32[1024,128]{1,0:T(8,128)S(1)}, f32[1024,128]{1,0:T(8,128)S(1)}, u32[]{:S(2)}, u32[]{:S(2)}) collective-permute-start(f32[1024,128]{1,0:T(8,128)S(1)} %shard_map.87.after), channel_id=1, source_target_pairs={{0,1},{1,0},{2,3},{3,2},{4,5},{5,4},{6,7},{7,6},{8,9},{9,8},{10,11... | collective-permute-start | bytes 1572872 | tf_op jit(solution)/shard_map/ppermute | solution.py:406
  51.2 10.3 %collective-permute-start.10 = (f32[512,128]{1,0:T(8,128)S(1)}, f32[512,128]{1,0:T(8,128)S(1)}, u32[]{:S(2)}, u32[]{:S(2)}) collective-permute-start(f32[512,128]{1,0:T(8,128)S(1)} %shard_map.86.after), channel_id=1, source_target_pairs={{2,0},{3,1},{4,2},{5,3},{6,4},{7,5},{8,6},{9,7},{10,8},{11,9},{12,... | collective-permute-start | bytes 786440 | tf_op jit(solution)/shard_map/ppermute | solution.py:30
  53.8 13.3 %collective-permute-start.11 = (f32[512,128]{1,0:T(8,128)S(1)}, f32[512,128]{1,0:T(8,128)S(1)}, u32[]{:S(2)}, u32[]{:S(2)}) collective-permute-start(f32[512,128]{1,0:T(8,128)S(1)} %shard_map.88.after), channel_id=1, source_target_pairs={{2,0},{3,1},{4,2},{5,3},{6,4},{7,5},{8,6},{9,7},{10,8},{11,9},{12,... | collective-permute-start | bytes 786440 | tf_op jit(solution)/shard_map/ppermute | solution.py:30
  68.4 9.1 %collective-permute-start.13 = (f32[512,128]{1,0:T(8,128)S(1)}, f32[512,128]{1,0:T(8,128)S(1)}, u32[]{:S(2)}, u32[]{:S(2)}) collective-permute-start(f32[512,128]{1,0:T(8,128)S(1)} %get-tuple-element.42), channel_id=1, source_target_pairs={{0,1},{1,0},{2,3},{3,2},{4,5},{5,4},{6,7},{7,6},{8,9},{9,8},{10,11... | collective-permute-start | bytes 786440 | tf_op jit(solution)/shard_map/ppermute | solution.py:406
  70.0 8.9 %collective-permute-start.12 = (f32[512,128]{1,0:T(8,128)S(1)}, f32[512,128]{1,0:T(8,128)S(1)}, u32[]{:S(2)}, u32[]{:S(2)}) collective-permute-start(f32[512,128]{1,0:T(8,128)S(1)} %get-tuple-element.39.vec), channel_id=1, source_target_pairs={{0,2},{1,3},{2,4},{3,5},{4,6},{5,7},{6,8},{7,9},{8,10},{9,11},{10,... | collective-permute-start | bytes 786440 | tf_op jit(solution)/shard_map/ppermute | solution.py:30
  77.6 11.3 %collective-permute-start.16 = (f32[512,128]{1,0:T(8,128)S(1)}, f32[512,128]{1,0:T(8,128)S(1)}, u32[]{:S(2)}, u32[]{:S(2)}) collective-permute-start(f32[512,128]{1,0:T(8,128)S(1)} %shard_map.93.after), channel_id=1, source_target_pairs={{2,0},{3,1},{4,2},{5,3},{6,4},{7,5},{8,6},{9,7},{10,8},{11,9},{12,... | collective-permute-start | bytes 786440 | tf_op jit(solution)/shard_map/ppermute | solution.py:30
  78.9 5.0 %collective-permute-start.14 = (f32[256,128]{1,0:T(8,128)S(1)}, f32[256,128]{1,0:T(8,128)S(1)}, u32[]{:S(2)}, u32[]{:S(2)}) collective-permute-start(f32[256,128]{1,0:T(8,128)S(1)} %get-tuple-element.43), channel_id=1, source_target_pairs={{0,1},{1,0},{2,3},{3,2},{4,5},{5,4},{6,7},{7,6},{8,9},{9,8},{10,11... | collective-permute-start | bytes 393224 | tf_op jit(solution)/shard_map/ppermute | solution.py:406
  80.6 6.0 %collective-permute-start.15 = (f32[256,128]{1,0:T(8,128)S(1)}, f32[256,128]{1,0:T(8,128)S(1)}, u32[]{:S(2)}, u32[]{:S(2)}) collective-permute-start(f32[256,128]{1,0:T(8,128)S(1)} %get-tuple-element.44.after), channel_id=1, source_target_pairs={{0,1},{1,0},{2,3},{3,2},{4,5},{5,4},{6,7},{7,6},{8,9},{9,8},{10,11... | collective-permute-start | bytes 393224 | tf_op jit(solution)/shard_map/ppermute | solution.py:406
  81.8 18.7 %copy-start.1 = (bf16[1280,1024]{1,0:T(8,128)(2,1)S(1)}, bf16[1280,1024]{1,0:T(8,128)(2,1)}, u32[]{:S(2)}) copy-start(bf16[1280,1024]{1,0:T(8,128)(2,1)} %genotypes.3) | copy-start | bytes 7864324
  81.8 18.7 %copy-start.4 = (f32[128]{0:T(128)S(1)}, f32[128]{0:T(128)}, u32[]{:S(2)}) copy-start(f32[128]{0:T(128)} %param.7) | copy-start | bytes 1540
  101.1 2.4 %collective-permute-start.17 = (f32[2,320,128]{2,1,0:T(8,128)S(1)}, f32[2,320,128]{2,1,0:T(8,128)S(1)}, u32[]{:S(2)}, u32[]{:S(2)}) collective-permute-start(f32[2,320,128]{2,1,0:T(8,128)S(1)} %get-tuple-element.47), channel_id=1, source_target_pairs={{0,8},{1,9},{2,10},{3,11},{4,12},{5,13},{6,14},{7,15},{8,0},{9,1},... | collective-permute-start | bytes 983048 | tf_op jit(solution)/shard_map/ppermute | solution.py:406
  101.3 1.7 %copy-start.2 = (bf16[1280,1024]{1,0:T(8,128)(2,1)S(1)}, bf16[1280,1024]{1,0:T(8,128)(2,1)}, u32[]{:S(2)}) copy-start(bf16[1280,1024]{1,0:T(8,128)(2,1)} %genotypes.3) | copy-start | bytes 7864324
  103.6 6.6 %collective-permute-start.18 = (f32[1,320,128]{2,1,0:T(8,128)S(1)}, f32[1,320,128]{2,1,0:T(8,128)S(1)}, u32[]{:S(2)}, u32[]{:S(2)}) collective-permute-start(f32[1,320,128]{2,1,0:T(8,128)S(1)} %get-tuple-element.48.after), channel_id=1, source_target_pairs={{0,16},{1,17},{2,18},{3,19},{4,20},{5,21},{6,22},{7,23},{8,24},{9,... | collective-permute-start | bytes 491528 | tf_op jit(solution)/shard_map/ppermute | solution.py:406
  110.9 10.9 %all-to-all-start.1 = ((f32[8,40,128]{2,1,0:T(8,128)}), f32[8,40,128]{2,1,0:T(8,128)S(1)}, u32[]{:S(2)}, u32[]{:S(2)}) async-start(f32[8,40,128]{2,1,0:T(8,128)} %bitcast.9), calls=%async_computation.1 | async-start | bytes 327680 | tf_op jit(solution)/shard_map/all_to_all | solution.py:402
